TPU v7x, 32 devices: a whole 2x2x4 slice. The times are simulated.
32 devices in a mesh: pole: 4 (over y, x), row: 4 (over z), col: 2 (over core).
Axes of the slice: x: 2, y: 2, z: 4, core: 2. Of those that a mesh axis runs over, the one named last changes fastest.
Arguments:
- root_inverse: float32 [8, 1024, 1024], P('pole', ('row', 'col')), may hold values from -100 to 100
- node_factor: float32 [8, 4, 1024, 512], P('pole', 'row', None, 'col'), may hold values from -0.1875 to 0.1875
- node_inverse: float32 [8, 4, 512, 512], P('pole', 'row'), may hold values from -100 to 100
- leaf_root_factor: float32 [8, 8, 1024, 256], P('pole', ('row', 'col')), may hold values from -0.1875 to 0.1875
- leaf_node_factor: float32 [8, 8, 512, 256], P('pole', ('row', 'col')), may hold values from -0.25 to 0.25
- leaf_inverse: float32 [8, 8, 256, 256], P('pole', ('row', 'col')), may hold values from -100 to 100
- leaf_pattern: int32 [8, 8], P(('row', 'col')), may hold values 0 or 1
- pole_weight: float32 [8], P('pole'), may hold values from 0.1 to 1
Outputs:
- root_block: float32 [1024, 1024], P(('row', 'col'))
- node_offdiag: float32 [4, 1024, 512], P('row', None, 'col')
- node_diag: float32 [4, 512, 512], P('row', 'col')
- leaf_root: float32 [8, 1024, 256], P(('row', 'col'))
- leaf_node: float32 [8, 512, 256], P(('row', 'col'))
- leaf_diag: float32 [8, 256, 256], P(('row', 'col'))
All inputs are finite; a program needn't handle non-finite values. No bound on the sum of `leaf_pattern` on one device may be relied on, other than what follows from the above.
Results may differ from a plain program's by a relative error of at most 0.0001.
Values sent between devices are 32-bit elements; how exact they have to be, the bound alone decides.
No kernel may reach another device: no remote copies, remote signals or barrier semaphores. Data moves between devices by JAX's collectives and lax.ppermute only.
A program may use at most 64 MiB of HBM per device.

v0:
```python
import jax
import jax.numpy as jnp
from jax import lax
from jax.sharding import PartitionSpec as P

highest = lax.Precision.HIGHEST


def product(left, right):
    return jnp.matmul(left, right, precision=highest)


def weighted(weights, values):
    return jnp.sum(weights[:, None, None] * values, axis=0)


def shards(
    root_inverse,
    node_factor,
    node_inverse,
    leaf_root_factor,
    leaf_node_factor,
    leaf_inverse,
    leaf_pattern,
    pole_weight,
):
    node_cols = node_factor[:, 0]
    node_inv = node_inverse[:, 0]
    node_leaf = leaf_node_factor[:, 0]
    leaf_inv = leaf_inverse[:, 0]
    block_rows = leaf_root_factor.shape[2] // leaf_pattern.shape[1]
    row_mask = jnp.repeat(leaf_pattern[0].astype(jnp.float32), block_rows)
    root_leaf = leaf_root_factor[:, 0] * row_mask[None, :, None]
    width = node_cols.shape[2]
    joined = jnp.concatenate([node_cols, root_leaf], axis=2)
    products = product(lax.all_gather(root_inverse, ("row", "col"), axis=1, tiled=True), joined)
    offdiag = -products[:, :, :width]
    root_times = products[:, :, width:]
    col_index = lax.axis_index("col")
    own_rows = lax.dynamic_slice_in_dim(node_inv, col_index * width, width, 1)
    factor_t = jnp.swapaxes(node_cols, 1, 2)
    piece = lax.all_gather(offdiag, "col", axis=2, tiled=True)
    root_sum = root_times
    root_sum = root_sum + product(piece, node_leaf)
    node_part = product(jnp.swapaxes(piece, 1, 2), root_leaf)
    cross = product(factor_t, piece)
    root_sum, node_part, cross = (root_sum, node_part, cross)
    diag_rows = own_rows - cross
    diag_times = product(lax.all_gather(diag_rows, "col", axis=1, tiled=True), node_leaf)
    upper_levels = (
        weighted(pole_weight, root_inverse),
        weighted(pole_weight, offdiag)[None],
        weighted(pole_weight, diag_rows)[None],
    )
    middle_part = node_part + diag_times
    lower_part = (
        leaf_inv
        + product(jnp.swapaxes(root_leaf, 1, 2), root_sum)
        + product(jnp.swapaxes(node_leaf, 1, 2), middle_part)
    )
    leaf_levels = (
        weighted(pole_weight, -root_sum)[None],
        weighted(pole_weight, -middle_part)[None],
        weighted(pole_weight, lower_part)[None],
    )
    totals = lax.psum(
        (
            upper_levels[0],
            upper_levels[1],
            upper_levels[2],
            leaf_levels[0],
            leaf_levels[1],
            leaf_levels[2],
        ),
        "pole",
    )
    return (totals[0], totals[1], totals[2], totals[3], totals[4], totals[5])


def solution(mesh):
    return jax.shard_map(
        shards,
        mesh=mesh,
        in_specs=(
            P("pole", ("row", "col"), None),
            P("pole", "row", None, "col"),
            P("pole", "row", None, None),
            P("pole", ("row", "col"), None, None),
            P("pole", ("row", "col"), None, None),
            P("pole", ("row", "col"), None, None),
            P(("row", "col"), None),
            P("pole"),
        ),
        out_specs=(
            P(("row", "col"), None),
            P("row", None, "col"),
            P("row", "col", None),
            P(("row", "col"), None, None),
            P(("row", "col"), None, None),
            P(("row", "col"), None, None),
        ),
        check_vma=False,
    )
```

profile of v0, /device:TPU:0, one launch (start us, length us, event | category | flops | bytes accessed | tf_op | source)
XLA Modules:
  0.0 285.1 jit_solution(15521781454342625008)
XLA Ops:
  8.0 2.9 %copy.26 = f32[2,1,1024,256]{2,3,0,1:T(8,128)} copy(f32[2,1,1024,256]{3,2,1,0:T(8,128)} %param.11) | data formatting | bytes 4194304 | tf_op args[3]
  10.9 2.9 %copy.25 = f32[2,1,1024,256]{2,3,0,1:T(8,128)} copy(f32[2,1,1024,256]{3,2,1,0:T(8,128)} %param.9) | data formatting | bytes 4194304 | tf_op args[1]
  13.9 3.3 %bitcast_multiply_fusion = f32[2,1024,256]{1,2,0:T(8,128)} fusion(f32[2,1,1024,256]{2,3,0,1:T(8,128)} %copy.26, f32[1024]{0:T(1024)S(1)} %broadcast_bitcast_fusion), kind=kLoop, calls=%fused_computation.9 | loop fusion | flops 524288 | bytes 4198400 | tf_op jit(solution)/shard_map/mul | solution.py:33
  17.2 77.2 %all-gather.4.cloned.1.call-done = f32[2,1024,1024]{2,1,0:T(8,128)} async-done(((f32[2,128,1024]{2,1,0:T(8,128)}), f32[2,1024,1024]{2,1,0:T(8,128)}) %all-gather.4.cloned.1.call-update) | async-done | bytes 8388624 | tf_op jit(solution)/shard_map/all_gather | solution.py:36
  94.4 16.7 %fusion.4 = f32[2,1024,512]{1,2,0:T(8,128)S(1)} fusion(f32[2,1024,1024]{2,1,0:T(8,128)} %all-gather.4.cloned.1.call-done, f32[2,1024,256]{1,2,0:T(8,128)} %bitcast_multiply_fusion, f32[2,1024,256]{1,2,0:T(8,128)} %bitcast.57), kind=kOutput, calls=%fused_computation.4 | convolution fusion | flops 12885950464 | bytes 16777216 | tf_op jit(solution)/shard_map/dot_general | solution.py:10
  111.2 2.0 copy-done.3
  113.2 1.5 slice_negate_fusion
  115.0 1.0 constant_dynamic-slice_fusion
  116.0 1.6 copy.27
  117.6 9.5 %all-gather.6.cloned.1.call-done = f32[2,1024,512]{1,2,0:T(8,128)} async-done(((f32[2,1024,256]{1,2,0:T(8,128)}), f32[2,1024,512]{1,2,0:T(8,128)}) %all-gather.6.cloned.1.call-update) | async-done | bytes 4194320 | tf_op jit(solution)/shard_map/all_gather | solution.py:42
  127.1 8.5 %multiply_reduce_fusion.3 = (f32[256,512]{0,1:T(8,128)}, f32[2,256,512]{1,2,0:T(8,128)}) fusion(f32[2]{0:T(128)S(1)} %copy-done.9, f32[2,1024,512]{1,2,0:T(8,128)} %all-gather.6.cloned.1.call-done, f32[2,1,1024,256]{3,2,1,0:T(8,128)} %param.9, f32[2,1,256,512]{2,3,0,1:T(8,128)S(1)} %copy.27), kind=kOutput, calls=%fused_computation.25 | convolution fusion | flops 3221880832 | bytes 8912904 | tf_op jit(solution)/shard_map/dot_general | solution.py:10
  135.6 2.3 multiply_reduce_fusion.4
  138.0 10.4 %multiply_reduce_fusion = (f32[1024,256]{0,1:T(8,128)}, f32[1024,256]{0,1:T(8,128)}, f32[2,1024,256]{1,2,0:T(8,128)S(1)}) fusion(f32[2]{0:T(128)S(1)} %copy-done.9, f32[2,1024,512]{1,2,0:T(8,128)} %copy-done.3, f32[2,1024,512]{1,2,0:T(8,128)} %all-gather.6.cloned.1.call-done, f32[2,1,512,256]{3,2,1,0:T(8,128)S(1)} %copy-done.4), kind=kOutput, calls=%fused_computation.10 | convolution fusion | flops 3224371200 | bytes 13631496 | tf_op jit(solution)/shard_map/dot_general | solution.py:10
  148.4 2.9 %convolution_add_fusion.1 = f32[2,256,256]{2,1,0:T(8,128)} fusion(f32[2,1024,256]{1,2,0:T(8,128)S(1)} %copy-done.2, f32[2,1024,256]{1,2,0:T(8,128)S(1)} %get-tuple-element.20, f32[2,1,256,256]{3,2,1,0:T(8,128)S(1)} %copy-done.7), kind=kOutput, calls=%fused_computation.17 | convolution fusion | flops 1610743808 | bytes 5242880 | tf_op jit(solution)/shard_map/dot_general | solution.py:10
  151.3 5.2 %fusion.19 = f32[2,512,256]{2,1,0:T(8,128)S(1)} fusion(f32[2,512,512]{1,2,0:T(8,128)} %all-gather.8.cloned.1.call-done, f32[2,1,512,256]{3,2,1,0:T(8,128)S(1)} %copy-done.4), kind=kOutput, calls=%fused_computation.21 | convolution fusion | flops 1610612736 | bytes 4194304 | tf_op jit(solution)/shard_map/dot_general | solution.py:10
  156.5 6.3 %multiply_reduce_fusion.2 = (f32[512,256]{1,0:T(8,128)}, f32[2,512,256]{2,1,0:T(8,128)S(1)}) fusion(f32[2]{0:T(128)S(1)} %copy-done.9, f32[2,512,256]{2,1,0:T(8,128)S(1)} %fusion.19, f32[2,1024,512]{1,2,0:T(8,128)S(1)} %copy-done.1, f32[2,1024,256]{1,2,0:T(8,128)} %bitcast_multiply_fusion), kind=kOutput, calls=%fused_computation.24 | convolution fusion | flops 3222142976 | bytes 8912904 | tf_op jit(solution)/shard_map/dot_general | solution.py:10
  162.9 2.6 fusion.17
  165.5 102.7 %all-reduce.3.cloned.1.call-done = (f32[128,1024]{1,0:T(8,128)}, f32[1,1024,256]{1,2,0:T(8,128)}, f32[1,256,512]{1,2,0:T(8,128)}, f32[1,1024,256]{1,2,0:T(8,128)...) async-done(((f32[128,1024]{1,0:T(8,128)}, f32[1,1024,256]{1,2,0:T(8,128)}, f32[1,256,512]{1,2,0:T(8,128)}, f32[1,1024,256]{1,2,0:T(8,128)}, f32[1,512,256]{2,1,0:T(8,128)}, ...) | async-done | bytes 3932176 | tf_op jit(solution)/shard_map/psum | solution.py:66
  268.1 2.6 copy.36
  270.7 2.0 copy.37
  272.8 1.3 copy.38
  274.1 1.9 copy.55
  276.0 1.9 copy.56
  277.8 0.7 copy.57
  (32 shorter events, 1.2 us)
Async XLA Ops:
  7.2 107.8 %copy-start = (f32[2,1,512,512]{3,2,1,0:T(8,128)S(1)}, f32[2,1,512,512]{3,2,1,0:T(8,128)}, u32[]{:S(2)}) copy-start(f32[2,1,512,512]{3,2,1,0:T(8,128)} %param.10) | copy-start | bytes 6291460
  7.2 87.2 %all-gather.4.cloned.1.call-start = ((), (), s32[]{:S(2)}) async-start(), calls=%async_computation | async-start | bytes 9437184 | tf_op jit(solution)/shard_map/all_gather | solution.py:36
  7.9 119.1 %all-gather.6.cloned.1.call-start = ((), (), s32[]{:S(2)}) async-start(), calls=%async_computation.1 | async-start | bytes 6291456 | tf_op jit(solution)/shard_map/all_gather | solution.py:42
  10.9 2.9 %copy-start.10 = (s32[1,8]{1,0:T(1,128)S(1)}, s32[1,8]{1,0:T(1,128)}, u32[]{:S(2)}) copy-start(s32[1,8]{1,0:T(1,128)} %param.14) | copy-start | bytes 100
  111.2 2.0 copy-start.3
  114.7 36.6 %all-gather.8.cloned.1.call-start = ((), (), s32[]{:S(2)}) async-start(), calls=%async_computation.2 | async-start | bytes 3145728 | tf_op jit(solution)/shard_map/all_gather | solution.py:49
  114.9 12.1 %copy-start.9 = (f32[2]{0:T(128)S(1)}, f32[2]{0:T(128)}, u32[]{:S(2)}) copy-start(f32[2]{0:T(128)} %param.15) | copy-start | bytes 28
  135.6 2.4 copy-start.4
  135.6 132.5 %all-reduce.3.cloned.1.call-start = ((), (), s32[]{:S(2)}) async-start(), calls=%async_computation.3 | async-start | bytes 7864320 | tf_op jit(solution)/shard_map/psum | solution.py:66
  137.9 10.4 %copy-start.2 = (f32[2,1024,256]{1,2,0:T(8,128)S(1)}, f32[2,1024,256]{1,2,0:T(8,128)}, u32[]{:S(2)}) copy-start(f32[2,1024,256]{1,2,0:T(8,128)} %bitcast_multiply_fusion) | copy-start | bytes 6291460
  138.0 10.4 %copy-start.7 = (f32[2,1,256,256]{3,2,1,0:T(8,128)S(1)}, f32[2,1,256,256]{3,2,1,0:T(8,128)}, u32[]{:S(2)}) copy-start(f32[2,1,256,256]{3,2,1,0:T(8,128)} %param.13) | copy-start | bytes 1572868
  151.3 5.2 %copy-start.1 = (f32[2,1024,512]{1,2,0:T(8,128)S(1)}, f32[2,1024,512]{1,2,0:T(8,128)}, u32[]{:S(2)}) copy-start(f32[2,1024,512]{1,2,0:T(8,128)} %all-gather.6.cloned.1.call-done) | copy-start | bytes 12582916
  156.5 6.3 %copy-start.5 = (f32[2,256,256]{2,1,0:T(8,128)S(1)}, f32[2,256,256]{2,1,0:T(8,128)}, u32[]{:S(2)}) copy-start(f32[2,256,256]{2,1,0:T(8,128)} %convolution_add_fusion.1) | copy-start | bytes 1572868
  268.1 4.7 %copy-start.6 = (f32[1,1024,256]{1,2,0:T(8,128)S(1)}, f32[1,1024,256]{1,2,0:T(8,128)}, u32[]{:S(2)}) copy-start(f32[1,1024,256]{1,2,0:T(8,128)} %get-tuple-element.17) | copy-start | bytes 3145732
  272.8 5.1 %copy-start.8 = (f32[1,256,256]{2,1,0:T(8,128)S(1)}, f32[1,256,256]{2,1,0:T(8,128)}, u32[]{:S(2)}) copy-start(f32[1,256,256]{2,1,0:T(8,128)} %get-tuple-element.30) | copy-start | bytes 786436
Sparse Core Ops, SparseCore 0:
  9.6 84.7 all-gather.3
  114.8 12.1 all-gather.5
  135.7 11.7 all-gather.7
  165.6 102.4 all-reduce.2
where the time goes:
time: 286 us; the launch traced here: 285 us
  waiting for transfers between devices  190 us (66%)
  matrix products  52.7 us (18%)
  local copies, waits for them, and re-layouts  21 us (7%)
  between operations  13.9 us (5%)
  other arithmetic  7.11 us (2%)
    psum x1, waiting for transfers between devices, shards(): lax.psum((upper_levels[0], upper_levels[1], upper_levels[2], leaf_levels[...  103 us
    all_gather x1, waiting for transfers between devices, shards(): lax.all_gather(root_inverse, ('row', 'col'), axis=1, tiled=True)  77.2 us
    dot_general x7, matrix products, product(): return jnp.matmul(left, right, precision=highest)  52.7 us
    unnamed x30, local copies, waits for them, and re-layouts  18.3 us
    all_gather x1, waiting for transfers between devices, shards(): piece = lax.all_gather(offdiag, 'col', axis=2, tiled=True)  9.49 us
  transfers between devices with their start and end apart: 4, of which 3 were waited for; matrix products, arithmetic and copies ran while one was open for 10% of the time, Pallas kernels for 0%

commit v1 on v0

v1 whole, which is shorter than its diff:
```python
import functools

import jax
import jax.numpy as jnp
from jax import lax
from jax.experimental import pallas as pl
from jax.experimental.pallas import tpu as pltpu
from jax.sharding import PartitionSpec as P

HIGH = lax.Precision.HIGH
SWAP = [(0, 1), (1, 0)]
MIB = 1 << 20


def product(left, right):
    return jnp.matmul(left, right, precision=HIGH)


def left_t(left, right):
    return jnp.einsum("pki,pkj->pij", left, right, precision=HIGH)


def weighted(weights, values):
    return jnp.sum(weights[:, None, None] * values, axis=0)


def general(
    root_inverse,
    node_factor,
    node_inverse,
    leaf_root_factor,
    leaf_node_factor,
    leaf_inverse,
    leaf_pattern,
    pole_weight,
):
    inv_n, leaf_n, inv_l = node_inverse[:, 0], leaf_node_factor[:, 0], leaf_inverse[:, 0]
    w1, width = inv_n.shape[2], node_factor.shape[3]
    start = lax.axis_index("col") * width
    row_mask = jnp.repeat(leaf_pattern[0].astype(jnp.float32), leaf_root_factor.shape[2] // leaf_pattern.shape[1])
    leaf = leaf_root_factor[:, 0] * row_mask[None, :, None]
    factor = lax.all_gather(node_factor[:, 0], "col", axis=2, tiled=True)
    root = lax.all_gather(root_inverse, ("row", "col"), axis=1, tiled=True)
    x = product(root, jnp.concatenate([factor, leaf - product(factor, leaf_n)], axis=2))
    gram = left_t(jnp.concatenate([factor, leaf], axis=2), x)
    sep = inv_n + gram[:, :w1, :w1]
    middle = jnp.swapaxes(gram[:, w1:, :w1], 1, 2) - product(sep, leaf_n)
    lower = inv_l + gram[:, w1:, w1:] - left_t(leaf_n, middle)
    rows = -weighted(pole_weight, x)
    totals = lax.psum(
        (
            weighted(pole_weight, root_inverse),
            lax.dynamic_slice_in_dim(rows, start, width, 1),
            lax.dynamic_slice_in_dim(weighted(pole_weight, sep), start, width, 0),
            rows[:, w1:],
            weighted(pole_weight, middle),
            weighted(pole_weight, lower),
        ),
        "pole",
    )
    return (totals[0],) + tuple(t[None] for t in totals[1:])


def split(x):
    high = x.astype(jnp.bfloat16)
    return high, (x - high.astype(jnp.float32)).astype(jnp.bfloat16)


def dot3(left, right, dims=((1,), (0,))):
    def one(a, b):
        return lax.dot_general(a, b, (dims, ((), ())), preferred_element_type=jnp.float32)

    return one(left[0], right[0]) + (one(left[0], right[1]) + one(left[1], right[0]))


def prepare_kernel(block, where, pattern, f_own, f_other, leaf, leaf_n, w_high, w_low, l_high, l_low, n_high, n_low):
    first = where[0] == 0
    own, other = f_own[0], f_other[0]
    f = jnp.concatenate([jnp.where(first, own, other), jnp.where(first, other, own)], axis=1)
    rows, w1 = f.shape
    step = pl.program_id(1)
    masked = []
    for i in range(0, rows, block):
        keep = pattern[0, step * (rows // block) + i // block]
        masked.append(jnp.where(keep != 0, leaf[0, i : i + block], 0.0))
    masked = jnp.concatenate(masked, axis=0)

    @pl.when(step == 0)
    def _():
        n_high[...], n_low[...] = split(leaf_n[0])

    fs = split(f)
    ds = split(masked - dot3(fs, (n_high[...], n_low[...])))
    w_high[0, :, :w1], w_low[0, :, :w1] = fs
    w_high[0, :, w1:], w_low[0, :, w1:] = ds
    l_high[0], l_low[0] = split(masked)


def prepare(where, pattern, f_own, f_other, leaf, leaf_n):
    poles, w0, width = f_own.shape
    w1, w2 = leaf_n.shape[1:]
    rows = 256
    lanes = w1 + w2

    def spec(*tail):
        return pl.BlockSpec((1, rows) + tail, lambda p, i, w, t: (p, i, 0))

    def out(*tail):
        return jax.ShapeDtypeStruct((poles, w0) + tail, jnp.bfloat16)

    return pl.pallas_call(
        functools.partial(prepare_kernel, w0 // pattern.shape[1]),
        grid_spec=pltpu.PrefetchScalarGridSpec(
            num_scalar_prefetch=2,
            grid=(poles, w0 // rows),
            in_specs=[spec(width), spec(width), spec(w2), pl.BlockSpec((1, w1, w2), lambda p, i, w, t: (p, 0, 0))],
            out_specs=[spec(lanes), spec(lanes), spec(w2), spec(w2)],
            scratch_shapes=[pltpu.VMEM((w1, w2), jnp.bfloat16)] * 2,
        ),
        out_shape=[out(lanes), out(lanes), out(w2), out(w2)],
        compiler_params=pltpu.CompilerParams(vmem_limit_bytes=24 * MIB),
        cost_estimate=pl.CostEstimate(flops=6 * poles * w0 * w1 * w2, bytes_accessed=15 * MIB, transcendentals=0),
        name="prepare",
    )(where, pattern, f_own, f_other, leaf, leaf_n)


def unit_kernel(choices, first_unit, last, pieces, where, weight, *refs):
    shards, refs = refs[: 2 * choices], refs[2 * choices :]
    (w_high, w_low, l_high, l_low), refs = refs[:4], refs[4:]
    if not first_unit:
        (gram_in, square_in), refs = refs[:2], refs[2:]
    if last:
        (inv_n, leaf_n, inv_l), refs = refs[:3], refs[3:]
    outs, refs = refs[:pieces], refs[pieces:]
    if not last:
        (gram, square), refs = refs[:2], refs[2:]
    (r_high, r_low) = refs
    p = pl.program_id(0)
    col, owner = where[0], where[1]
    rows = shards[0].shape[1]
    unit = 2 * rows
    for i in range(2):
        value = shards[i][0]
        if choices == 2:
            value = jnp.where(where[2] == 0, value, shards[2 + i][0])
        at = pl.ds(pl.multiple_of(jnp.where(col == i, 0, rows), rows), rows)
        r_high[at], r_low[at] = split(value)
    lanes = w_high.shape[2]
    w2 = l_high.shape[2]
    w1 = lanes - w2
    width = w1 // 2
    x = dot3((r_high[...], r_low[...]), (w_high[0], w_low[0]))
    scale = weight[p]
    mine = jnp.where(col == 0, x[:, :width], x[:, width:w1])
    sent = -scale * jnp.concatenate([mine, x[:, w1:]], axis=1)
    here = pl.ds(pl.multiple_of(owner * unit, unit), unit)
    fs = (w_high[0, here, :w1], w_low[0, here, :w1])
    ls = (l_high[0, here], l_low[0, here])
    xs = split(x)
    ps = (xs[0][:, :w1], xs[1][:, :w1])
    us = (xs[0][:, w1:], xs[1][:, w1:])
    across = ((0,), (0,))
    cross = dot3(fs, ps, across)
    below = dot3(ls, ps, across)
    inner = dot3(ls, us, across)
    if not first_unit:
        cross = cross + gram_in[0, :w1]
        below = below + gram_in[0, w1:]
        inner = inner + square_in[0]

    def put(ref, at, value):
        @pl.when(p == 0)
        def _():
            ref[at] = value

        @pl.when(p > 0)
        def _():
            ref[at] += value

    if not last:
        gram[0, :w1] = cross
        gram[0, w1:] = below
        square[0] = inner
        if first_unit:
            put(outs[0], slice(None), sent)
            root = scale * shards[0][0]
            half = root.shape[1] // 2
            put(outs[1], slice(0, rows), root[:, :half])
            put(outs[1], slice(rows, 2 * rows), root[:, half:])
        else:
            put(outs[0], slice(None), sent[:rows])
            put(outs[1], slice(None), sent[rows:])
        return
    sep = inv_n[0] + cross
    ns = split(leaf_n[0])
    middle = below.T - dot3(split(sep), ns)
    lower = inv_l[0] + inner - dot3(ns, split(middle), across)
    sep = scale * jnp.where(col == 0, sep[:width], sep[width:])
    middle = scale * middle
    lower = scale * lower
    a, b = outs
    head = a.shape[0] - unit
    put(a, slice(0, unit), sent)
    put(a, slice(unit, unit + head), sep[:head])
    rest = width - head
    put(b, slice(0, rest), sep[head:])
    put(b, slice(rest, rest + width), jnp.concatenate([middle[:width], middle[width:]], axis=1))
    put(b, slice(rest + width, rest + width + w2 // 2), jnp.concatenate([lower[: w2 // 2], lower[w2 // 2 :]], axis=1))


def tail_rows(unit, width, w2):
    half = (unit + 2 * width + w2 // 2) // 2
    return half, half - unit


def unit_call(where, weight, shards, split_factors, sums, ends, name):
    poles, rows, w0 = shards[0].shape
    w_high, w_low, l_high, l_low = split_factors
    lanes, w2 = w_high.shape[2], l_high.shape[2]
    w1 = lanes - w2
    unit = 2 * rows
    first_unit, last = not sums, bool(ends)

    def whole(x):
        return pl.BlockSpec((1,) + x.shape[1:], lambda p, w, t: (p, 0, 0))

    def kept(x):
        return pl.BlockSpec(x.shape, lambda p, w, t: (0, 0))

    f32 = jnp.float32
    gram = [jax.ShapeDtypeStruct((poles, lanes, w1), f32), jax.ShapeDtypeStruct((poles, w2, w2), f32)]
    if last:
        half, _ = tail_rows(unit, w1 // 2, w2)
        outs = [jax.ShapeDtypeStruct((half, w1), f32)] * 2
    elif first_unit:
        outs = [jax.ShapeDtypeStruct((unit, w1), f32)] * 2
    else:
        outs = [jax.ShapeDtypeStruct((rows, w1), f32)] * 2
    args = list(shards) + list(split_factors) + list(sums) + list(ends)
    out_specs = [kept(o) for o in outs]
    if not last:
        outs = outs + gram
        out_specs = out_specs + [whole(g) for g in gram]
    flops = 6 * poles * (unit * w0 * lanes + unit * w1 * lanes + unit * w2 * w2)
    return pl.pallas_call(
        functools.partial(unit_kernel, len(shards) // 2, first_unit, last, 2),
        grid_spec=pltpu.PrefetchScalarGridSpec(
            num_scalar_prefetch=2,
            grid=(poles,),
            in_specs=[whole(a) for a in args],
            out_specs=out_specs,
            scratch_shapes=[pltpu.VMEM((unit, w0), jnp.bfloat16)] * 2,
        ),
        out_shape=outs,
        compiler_params=pltpu.CompilerParams(vmem_limit_bytes=40 * MIB),
        cost_estimate=pl.CostEstimate(flops=flops, bytes_accessed=16 * MIB, transcendentals=0),
        name=name,
    )(where, weight, *args)


def place_kernel(unit, order, *refs):
    rows, w1 = unit // 2, refs[0].shape[1]
    width = w1 // 2
    root, off, upper = refs[-3:]

    def put(owner, at, value):
        here = pl.ds(pl.multiple_of(owner * unit + at, rows), value.shape[0])
        off[here] = value[:, :width]
        upper[here] = value[:, width:]

    put(order[0], 0, refs[0][...] + refs[1][...])
    total = refs[2][...] + refs[3][...]
    root[:, :w1] = total[:rows]
    root[:, w1:] = total[rows:]
    for k in range(1, (len(refs) - 3) // 4):
        put(order[k], 0, refs[4 * k][...] + refs[4 * k + 1][...])
        put(order[k], rows, refs[4 * k + 2][...] + refs[4 * k + 3][...])


def place(order, early, unit, w0, w2):
    w1 = early[0].shape[1]

    def whole(shape):
        return pl.BlockSpec(shape, lambda w: (0, 0))

    outs = [(unit // 2, w0), (w0, w1 // 2), (w0, w2)]
    return pl.pallas_call(
        functools.partial(place_kernel, unit),
        grid_spec=pltpu.PrefetchScalarGridSpec(
            num_scalar_prefetch=1,
            grid=(),
            in_specs=[pl.BlockSpec(memory_space=pltpu.VMEM)] * len(early),
            out_specs=[pl.BlockSpec(memory_space=pltpu.VMEM)] * 3,
        ),
        out_shape=[jax.ShapeDtypeStruct(o, jnp.float32) for o in outs],
        compiler_params=pltpu.CompilerParams(vmem_limit_bytes=24 * MIB),
        cost_estimate=pl.CostEstimate(flops=MIB, bytes_accessed=8 * MIB, transcendentals=0),
        name="place",
    )(order, *early)


def finish_kernel(unit, head, where, a, a_in, b, b_in, _off, _upper, off, upper, sep, middle, lower):
    total_a = a[...] + a_in[...]
    total_b = b[...] + b_in[...]
    width = off.shape[1]
    off[...] = total_a[:unit, :width]
    upper[...] = total_a[:unit, width:]
    sep[:head] = total_a[unit:]
    rest = width - head
    sep[head:] = total_b[:rest]
    w2 = lower.shape[1]
    middle[:width] = total_b[rest : rest + width, :w2]
    middle[width:] = total_b[rest : rest + width, w2:]
    lower[: w2 // 2] = total_b[rest + width :, :w2]
    lower[w2 // 2 :] = total_b[rest + width :, w2:]


def finish(where, late, off, upper, unit, w1, w2):
    width = w1 // 2
    half, head = tail_rows(unit, width, w2)
    piece = pl.BlockSpec((half, w1), lambda i, w: (0, 0))
    anywhere = pl.BlockSpec(memory_space=pl.ANY)

    def rows(x):
        return pl.BlockSpec((unit, x.shape[1]), lambda i, w: (w[1], 0))

    def whole(*shape):
        return pl.BlockSpec(shape, lambda i, w: (0, 0))

    shapes = [off.shape, upper.shape, (width, w1), (w1, w2), (w2, w2)]
    return pl.pallas_call(
        functools.partial(finish_kernel, unit, head),
        grid_spec=pltpu.PrefetchScalarGridSpec(
            num_scalar_prefetch=1,
            grid=(1,),
            in_specs=[piece] * 4 + [anywhere] * 2,
            out_specs=[rows(off), rows(upper)] + [whole(*s) for s in shapes[2:]],
        ),
        out_shape=[jax.ShapeDtypeStruct(s, jnp.float32) for s in shapes],
        input_output_aliases={5: 0, 6: 1},
        compiler_params=pltpu.CompilerParams(vmem_limit_bytes=24 * MIB),
        cost_estimate=pl.CostEstimate(flops=MIB, bytes_accessed=6 * MIB, transcendentals=0),
        name="finish",
    )(where, *late, off, upper)


def line_plan(n):
    plan = []
    for j in range(n):
        above = [(j % 2, s, j + s) for s in range(1, n - j)]
        below = [(1 - j % 2, s, j - s) for s in range(1, j + 1)]
        plan.append(sorted(above + below, key=lambda e: (e[1], e[0])))
    return plan


def line_pairs(n, kind, slot):
    pairs = []
    for k in range(kind, n - 1, 2):
        if k - slot + 1 >= 0:
            pairs.append((k, k + 1))
        if k + slot <= n - 1:
            pairs.append((k + 1, k))
    return pairs


def pole_pairs(n, bit):
    return [(p, p ^ bit) for p in range(n)]


def pole_step(a, b, n_pole, step):
    bits = [1 << i for i in range(n_pole.bit_length() - 1)]
    return (
        lax.ppermute(a, "pole", pole_pairs(n_pole, bits[step])),
        lax.ppermute(b, "pole", pole_pairs(n_pole, bits[-1 - step])),
    )


def together(*groups):
    flat, tree = jax.tree.flatten(groups)
    return jax.tree.unflatten(tree, lax.optimization_barrier(tuple(flat)))


def paired(
    n_pole,
    n_row,
    root_inverse,
    node_factor,
    node_inverse,
    leaf_root_factor,
    leaf_node_factor,
    leaf_inverse,
    leaf_pattern,
    pole_weight,
):
    row, col = lax.axis_index("row"), lax.axis_index("col")
    w0 = root_inverse.shape[2]
    w1, w2 = leaf_node_factor.shape[2:]
    unit = 2 * root_inverse.shape[1]
    steps = n_pole.bit_length() - 1
    plan = line_plan(n_row)
    entries = [[(0, 0, j) for j in range(n_row)]] + [[plan[j][k] for j in range(n_row)] for k in range(n_row - 1)]
    order = [jnp.array([e[2] for e in entry], jnp.int32)[row] for entry in entries]
    moved = {(0, 0): root_inverse, (1, 0): root_inverse}
    other = {}

    def swap(key):
        if key not in other:
            other[key] = lax.ppermute(moved[key], "col", SWAP)

    def advance(slot):
        for kind in range(2):
            pairs = line_pairs(n_row, kind, slot)
            if pairs:
                moved[kind, slot] = lax.ppermute(moved[1 - kind, slot - 1], "row", pairs)

    f_own = node_factor[:, 0]
    f_other = lax.ppermute(f_own, "col", SWAP)
    factors = prepare(
        jnp.stack([col, row]).astype(jnp.int32), leaf_pattern, f_own, f_other, leaf_root_factor[:, 0], leaf_node_factor[:, 0]
    )
    sums, early, waiting = [], [], []
    for k in range(n_row):
        kinds = sorted({e[:2] for e in entries[k]})
        for kind in kinds:
            swap(kind)
        if k < n_row - 1:
            advance(k + 1)
        choice = jnp.array([kinds.index(e[:2]) for e in entries[k]], jnp.int32)[row]
        where = jnp.stack([col.astype(jnp.int32), order[k], choice])
        shards = [s for kind in kinds for s in (moved[kind], other[kind])]
        last = k == n_row - 1
        ends = [node_inverse[:, 0], leaf_node_factor[:, 0], leaf_inverse[:, 0]] if last else []
        outs = unit_call(where, pole_weight, shards, factors, sums, ends, "unit")
        sums = list(outs[2:])
        a, b = outs[:2]
        if not last:
            moved, other, sums, a, b, early = together(moved, other, sums, a, b, early)
        late = []
        for step in range(steps):
            a_in, b_in = pole_step(a, b, n_pole, step)
            if step < steps - 1:
                a, b = a + a_in, b + b_in
        if not last:
            early += [a, a_in, b, b_in]
    late = [a, a_in, b, b_in]
    root, off, upper = place(jnp.stack(order), early, unit, w0, w2)
    off, upper, sep, middle, lower = finish(where, late, off, upper, unit, w1, w2)
    return root, off[None], sep[None], upper[None], middle[None], lower[None]


def solution(mesh):
    n_pole, n_row, n_col = (mesh.shape[axis] for axis in ("pole", "row", "col"))

    def shards(root_inverse, node_factor, *rest):
        fits = n_col == 2 and n_row == 4 and n_pole > 1 and n_pole & (n_pole - 1) == 0
        form = functools.partial(paired, n_pole, n_row) if fits else general
        return form(root_inverse, node_factor, *rest)

    return jax.shard_map(
        shards,
        mesh=mesh,
        in_specs=(
            P("pole", ("row", "col"), None),
            P("pole", "row", None, "col"),
            P("pole", "row", None, None),
            P("pole", ("row", "col"), None, None),
            P("pole", ("row", "col"), None, None),
            P("pole", ("row", "col"), None, None),
            P(("row", "col"), None),
            P("pole"),
        ),
        out_specs=(
            P(("row", "col"), None),
            P("row", None, "col"),
            P("row", "col", None),
            P(("row", "col"), None, None),
            P(("row", "col"), None, None),
            P(("row", "col"), None, None),
        ),
        check_vma=False,
    )
```

time: 286 us -> 170 us (0.59)
  waiting for transfers between devices: 190 us -> 77.5 us
  matrix products: 52.7 us -> 0 us
  Pallas kernels: 0 us -> 44.8 us
  starting transfers between devices: 0.34 us -> 27.5 us
  between operations: 13.9 us -> 0.86 us
  local copies, waits for them, and re-layouts: 21 us -> 12.5 us
    psum x1 -> x0, waiting for transfers between devices: 103 us -> none  [shards(): lax.psum((upper_levels[0], upper_levels[1], upper_levels[2], leaf_levels[...]
    all_gather x3 -> x0, waiting for transfers between devices: 86.7 us -> none  [the longest x1 77.2 us: shards(): lax.all_gather(root_inverse, ('row', 'col'), axis=1, tiled=True)]
    ppermute x0 -> x28, waiting for transfers between devices: none -> 77.5 us  [the longest x8 60.8 us: pole_step(): lax.ppermute(b, 'pole', pole_pairs(n_pole, bits[-1 - step]))]
    dot_general x7 -> x0, matrix products: 52.7 us -> none  [product(): return jnp.matmul(left, right, precision=highest)]
    pallas_call x0 -> x7, Pallas kernels: none -> 44.8 us  [the longest x4 35.8 us: unit_call(): pl.pallas_call(functools.partial(unit_kernel, len(shards) // 2, first_uni...]
    ppermute x0 -> x28, starting transfers between devices: none -> 27.5 us  [the longest x8 9.94 us: pole_step(): lax.ppermute(b, 'pole', pole_pairs(n_pole, bits[-1 - step]))]
    unnamed x30 -> x36, local copies, waits for them, and re-layouts: 18.3 us -> 10.1 us
    another operation x0 -> x6, other arithmetic: none -> 5.61 us  [the longest x4 3.53 us: paired(): where = jnp.stack([col.astype(jnp.int32), order[k], choice])]
  transfers between devices with their start and end apart: 4 -> 28, of which waited for: 3 -> 13; matrix products, arithmetic and copies ran while one was open for 10% -> 5% of each run, Pallas kernels for 0% -> 19%
where the time goes in v1:
time: 170 us
  waiting for transfers between devices  77.5 us (46%)
  Pallas kernels  44.8 us (26%)
  starting transfers between devices  27.5 us (16%)
  local copies, waits for them, and re-layouts  12.5 us (7%)
  other arithmetic  6.29 us (4%)
    ppermute x8, waiting for transfers between devices, pole_step(): lax.ppermute(b, 'pole', pole_pairs(n_pole, bits[-1 - step]))  60.8 us
    pallas_call x4, Pallas kernels, unit_call(): pl.pallas_call(functools.partial(unit_kernel, len(shards) // 2, first_uni...  35.8 us
    ppermute x5, waiting for transfers between devices, advance(): moved[kind, slot] = lax.ppermute(moved[1 - kind, slot - 1], 'row', pairs)  12.6 us
    unnamed x36, local copies, waits for them, and re-layouts  10.1 us
    ppermute x8, starting transfers between devices, pole_step(): lax.ppermute(b, 'pole', pole_pairs(n_pole, bits[-1 - step]))  9.94 us
    ppermute x5, starting transfers between devices, advance(): moved[kind, slot] = lax.ppermute(moved[1 - kind, slot - 1], 'row', pairs)  8.08 us
    ppermute x8, starting transfers between devices, pole_step(): lax.ppermute(a, 'pole', pole_pairs(n_pole, bits[step]))  7.83 us
    pallas_call x1, Pallas kernels, prepare(): pl.pallas_call(functools.partial(prepare_kernel, w0 // pattern.shape[1]),...  4.79 us
  transfers between devices with their start and end apart: 28, of which 13 were waited for; matrix products, arithmetic and copies ran while one was open for 5% of the time, Pallas kernels for 19%

profile of v1, /device:TPU:0, one launch (start us, length us, event | category | flops | bytes accessed | tf_op | source)
XLA Modules:
  0.0 169.5 jit_solution(12919692022326604675)
XLA Ops:
  1.2 3.0 %collective-permute-start = (f32[2,128,1024]{2,1,0:T(8,128)}, f32[2,128,1024]{2,1,0:T(8,128)S(1)}, u32[]{:S(2)}, u32[]{:S(2)}) collective-permute-start(f32[2,128,1024]{2,1,0:T(8,128)} %refs_0_.1), channel_id=1, source_target_pairs={{0,2},{2,0},{4,6},{6,4},{1,3},{3,1},{5,7},{7,5},{8,10},{10,8},{12,... | collective-permute-start | bytes 3145736 | tf_op jit(solution)/shard_map/ppermute | solution.py:414
  4.2 1.6 collective-permute-start.1
  7.9 1.6 copy-done.8
  9.5 1.6 copy-done.9
  11.7 4.8 %prepare.1 = (bf16[2,1024,768]{2,1,0:T(8,128)(2,1)S(1)}, bf16[2,1024,768]{2,1,0:T(8,128)(2,1)S(1)}, bf16[2,1024,256]{2,1,0:T(8,128)(2,1)S(1)}, bf16[2,1024,256]{2,1,0:T(8,128)(2,1)S(1)}) custom-call(s32[2]{0:T(128)S(1)} %pad_add_fusion.3.where, s32[1,8]{1,0:T(1,128)S(1)} %copy-done.12, f32[2,1024,256]{2,1,0:T(8,128)S(1)} %bitcast.17, ...), custom_call_target="tpu_custom_call" | custom-call | flops 1610612736 | bytes 15728640 | tf_op jit(solution)/shard_map/prepare/pallas_call | solution.py:111
  16.5 1.6 copy-done.1
  18.1 8.3 %unit.4 = (f32[256,512]{1,0:T(8,128)S(1)}, f32[256,512]{1,0:T(8,128)S(1)}, f32[2,768,512]{2,1,0:T(8,128)S(1)}, f32[2,256,256]{2,1,0:T(8,128)S(1)}) custom-call(s32[3]{0:T(128)S(1)} %pad_add_fusion.1.where, f32[2]{0:T(128)S(1)} %copy-done.11, f32[2,128,1024]{2,1,0:T(8,128)S(1)} %copy-done.13, f32[2,128,1024]{2,1,0:T(8,128)} %collective-permute-done.2.refs_1_, ...), custom_call_target="tpu_custom_call" | custom-call | flops 3825205248 | bytes 16777216 | tf_op jit(solution)/shard_map/unit/pallas_call | solution.py:245
  28.6 1.8 %collective-permute-start.9 = (f32[256,512]{1,0:T(8,128)S(1)}, f32[256,512]{1,0:T(8,128)S(1)}, u32[]{:S(2)}, u32[]{:S(2)}) collective-permute-start(f32[256,512]{1,0:T(8,128)S(1)} %get-tuple-element.80), channel_id=1, source_target_pairs={{0,16},{8,24},{16,0},{24,8},{1,17},{9,25},{17,1},{25,9},{2,18},{10... | collective-permute-start | bytes 1572872 | tf_op jit(solution)/shard_map/ppermute | solution.py:374
  33.3 9.7 %collective-permute-done.9 = f32[256,512]{1,0:T(8,128)S(1)} collective-permute-done((f32[256,512]{1,0:T(8,128)S(1)}, f32[256,512]{1,0:T(8,128)S(1)}, u32[]{:S(2)}, u32[]{:S(2)}) %collective-permute-start.9) | collective-permute-done | bytes 524320 | tf_op jit(solution)/shard_map/ppermute | solution.py:374
  43.1 1.7 %collective-permute-start.10 = (f32[256,512]{1,0:T(8,128)S(1)}, f32[256,512]{1,0:T(8,128)S(1)}, u32[]{:S(2)}, u32[]{:S(2)}) collective-permute-start(f32[256,512]{1,0:T(8,128)S(1)} %add.36.refs_2_), channel_id=1, source_target_pairs={{0,8},{8,0},{16,24},{24,16},{1,9},{9,1},{17,25},{25,17},{2,10},{10... | collective-permute-start | bytes 1572872 | tf_op jit(solution)/shard_map/ppermute | solution.py:374
  47.8 8.0 %unit.5 = (f32[128,512]{1,0:T(8,128)S(1)}, f32[128,512]{1,0:T(8,128)S(1)}, f32[2,768,512]{2,1,0:T(8,128)S(1)}, f32[2,256,256]{2,1,0:T(8,128)S(1)}) custom-call(s32[3]{0:T(128)S(1)} %pad_add_fusion.where, f32[2]{0:T(128)S(1)} %copy-done.11, f32[2,128,1024]{2,1,0:T(8,128)S(1)} %collective-permute-done.refs_0_, ...), custom_call_target="tpu_custom_call" | custom-call | flops 3825205248 | bytes 16777216 | tf_op jit(solution)/shard_map/unit/pallas_call | solution.py:245
  55.8 1.7 %copy-done.4 = f32[2,768,512]{2,1,0:T(8,128)} copy-done((f32[2,768,512]{2,1,0:T(8,128)}, f32[2,768,512]{2,1,0:T(8,128)S(1)}, u32[]{:S(2)}) %copy-start.4) | copy-done | bytes 3145752
  57.5 5.2 %collective-permute-done.4.refs_0_ = f32[2,128,1024]{2,1,0:T(8,128)S(1)} collective-permute-done((f32[2,128,1024]{2,1,0:T(8,128)}, f32[2,128,1024]{2,1,0:T(8,128)S(1)}, u32[]{:S(2)}, u32[]{:S(2)}) %collective-permute-start.4) | collective-permute-done | bytes 1048608 | tf_op jit(solution)/shard_map/ppermute | solution.py:414
  69.3 3.8 %collective-permute-done.16 = f32[128,512]{1,0:T(8,128)S(1)} collective-permute-done((f32[128,512]{1,0:T(8,128)S(1)}, f32[128,512]{1,0:T(8,128)S(1)}, u32[]{:S(2)}, u32[]{:S(2)}) %collective-permute-start.16) | collective-permute-done | bytes 262176 | tf_op jit(solution)/shard_map/ppermute | solution.py:374
  75.4 8.2 %unit.6 = (f32[128,512]{1,0:T(8,128)S(1)}, f32[128,512]{1,0:T(8,128)S(1)}, f32[2,768,512]{2,1,0:T(8,128)S(1)}, f32[2,256,256]{2,1,0:T(8,128)S(1)}) custom-call(s32[3]{0:T(128)S(1)} %add_add_fusion.where, f32[2]{0:T(128)S(1)} %copy-done.11, f32[2,128,1024]{2,1,0:T(8,128)S(1)} %collective-permute-done.4.refs_0_, ...), custom_call_target="tpu_custom_call" | custom-call | flops 3825205248 | bytes 16777216 | tf_op jit(solution)/shard_map/unit/pallas_call | solution.py:245
  83.6 1.7 %copy-done.6 = f32[2,768,512]{2,1,0:T(8,128)} copy-done((f32[2,768,512]{2,1,0:T(8,128)}, f32[2,768,512]{2,1,0:T(8,128)S(1)}, u32[]{:S(2)}) %copy-start.6) | copy-done | bytes 3145752
  85.3 6.0 %collective-permute-done.11.refs_0_ = f32[2,128,1024]{2,1,0:T(8,128)S(1)} collective-permute-done((f32[2,128,1024]{2,1,0:T(8,128)S(1)}, f32[2,128,1024]{2,1,0:T(8,128)S(1)}, u32[]{:S(2)}, u32[]{:S(2)}) %collective-permute-start.11) | collective-permute-done | bytes 1048608 | tf_op jit(solution)/shard_map/ppermute | solution.py:414
  95.5 11.3 %unit.7 = (f32[448,512]{1,0:T(8,128)S(1)}, f32[448,512]{1,0:T(8,128)S(1)}) custom-call(s32[3]{0:T(128)S(1)} %add_add_fusion.1.where, f32[2]{0:T(128)S(1)} %copy-done.11, f32[2,128,1024]{2,1,0:T(8,128)S(1)} %collective-permute-done.11.refs_0_, f32[2,128,1024]{2,1,0:T(8,128)S(1)} %collective-permute-done.22.refs_1_, ...), custom_call_target="tpu_custom_call" | custom-call | flops 3825205248 | bytes 16777216 | tf_op jit(solution)/shard_map/unit/pallas_call | solution.py:245
  109.1 20.2 %collective-permute-done.26 = f32[448,512]{1,0:T(8,128)S(1)} collective-permute-done((f32[448,512]{1,0:T(8,128)S(1)}, f32[448,512]{1,0:T(8,128)S(1)}, u32[]{:S(2)}, u32[]{:S(2)}) %collective-permute-start.26) | collective-permute-done | bytes 917536 | tf_op jit(solution)/shard_map/ppermute | solution.py:374
  133.8 24.3 %collective-permute-done.20 = f32[128,512]{1,0:T(8,128)S(1)} collective-permute-done((f32[128,512]{1,0:T(8,128)S(1)}, f32[128,512]{1,0:T(8,128)S(1)}, u32[]{:S(2)}, u32[]{:S(2)}) %collective-permute-start.20) | collective-permute-done | bytes 262176 | tf_op jit(solution)/shard_map/ppermute | solution.py:374
  159.8 2.0 %pad_add_fusion.2.order = s32[4]{0:T(128)S(1)} fusion(s32[1]{0:T(128)} %dynamic_slice.27, s32[1]{0:T(128)} %dynamic_slice.26, s32[1]{0:T(128)} %dynamic_slice.25, s32[1]{0:T(128)} %bitcast), kind=kLoop, calls=%fused_computation.2 | loop fusion | flops 12 | bytes 32 | tf_op jit(solution)/shard_map/stack | solution.py:446
  161.8 2.8 %collective-permute-done.21.refs_11_ = f32[128,512]{1,0:T(8,128)S(1)} collective-permute-done((f32[128,512]{1,0:T(8,128)S(1)}, f32[128,512]{1,0:T(8,128)S(1)}, u32[]{:S(2)}, u32[]{:S(2)}) %collective-permute-start.21) | collective-permute-done | bytes 262176 | tf_op jit(solution)/shard_map/ppermute | solution.py:374
  165.2 2.3 %place.1 = (f32[128,1024]{1,0:T(8,128)}, f32[1024,256]{1,0:T(8,128)}, f32[1024,256]{1,0:T(8,128)}) custom-call(s32[4]{0:T(128)S(1)} %pad_add_fusion.2.order, f32[256,512]{1,0:T(8,128)S(1)} %add.35.refs_0_, f32[256,512]{1,0:T(8,128)S(1)} %collective-permute-done.8.refs_1_, f32[256,512]{1,0:T(8,128)S(1)} %add.36.refs_2_, ...), custom_call_target="tpu_custom_call" | custom-call | flops 1048576 | bytes 8388608 | tf_op jit(solution)/shard_map/place/pallas_call | solution.py:287
  167.5 2.0 %finish.1 = (f32[1024,256]{1,0:T(8,128)}, f32[1024,256]{1,0:T(8,128)}, f32[256,512]{1,0:T(8,128)}, f32[512,256]{1,0:T(8,128)}, f32[256,256]{1,0:T(8,128)}) custom-call(s32[3]{0:T(128)S(1)} %add_add_fusion.1.where, f32[448,512]{1,0:T(8,128)S(1)} %add.41.a, f32[448,512]{1,0:T(8,128)S(1)} %collective-permute-done.25.a_in, ...), custom_call_target="tpu_custom_call", output_to_operand_aliasing={{0}: (5, {}), {1}: (6, {})} | custom-call | flops 1048576 | bytes 6291456 | tf_op jit(solution)/shard_map/finish/pallas_call | solution.py:331
  (93 shorter events, 33.4 us)
Async XLA Ops:
  1.1 17.0 %collective-permute-start.2 = (f32[2,128,1024]{2,1,0:T(8,128)}, f32[2,128,1024]{2,1,0:T(8,128)}, u32[]{:S(2)}, u32[]{:S(2)}) collective-permute-start(f32[2,128,1024]{2,1,0:T(8,128)} %refs_0_.1), channel_id=1, source_target_pairs={{0,1},{1,0},{2,3},{3,2},{4,5},{5,4},{6,7},{7,6},{8,9},{9,8},{10,11... | collective-permute-start | bytes 3145736 | tf_op jit(solution)/shard_map/ppermute | solution.py:408
  1.2 26.6 %collective-permute-start = (f32[2,128,1024]{2,1,0:T(8,128)}, f32[2,128,1024]{2,1,0:T(8,128)S(1)}, u32[]{:S(2)}, u32[]{:S(2)}) collective-permute-start(f32[2,128,1024]{2,1,0:T(8,128)} %refs_0_.1), channel_id=1, source_target_pairs={{0,2},{2,0},{4,6},{6,4},{1,3},{3,1},{5,7},{7,5},{8,10},{10,8},{12,... | collective-permute-start | bytes 3145736 | tf_op jit(solution)/shard_map/ppermute | solution.py:414
  4.2 23.6 %collective-permute-start.1 = (f32[2,128,1024]{2,1,0:T(8,128)}, f32[2,128,1024]{2,1,0:T(8,128)}, u32[]{:S(2)}, u32[]{:S(2)}) collective-permute-start(f32[2,128,1024]{2,1,0:T(8,128)} %refs_0_.1), channel_id=1, source_target_pairs={{2,4},{4,2},{3,5},{5,3},{10,12},{12,10},{11,13},{13,11},{18,20},{2... | collective-permute-start | bytes 3145736 | tf_op jit(solution)/shard_map/ppermute | solution.py:414
  27.8 19.9 %collective-permute-start.6 = (f32[2,128,1024]{2,1,0:T(8,128)S(1)}, f32[2,128,1024]{2,1,0:T(8,128)S(1)}, u32[]{:S(2)}, u32[]{:S(2)}) collective-permute-start(f32[2,128,1024]{2,1,0:T(8,128)S(1)} %collective-permute-done.refs_0_), channel_id=1, source_target_pairs={{0,1},{1,0},{2,3},{3,2},{4,5},{5,4},{6,7},{7,6},{8,9},{9,8},{10,11... | collective-permute-start | bytes 3145736 | tf_op jit(solution)/shard_map/ppermute | solution.py:408
  27.8 34.8 %collective-permute-start.5 = (f32[2,128,1024]{2,1,0:T(8,128)S(1)}, f32[2,128,1024]{2,1,0:T(8,128)S(1)}, u32[]{:S(2)}, u32[]{:S(2)}) collective-permute-start(f32[2,128,1024]{2,1,0:T(8,128)S(1)} %collective-permute-done.refs_0_), channel_id=1, source_target_pairs={{2,4},{4,2},{3,5},{5,3},{10,12},{12,10},{11,13},{13,11},{18,20},{2... | collective-permute-start | bytes 3145736 | tf_op jit(solution)/shard_map/ppermute | solution.py:414
  28.6 14.4 %collective-permute-start.9 = (f32[256,512]{1,0:T(8,128)S(1)}, f32[256,512]{1,0:T(8,128)S(1)}, u32[]{:S(2)}, u32[]{:S(2)}) collective-permute-start(f32[256,512]{1,0:T(8,128)S(1)} %get-tuple-element.80), channel_id=1, source_target_pairs={{0,16},{8,24},{16,0},{24,8},{1,17},{9,25},{17,1},{25,9},{2,18},{10... | collective-permute-start | bytes 1572872 | tf_op jit(solution)/shard_map/ppermute | solution.py:374
  30.4 32.3 %collective-permute-start.4 = (f32[2,128,1024]{2,1,0:T(8,128)}, f32[2,128,1024]{2,1,0:T(8,128)S(1)}, u32[]{:S(2)}, u32[]{:S(2)}) collective-permute-start(f32[2,128,1024]{2,1,0:T(8,128)} %collective-permute-done.1.refs_2_), channel_id=1, source_target_pairs={{2,0},{4,6},{3,1},{5,7},{10,8},{12,14},{11,9},{13,15},{18,16},{20,... | collective-permute-start | bytes 3145736 | tf_op jit(solution)/shard_map/ppermute | solution.py:414
  31.7 14.3 %collective-permute-start.7 = (f32[256,512]{1,0:T(8,128)S(1)}, f32[256,512]{1,0:T(8,128)S(1)}, u32[]{:S(2)}, u32[]{:S(2)}) collective-permute-start(f32[256,512]{1,0:T(8,128)S(1)} %get-tuple-element.79), channel_id=1, source_target_pairs={{0,8},{8,0},{16,24},{24,16},{1,9},{9,1},{17,25},{25,17},{2,10},{10... | collective-permute-start | bytes 1572872 | tf_op jit(solution)/shard_map/ppermute | solution.py:373
  43.1 19.6 %collective-permute-start.10 = (f32[256,512]{1,0:T(8,128)S(1)}, f32[256,512]{1,0:T(8,128)S(1)}, u32[]{:S(2)}, u32[]{:S(2)}) collective-permute-start(f32[256,512]{1,0:T(8,128)S(1)} %add.36.refs_2_), channel_id=1, source_target_pairs={{0,8},{8,0},{16,24},{24,16},{1,9},{9,1},{17,25},{25,17},{2,10},{10... | collective-permute-start | bytes 1572872 | tf_op jit(solution)/shard_map/ppermute | solution.py:374
  46.1 16.6 %collective-permute-start.8 = (f32[256,512]{1,0:T(8,128)S(1)}, f32[256,512]{1,0:T(8,128)S(1)}, u32[]{:S(2)}, u32[]{:S(2)}) collective-permute-start(f32[256,512]{1,0:T(8,128)S(1)} %add.35.refs_0_), channel_id=1, source_target_pairs={{0,16},{8,24},{16,0},{24,8},{1,17},{9,25},{17,1},{25,9},{2,18},{10... | collective-permute-start | bytes 1572872 | tf_op jit(solution)/shard_map/ppermute | solution.py:373
  62.7 12.7 %collective-permute-start.12 = (f32[2,128,1024]{2,1,0:T(8,128)S(1)}, f32[2,128,1024]{2,1,0:T(8,128)S(1)}, u32[]{:S(2)}, u32[]{:S(2)}) collective-permute-start(f32[2,128,1024]{2,1,0:T(8,128)S(1)} %collective-permute-done.4.refs_0_), channel_id=1, source_target_pairs={{0,1},{1,0},{2,3},{3,2},{4,5},{5,4},{6,7},{7,6},{8,9},{9,8},{10,11... | collective-permute-start | bytes 3145736 | tf_op jit(solution)/shard_map/ppermute | solution.py:408
  62.8 12.6 %collective-permute-start.13 = (f32[2,128,1024]{2,1,0:T(8,128)}, f32[2,128,1024]{2,1,0:T(8,128)S(1)}, u32[]{:S(2)}, u32[]{:S(2)}) collective-permute-start(f32[2,128,1024]{2,1,0:T(8,128)} %collective-permute-done.1.refs_2_), channel_id=1, source_target_pairs={{0,1},{1,0},{2,3},{3,2},{4,5},{5,4},{6,7},{7,6},{8,9},{9,8},{10,11... | collective-permute-start | bytes 3145736 | tf_op jit(solution)/shard_map/ppermute | solution.py:408
  63.3 28.0 %collective-permute-start.11 = (f32[2,128,1024]{2,1,0:T(8,128)S(1)}, f32[2,128,1024]{2,1,0:T(8,128)S(1)}, u32[]{:S(2)}, u32[]{:S(2)}) collective-permute-start(f32[2,128,1024]{2,1,0:T(8,128)S(1)} %collective-permute-done.5.refs_2_), channel_id=1, source_target_pairs={{2,0},{4,6},{3,1},{5,7},{10,8},{12,14},{11,9},{13,15},{18,16},{20,... | collective-permute-start | bytes 3145736 | tf_op jit(solution)/shard_map/ppermute | solution.py:414
  64.7 8.4 %collective-permute-start.16 = (f32[128,512]{1,0:T(8,128)S(1)}, f32[128,512]{1,0:T(8,128)S(1)}, u32[]{:S(2)}, u32[]{:S(2)}) collective-permute-start(f32[128,512]{1,0:T(8,128)S(1)} %get-tuple-element.95), channel_id=1, source_target_pairs={{0,16},{8,24},{16,0},{24,8},{1,17},{9,25},{17,1},{25,9},{2,18},{10... | collective-permute-start | bytes 786440 | tf_op jit(solution)/shard_map/ppermute | solution.py:374
  65.3 9.4 %collective-permute-start.14 = (f32[128,512]{1,0:T(8,128)S(1)}, f32[128,512]{1,0:T(8,128)S(1)}, u32[]{:S(2)}, u32[]{:S(2)}) collective-permute-start(f32[128,512]{1,0:T(8,128)S(1)} %get-tuple-element.94), channel_id=1, source_target_pairs={{0,8},{8,0},{16,24},{24,16},{1,9},{9,1},{17,25},{25,17},{2,10},{10... | collective-permute-start | bytes 786440 | tf_op jit(solution)/shard_map/ppermute | solution.py:373
  73.1 12.1 %collective-permute-start.17 = (f32[128,512]{1,0:T(8,128)S(1)}, f32[128,512]{1,0:T(8,128)S(1)}, u32[]{:S(2)}, u32[]{:S(2)}) collective-permute-start(f32[128,512]{1,0:T(8,128)S(1)} %add.38.refs_6_), channel_id=1, source_target_pairs={{0,8},{8,0},{16,24},{24,16},{1,9},{9,1},{17,25},{25,17},{2,10},{10... | collective-permute-start | bytes 786440 | tf_op jit(solution)/shard_map/ppermute | solution.py:374
  74.8 10.5 %collective-permute-start.15 = (f32[128,512]{1,0:T(8,128)S(1)}, f32[128,512]{1,0:T(8,128)S(1)}, u32[]{:S(2)}, u32[]{:S(2)}) collective-permute-start(f32[128,512]{1,0:T(8,128)S(1)} %add.37.refs_4_), channel_id=1, source_target_pairs={{0,16},{8,24},{16,0},{24,8},{1,17},{9,25},{17,1},{25,9},{2,18},{10... | collective-permute-start | bytes 786440 | tf_op jit(solution)/shard_map/ppermute | solution.py:373
  106.8 22.5 %collective-permute-start.26 = (f32[448,512]{1,0:T(8,128)S(1)}, f32[448,512]{1,0:T(8,128)S(1)}, u32[]{:S(2)}, u32[]{:S(2)}) collective-permute-start(f32[448,512]{1,0:T(8,128)S(1)} %get-tuple-element.112), channel_id=1, source_target_pairs={{0,16},{8,24},{16,0},{24,8},{1,17},{9,25},{17,1},{25,9},{2,18},{10... | collective-permute-start | bytes 2752520 | tf_op jit(solution)/shard_map/ppermute | solution.py:374
  107.6 23.4 %collective-permute-start.24 = (f32[448,512]{1,0:T(8,128)S(1)}, f32[448,512]{1,0:T(8,128)S(1)}, u32[]{:S(2)}, u32[]{:S(2)}) collective-permute-start(f32[448,512]{1,0:T(8,128)S(1)} %get-tuple-element.111), channel_id=1, source_target_pairs={{0,8},{8,0},{16,24},{24,16},{1,9},{9,1},{17,25},{25,17},{2,10},{10... | collective-permute-start | bytes 2752520 | tf_op jit(solution)/shard_map/ppermute | solution.py:373
  129.4 38.1 %collective-permute-start.27 = (f32[448,512]{1,0:T(8,128)S(1)}, f32[448,512]{1,0:T(8,128)S(1)}, u32[]{:S(2)}, u32[]{:S(2)}) collective-permute-start(f32[448,512]{1,0:T(8,128)S(1)} %add.42.b), channel_id=1, source_target_pairs={{0,8},{8,0},{16,24},{24,16},{1,9},{9,1},{17,25},{25,17},{2,10},{10... | collective-permute-start | bytes 2752520 | tf_op jit(solution)/shard_map/ppermute | solution.py:374
  131.2 36.3 %collective-permute-start.25 = (f32[448,512]{1,0:T(8,128)S(1)}, f32[448,512]{1,0:T(8,128)S(1)}, u32[]{:S(2)}, u32[]{:S(2)}) collective-permute-start(f32[448,512]{1,0:T(8,128)S(1)} %add.41.a), channel_id=1, source_target_pairs={{0,16},{8,24},{16,0},{24,8},{1,17},{9,25},{17,1},{25,9},{2,18},{10... | collective-permute-start | bytes 2752520 | tf_op jit(solution)/shard_map/ppermute | solution.py:373
  131.9 26.2 %collective-permute-start.20 = (f32[128,512]{1,0:T(8,128)S(1)}, f32[128,512]{1,0:T(8,128)S(1)}, u32[]{:S(2)}, u32[]{:S(2)}) collective-permute-start(f32[128,512]{1,0:T(8,128)S(1)} %get-tuple-element.105), channel_id=1, source_target_pairs={{0,16},{8,24},{16,0},{24,8},{1,17},{9,25},{17,1},{25,9},{2,18},{10... | collective-permute-start | bytes 786440 | tf_op jit(solution)/shard_map/ppermute | solution.py:374
  133.2 25.5 %collective-permute-start.18 = (f32[128,512]{1,0:T(8,128)S(1)}, f32[128,512]{1,0:T(8,128)S(1)}, u32[]{:S(2)}, u32[]{:S(2)}) collective-permute-start(f32[128,512]{1,0:T(8,128)S(1)} %get-tuple-element.104), channel_id=1, source_target_pairs={{0,8},{8,0},{16,24},{24,16},{1,9},{9,1},{17,25},{25,17},{2,10},{10... | collective-permute-start | bytes 786440 | tf_op jit(solution)/shard_map/ppermute | solution.py:373
  158.2 6.4 %collective-permute-start.21 = (f32[128,512]{1,0:T(8,128)S(1)}, f32[128,512]{1,0:T(8,128)S(1)}, u32[]{:S(2)}, u32[]{:S(2)}) collective-permute-start(f32[128,512]{1,0:T(8,128)S(1)} %add.40.refs_10_), channel_id=1, source_target_pairs={{0,8},{8,0},{16,24},{24,16},{1,9},{9,1},{17,25},{25,17},{2,10},{10... | collective-permute-start | bytes 786440 | tf_op jit(solution)/shard_map/ppermute | solution.py:374
  (22 other events, 258.6 us)

commit v2 on v0

v2 whole, which is shorter than its diff:
```python
import functools

import jax
import jax.numpy as jnp
from jax import lax
from jax.experimental import pallas as pl
from jax.experimental.pallas import tpu as pltpu
from jax.sharding import PartitionSpec as P

HIGH = lax.Precision.HIGH
SWAP = [(0, 1), (1, 0)]
MIB = 1 << 20


def product(left, right):
    return jnp.matmul(left, right, precision=HIGH)


def left_t(left, right):
    return jnp.einsum("pki,pkj->pij", left, right, precision=HIGH)


def weighted(weights, values):
    return jnp.sum(weights[:, None, None] * values, axis=0)


def general(
    root_inverse,
    node_factor,
    node_inverse,
    leaf_root_factor,
    leaf_node_factor,
    leaf_inverse,
    leaf_pattern,
    pole_weight,
):
    inv_n, leaf_n, inv_l = node_inverse[:, 0], leaf_node_factor[:, 0], leaf_inverse[:, 0]
    w1, width = inv_n.shape[2], node_factor.shape[3]
    start = lax.axis_index("col") * width
    row_mask = jnp.repeat(leaf_pattern[0].astype(jnp.float32), leaf_root_factor.shape[2] // leaf_pattern.shape[1])
    leaf = leaf_root_factor[:, 0] * row_mask[None, :, None]
    factor = lax.all_gather(node_factor[:, 0], "col", axis=2, tiled=True)
    root = lax.all_gather(root_inverse, ("row", "col"), axis=1, tiled=True)
    x = product(root, jnp.concatenate([factor, leaf - product(factor, leaf_n)], axis=2))
    gram = left_t(jnp.concatenate([factor, leaf], axis=2), x)
    sep = inv_n + gram[:, :w1, :w1]
    middle = jnp.swapaxes(gram[:, w1:, :w1], 1, 2) - product(sep, leaf_n)
    lower = inv_l + gram[:, w1:, w1:] - left_t(leaf_n, middle)
    rows = -weighted(pole_weight, x)
    totals = lax.psum(
        (
            weighted(pole_weight, root_inverse),
            lax.dynamic_slice_in_dim(rows, start, width, 1),
            lax.dynamic_slice_in_dim(weighted(pole_weight, sep), start, width, 0),
            rows[:, w1:],
            weighted(pole_weight, middle),
            weighted(pole_weight, lower),
        ),
        "pole",
    )
    return (totals[0],) + tuple(t[None] for t in totals[1:])


VMEM = pl.BlockSpec(memory_space=pltpu.VMEM)
SMEM = pl.BlockSpec(memory_space=pltpu.SMEM)
ACROSS = ((0,), (0,))


def call(kernel, name, outs, args, smem, **options):
    return pl.pallas_call(
        kernel,
        in_specs=[SMEM] * smem + [VMEM] * (len(args) - smem),
        out_specs=[VMEM] * len(outs),
        out_shape=outs,
        compiler_params=pltpu.CompilerParams(vmem_limit_bytes=20 * MIB),
        cost_estimate=pl.CostEstimate(flops=1, bytes_accessed=1, transcendentals=0),
        name=name,
        **options,
    )(*args)


def split(x):
    high = x.astype(jnp.bfloat16)
    return high, (x - high.astype(jnp.float32)).astype(jnp.bfloat16)


def dot3(left, right, dims=((1,), (0,))):
    def one(a, b):
        return lax.dot_general(a, b, (dims, ((), ())), preferred_element_type=jnp.float32)

    return one(left[0], right[0]) + (one(left[0], right[1]) + one(left[1], right[0]))


def pick(table, row):
    value = jnp.int32(table[0])
    for j in range(1, len(table)):
        value = jnp.where(row == j, table[j], value)
    return value


def prepare_kernel(
    where, pattern, f_other, f_hbm, leaf_hbm, leaf_n_hbm, w_high, w_low, l_high, l_low, f_own, leaf, leaf_n, sems, n_sems
):
    poles, w0, width = f_own.shape
    w1 = 2 * width
    block = w0 // pattern.shape[1]
    rows = w0 // sems.shape[1]
    first = where[0] == 0

    def copies(p, i):
        here = pl.ds(i * rows, rows)
        return [
            pltpu.make_async_copy(hbm.at[p, here], ref.at[p, here], sems.at[p, i, j])
            for j, (hbm, ref) in enumerate([(f_hbm, f_own), (leaf_hbm, leaf)])
        ]

    def copy_n(p):
        return pltpu.make_async_copy(leaf_n_hbm.at[p], leaf_n.at[p], n_sems.at[p])

    for p in range(poles):
        copy_n(p).start()
        for i in range(w0 // rows):
            for copy in copies(p, i):
                copy.start()
    for p in range(poles):
        copy_n(p).wait()
        ns = split(leaf_n[p])
        for i in range(w0 // rows):
            for copy in copies(p, i):
                copy.wait()
            here = pl.ds(i * rows, rows)
            own, other = f_own[p, here], f_other[p, here]
            f = jnp.concatenate([jnp.where(first, own, other), jnp.where(first, other, own)], axis=1)
            masked = leaf[p, here]
            kept = []
            for j in range(0, rows, block):
                kept.append(jnp.where(pattern[0, (i * rows + j) // block] != 0, masked[j : j + block], 0.0))
            masked = jnp.concatenate(kept, axis=0)
            fs = split(f)
            ds = split(masked - dot3(fs, ns))
            w_high[p, here, :w1], w_low[p, here, :w1] = fs
            w_high[p, here, w1:], w_low[p, here, w1:] = ds
            l_high[p, here], l_low[p, here] = split(masked)


def prepare(where, pattern, f_own, f_other, leaf, leaf_n):
    poles, w0, width = f_own.shape
    w1, w2 = leaf_n.shape[1:]
    parts = 4
    hbm = [pltpu.with_memory_space_constraint(x, pltpu.HBM) for x in (f_own, leaf, leaf_n)]
    return pl.pallas_call(
        prepare_kernel,
        in_specs=[SMEM] * 2 + [VMEM] + [pl.BlockSpec(memory_space=pltpu.HBM)] * 3,
        out_specs=[VMEM] * 4,
        out_shape=[pltpu.VMEM((poles, w0, n), jnp.bfloat16) for n in (w1 + w2, w1 + w2, w2, w2)],
        scratch_shapes=[
            pltpu.VMEM((poles, w0, width), jnp.float32),
            pltpu.VMEM((poles, w0, w2), jnp.float32),
            pltpu.VMEM((poles, w1, w2), jnp.float32),
            pltpu.SemaphoreType.DMA((poles, parts, 2)),
            pltpu.SemaphoreType.DMA((poles,)),
        ],
        compiler_params=pltpu.CompilerParams(vmem_limit_bytes=20 * MIB),
        cost_estimate=pl.CostEstimate(flops=1, bytes_accessed=1, transcendentals=0),
        name="prepare",
    )(where, pattern, f_other, *hbm)


def unit_kernel(form, slots, owners, slot_of, ways, where, weight, *refs):
    count = {"first": 1, "next": 2, "part": 1, "last": 1}[form]
    shards, refs = refs[: 2 * slots * count], refs[2 * slots * count :]
    (w_high, w_low, l_high, l_low), refs = refs[:4], refs[4:]
    if form in ("next", "last"):
        (gram_in, square_in), refs = refs[:2], refs[2:]
    if form == "last":
        (kept_rows, kept_high, kept_low, inv_n, leaf_n, inv_l), refs = refs[:6], refs[6:]
    if form == "last":
        outs, (r_high, r_low, sent_at, rest_at) = refs[:-4], refs[-4:]
    else:
        outs, (r_high, r_low) = refs[:-2], refs[-2:]
    col, row = where[0], where[1]
    owner, slot, way = (pick(table, row) for table in (owners, slot_of, ways))
    poles, rows, _ = shards[0].shape
    w2 = l_high.shape[2]
    w1 = w_high.shape[2] - w2
    width = w1 // 2
    begin = [pl.multiple_of(jnp.where(way == i, 0, rows), rows) for i in range(2)]
    if form == "first":
        for i in range(2):
            at = pl.ds(pl.multiple_of(jnp.where(col == i, 0, rows), rows), rows)
            for p in range(poles):
                r_high[p, at], r_low[p, at] = split(shards[i][p])
    else:
        for i in range(count):
            at = pl.ds(begin[i] if count == 2 else 0, rows)
            for s in range(slots):
                for j in range(2):
                    ref = shards[(2 * s + j) * count + i]

                    @pl.when((slot == s) & ((way == col) == (j == 0)))
                    def _():
                        for p in range(poles):
                            r_high[p, at], r_low[p, at] = split(ref[p])

    span = r_high.shape[1]
    base = owner * 2 * rows
    if form == "last":
        heres = [pl.ds(pl.multiple_of(base + begin[i], rows), rows) for i in range(2)]
    else:
        heres = [pl.ds(pl.multiple_of(base, 2 * rows), span)]
    for p in range(poles):
        x = dot3((r_high[p], r_low[p]), (w_high[p], w_low[p]))
        scale = weight[p]
        mine = jnp.where(col == 0, x[:, :width], x[:, width:w1])
        sent = -scale * jnp.concatenate([mine, x[:, w1:]], axis=1)
        sent_ref = sent_at if form == "last" else outs[0]
        if p == 0:
            sent_ref[...] = sent
        else:
            sent_ref[...] += sent
        xs = split(x)
        if form == "part":
            outs[1][p], outs[2][p] = xs
            continue
        if form == "last":
            xs = [jnp.concatenate([kept[p], v], axis=0) for kept, v in zip((kept_high, kept_low), xs)]
        fs = [jnp.concatenate([w[p, here, :w1] for here in heres], axis=0) for w in (w_high, w_low)]
        ls = [jnp.concatenate([l[p, here] for here in heres], axis=0) for l in (l_high, l_low)]
        ps = [v[:, :w1] for v in xs]
        us = [v[:, w1:] for v in xs]
        cross = dot3(fs, ps, ACROSS)
        below = dot3(ls, ps, ACROSS)
        inner = dot3(ls, us, ACROSS)
        if form != "first":
            cross = cross + gram_in[p, :w1]
            below = below + gram_in[p, w1:]
            inner = inner + square_in[p]
        if form != "last":
            gram, square = outs[-2:]
            gram[p, :w1] = cross
            gram[p, w1:] = below
            square[p] = inner
            continue
        sep = inv_n[p] + cross
        ns = split(leaf_n[p])
        middle = below.T - dot3(split(sep), ns)
        lower = inv_l[p] + inner - dot3(ns, split(middle), ACROSS)
        sep = scale * jnp.where(col == 0, sep[:width], sep[width:])
        middle = scale * jnp.concatenate([middle[:width], middle[width:]], axis=1)
        lower = scale * jnp.concatenate([lower[: w2 // 2], lower[w2 // 2 :]], axis=1)
        value = jnp.concatenate([sep, middle, lower], axis=0)
        if p == 0:
            rest_at[...] = value
        else:
            rest_at[...] += value
    if form == "last":
        keep, send = outs
        head = keep.shape[0] - 2 * rows
        for i, halves in enumerate([(keep, send), (send, keep)]):

            @pl.when(where[2] == i)
            def _():
                halves[0][:rows] = kept_rows[...]
                halves[0][rows : 2 * rows] = sent_at[...]
                halves[0][2 * rows :] = rest_at[:head]
                halves[1][...] = rest_at[head:]


def unit_call(form, tables, where, weight, shards, factors, sums=(), ends=()):
    poles, rows, w0 = shards[0].shape
    lanes, w2 = factors[0].shape[2], factors[2].shape[2]
    w1 = lanes - w2
    f32 = jnp.float32
    gram = [pltpu.VMEM((poles, lanes, w1), f32), pltpu.VMEM((poles, w2, w2), f32)]
    outs = {
        "first": [pltpu.VMEM((2 * rows, w1), f32)] + gram,
        "next": [pltpu.VMEM((2 * rows, w1), f32)] + gram,
        "part": [pltpu.VMEM((rows, w1), f32)] + [pltpu.VMEM((poles, rows, lanes), jnp.bfloat16)] * 2,
        "last": [pltpu.VMEM(((2 * rows + w1 // 2 + w1 // 2 + w2 // 2) // 2, w1), f32)] * 2,
    }[form]
    args = [where, weight, *shards, *factors, *sums, *ends]
    slots = len(shards) // (4 if form == "next" else 2)
    span = rows * (2 if form in ("first", "next") else 1)
    options = {"scratch_shapes": [pltpu.VMEM((poles, span, w0), jnp.bfloat16)] * 2}
    if form == "last":
        options["scratch_shapes"] += [pltpu.VMEM((rows, w1), f32), pltpu.VMEM((w1 + w2 // 2, w1), f32)]
    if form == "next":
        options["input_output_aliases"] = {len(args) - 2: 1, len(args) - 1: 2}
    return list(call(functools.partial(unit_kernel, form, slots, *tables), form, outs, args, 2, **options))


def place_kernel(unit, owners, pieces, where, *refs):
    sums, (root, off, upper) = refs[:-3], refs[-3:]
    width = off.shape[1]
    for pair, start, rows, k, at in pieces:
        here = pl.ds(start, rows)
        total = sums[2 * pair][here] + sums[2 * pair + 1][here]
        if k is None:
            root[:, at : at + total.shape[1]] = total
            continue
        there = pl.ds(pl.multiple_of(pick(owners[k], where[1]) * unit + at, unit // 2), rows)
        off[there] = total[:, :width]
        upper[there] = total[:, width:]


def place(owners, pieces, where, sums, unit, w0, w2):
    w1 = sums[0].shape[1]
    outs = [jax.ShapeDtypeStruct(o, jnp.float32) for o in [(unit // 2, w0), (w0, w1 // 2), (w0, w2)]]
    return call(functools.partial(place_kernel, unit, owners, pieces), "place", outs, [where, *sums], 1)


def finish_kernel(unit, owners, ways, where, kept, got, _off, _upper, off, upper, sep, middle, lower, *scratch):
    off_part, upper_part, sem = scratch
    rows = unit // 2
    width = off.shape[1]
    w2 = lower.shape[1]
    head = kept.shape[0] - unit
    base, way = (pick(table, where[1]) for table in (owners, ways))
    copies = []
    for i in range(2):
        here = pl.ds(i * rows, rows)
        there = pl.ds(pl.multiple_of(base * unit + jnp.where(way == i, 0, rows), rows), rows)
        for part, out in [(off_part, off), (upper_part, upper)]:
            copies.append(pltpu.make_async_copy(part.at[here], out.at[there], sem.at[len(copies)]))
    for i, (a, b) in enumerate([(kept, got), (got, kept)]):

        @pl.when(where[2] == i)
        def _():
            off_part[...] = a[:unit, :width]
            upper_part[...] = a[:unit, width:]
            sep[:head] = a[unit:]
            sep[head:] = b[: width - head]
            at = width - head
            middle[:width] = b[at : at + width, :w2]
            middle[width:] = b[at : at + width, w2:]
            at += width
            lower[: w2 // 2] = b[at:, :w2]
            lower[w2 // 2 :] = b[at:, w2:]

    for copy in copies:
        copy.start()
    for copy in copies:
        copy.wait()


def finish(tables, where, kept, got, off, upper, unit, w1, w2):
    anywhere = pl.BlockSpec(memory_space=pl.ANY)
    shapes = [off.shape, upper.shape, (w1 // 2, w1), (w1, w2), (w2, w2)]
    return pl.pallas_call(
        functools.partial(finish_kernel, unit, *tables),
        in_specs=[SMEM] + [VMEM] * 2 + [anywhere] * 2,
        out_specs=[anywhere] * 2 + [VMEM] * 3,
        out_shape=[jax.ShapeDtypeStruct(s, jnp.float32) for s in shapes],
        scratch_shapes=[
            pltpu.VMEM((unit, w1 // 2), jnp.float32),
            pltpu.VMEM((unit, w2), jnp.float32),
            pltpu.SemaphoreType.DMA((4,)),
        ],
        input_output_aliases={3: 0, 4: 1},
        compiler_params=pltpu.CompilerParams(vmem_limit_bytes=20 * MIB),
        cost_estimate=pl.CostEstimate(flops=1, bytes_accessed=1, transcendentals=0),
        name="finish",
    )(where, kept, got, off, upper)


def line_plan(n):
    plan = []
    for j in range(n):
        above = [(s, 0, j + s) for s in range(1, n - j)]
        below = [(s, 1, j - s) for s in range(1, j + 1)]
        plan.append(sorted(above + below, key=lambda e: (e[0], e[1] if j < n // 2 else -e[1])))
    return plan


def together(*groups):
    flat, tree = jax.tree.flatten(groups)
    return jax.tree.unflatten(tree, lax.optimization_barrier(tuple(flat)))


def paired(
    n_pole,
    n_row,
    root_inverse,
    node_factor,
    node_inverse,
    leaf_root_factor,
    leaf_node_factor,
    leaf_inverse,
    leaf_pattern,
    pole_weight,
):
    pole, col = lax.axis_index("pole"), lax.axis_index("col")
    where = jnp.stack([col, lax.axis_index("row"), jnp.where(col == 0, pole & 1, pole // 2)]).astype(jnp.int32)
    w0 = root_inverse.shape[2]
    w1, w2 = leaf_node_factor.shape[2:]
    own_rows = root_inverse.shape[1]
    unit = 2 * own_rows
    units = [[(0, 0, j) for j in range(n_row)]] + [list(unit) for unit in zip(*line_plan(n_row))]
    slots = [sorted({e[0] for e in unit}) for unit in units]
    tables = [
        ([e[2] for e in unit], [slot.index(e[0]) for e in unit], [e[1] for e in unit]) for unit, slot in zip(units, slots)
    ]
    owners = [table[0] for table in tables]
    moved, other = {}, {}

    def advance(slot, i):
        down = [(2 * j, 2 * (j - 1)) for j in range(1, n_row - slot + 1)]
        up = [(2 * j + 1, 2 * j + 3) for j in range(slot - 1, n_row - 1)]
        moved[slot, i] = lax.ppermute(moved[slot - 1, i], ("row", "col"), down + up)

    def swap(key):
        other[key] = lax.ppermute(moved[key], "col", SWAP)

    token = pole_weight

    def hold(keys, *rest):
        nonlocal token
        got, over, token, rest = together(
            [moved[key] for key in keys], [other[key] for key in keys if key in other], token, rest
        )
        moved.update(zip(keys, got, strict=True))
        other.update(zip([key for key in keys if key in other], over, strict=True))
        return rest

    def step(value, turn):
        pairs = [(2 * p + c, 2 * (p ^ (1 << (c ^ turn))) + c) for p in range(n_pole) for c in range(2)]
        return lax.ppermute(value, ("pole", "col"), pairs)

    def cut(pair, rows):
        return pair[0][:rows] + pair[1][:rows]

    def unit_of(form, k, which, *rest):
        shards = [held[slot, i] for slot in slots[k] for held in (moved, other) for i in which]
        return unit_call(form, tables[k], where, token, shards, *rest)

    f_own = node_factor[:, 0]
    f_other = lax.ppermute(f_own, "col", SWAP)
    moved[0, 0] = root_inverse
    advance(1, 0)
    swap((0, 0))
    moved[0, 1] = other[0, 0]
    advance(1, 1)
    root = weighted(pole_weight, root_inverse)
    root = jnp.concatenate([root[:, :w1], root[:, w1:]], axis=0)
    roots = (root, step(root, 0))
    factors = prepare(where, leaf_pattern, f_own, f_other, leaf_root_factor[:, 0], leaf_node_factor[:, 0])

    (factors,) = hold([(1, 0)], factors)
    swap((1, 0))
    advance(2, 0)
    rows, *sums = unit_of("first", 0, (0,), factors)
    rows, sums = hold([(1, 1)], rows, sums)
    (roots,) = hold([], roots)
    value = jnp.concatenate([rows, roots[0] + roots[1]], axis=0)
    first = (value, step(value, 1))
    swap((1, 1))
    advance(2, 1)
    hold([(1, 0)])

    hold([(2, 0)])
    swap((2, 0))
    advance(3, 0)
    (first,) = hold([], first)
    hold([(1, 1)])
    rows, *sums = unit_of("next", 1, (0, 1), factors, sums)
    rows, sums = hold([], rows, sums)
    value = jnp.concatenate([rows, cut(first, unit)], axis=0)
    second = (value, step(value, 0))

    hold([(2, 1)])
    swap((2, 1))
    advance(3, 1)
    hold([(2, 0)])

    hold([(3, 0)])
    swap((3, 0))
    (second,) = hold([], second)
    value = cut(second, unit)
    third = (value, step(value, 1))
    hold([(2, 1)])
    rows, *sums = unit_of("next", 2, (0, 1), factors, sums)
    rows, sums = hold([], rows, sums)
    fourth = (rows, step(rows, 0))

    hold([(3, 1)])
    swap((3, 1))
    hold([(3, 0)])
    kept = unit_of("part", 3, (0,), factors)
    (third,) = hold([], third)
    fourth, kept = hold([], fourth, kept)
    value = cut(fourth, unit)
    fifth = (value, step(value, 1))
    hold([(3, 1)])
    ends = (*kept, node_inverse[:, 0], leaf_node_factor[:, 0], leaf_inverse[:, 0])
    keep, send = unit_of("last", 3, (1,), factors, sums, ends)
    got = step(send, 0)
    pieces = [(0, unit, own_rows, None, 0), (0, unit + own_rows, own_rows, None, w1), (1, unit, unit, 0, 0)]
    pieces += [(2, 0, unit, 1, 0), (3, 0, unit, 2, 0)]
    early = [v for pair in (first, second, third, fifth) for v in pair]
    root, off, upper = place(owners, pieces, where, early, unit, w0, w2)
    keep, got, root, off, upper = hold([], keep, got, root, off, upper)
    keep = keep + got
    keep = keep + step(keep, 1)
    got = step(keep, 0)
    off, upper, sep, middle, lower = finish(tables[3][::2], where, keep, got, off, upper, unit, w1, w2)
    return root, off[None], sep[None], upper[None], middle[None], lower[None]


def solution(mesh):
    n_pole, n_row, n_col = (mesh.shape[axis] for axis in ("pole", "row", "col"))

    def shards(root_inverse, node_factor, *rest):
        fits = n_col == 2 and n_row == 4 and n_pole == 4
        form = functools.partial(paired, n_pole, n_row) if fits else general
        return form(root_inverse, node_factor, *rest)

    return jax.shard_map(
        shards,
        mesh=mesh,
        in_specs=(
            P("pole", ("row", "col"), None),
            P("pole", "row", None, "col"),
            P("pole", "row", None, None),
            P("pole", ("row", "col"), None, None),
            P("pole", ("row", "col"), None, None),
            P("pole", ("row", "col"), None, None),
            P(("row", "col"), None),
            P("pole"),
        ),
        out_specs=(
            P(("row", "col"), None),
            P("row", None, "col"),
            P("row", "col", None),
            P(("row", "col"), None, None),
            P(("row", "col"), None, None),
            P(("row", "col"), None, None),
        ),
        check_vma=False,
    )
```

time: 286 us -> 147 us (0.51)
  waiting for transfers between devices: 190 us -> 74.9 us
  matrix products: 52.7 us -> 0 us
  Pallas kernels: 0 us -> 42.4 us
  starting transfers between devices: 0.34 us -> 24.3 us
  local copies, waits for them, and re-layouts: 21 us -> 0.07 us
  between operations: 13.9 us -> 1.1 us
    psum x1 -> x0, waiting for transfers between devices: 103 us -> none  [shards(): lax.psum((upper_levels[0], upper_levels[1], upper_levels[2], leaf_levels[...]
    all_gather x3 -> x0, waiting for transfers between devices: 86.7 us -> none  [the longest x1 77.2 us: shards(): lax.all_gather(root_inverse, ('row', 'col'), axis=1, tiled=True)]
    ppermute x0 -> x23, waiting for transfers between devices: none -> 74.9 us  [the longest x9 57.2 us: step(): return lax.ppermute(value, ('pole', 'col'), pairs)]
    dot_general x7 -> x0, matrix products: 52.7 us -> none  [product(): return jnp.matmul(left, right, precision=highest)]
    pallas_call x0 -> x8, Pallas kernels: none -> 42.4 us  [the longest x6 31.1 us: call(): pl.pallas_call(kernel, in_specs=[SMEM] * smem + [VMEM] * (len(args) - sme...]
    ppermute x0 -> x23, starting transfers between devices: none -> 24.3 us  [the longest x9 13.3 us: step(): return lax.ppermute(value, ('pole', 'col'), pairs)]
    unnamed x30 -> x12, local copies, waits for them, and re-layouts: 18.3 us -> 0.03 us
    mul x1 -> x0, other arithmetic: 3.28 us -> none  [shards(): root_leaf = leaf_root_factor[:, 0] * row_mask[None, :, None]]
  transfers between devices with their start and end apart: 4 -> 23, of which waited for: 3 -> 10; matrix products, arithmetic and copies ran while one was open for 10% -> 3% of each run, Pallas kernels for 0% -> 22%
where the time goes in v2:
time: 147 us
  waiting for transfers between devices  74.9 us (51%)
  Pallas kernels  42.4 us (29%)
  starting transfers between devices  24.3 us (17%)
  other arithmetic  4.37 us (3%)
    ppermute x9, waiting for transfers between devices, step(): return lax.ppermute(value, ('pole', 'col'), pairs)  57.2 us
    pallas_call x6, Pallas kernels, call(): pl.pallas_call(kernel, in_specs=[SMEM] * smem + [VMEM] * (len(args) - sme...  31.1 us
    ppermute x6, waiting for transfers between devices, advance(): moved[slot, i] = lax.ppermute(moved[slot - 1, i], ('row', 'col'), down + up)  13.6 us
    ppermute x9, starting transfers between devices, step(): return lax.ppermute(value, ('pole', 'col'), pairs)  13.3 us
    pallas_call x1, Pallas kernels, prepare(): pl.pallas_call(prepare_kernel, in_specs=[SMEM] * 2 + [VMEM] + [pl.BlockSp...  8.71 us
    ppermute x6, starting transfers between devices, advance(): moved[slot, i] = lax.ppermute(moved[slot - 1, i], ('row', 'col'), down + up)  7.68 us
    ppermute x7, waiting for transfers between devices, swap(): other[key] = lax.ppermute(moved[key], 'col', SWAP)  4.06 us
  transfers between devices with their start and end apart: 23, of which 10 were waited for; matrix products, arithmetic and copies ran while one was open for 3% of the time, Pallas kernels for 22%

profile of v2, /device:TPU:0, one launch (start us, length us, event | category | flops | bytes accessed | tf_op | source)
XLA Modules:
  0.0 147.0 jit_solution(13380782739431640675)
XLA Ops:
  2.5 4.0 %collective-permute-done.refs_1_ = f32[2,128,1024]{2,1,0:T(8,128)S(1)} collective-permute-done((f32[2,128,1024]{2,1,0:T(8,128)}, f32[2,128,1024]{2,1,0:T(8,128)S(1)}, u32[]{:S(2)}, u32[]{:S(2)}) %collective-permute-start) | collective-permute-done | bytes 1048608 | tf_op jit(solution)/shard_map/ppermute | solution.py:412
  7.9 1.4 multiply_reduce_fusion
  10.2 2.6 %collective-permute-start.8 = (f32[256,512]{1,0:T(8,128)}, f32[256,512]{1,0:T(8,128)}, u32[]{:S(2)}, u32[]{:S(2)}) collective-permute-start(f32[256,512]{1,0:T(8,128)} %pad_maximum_fusion.2), channel_id=1, source_target_pairs={{0,8},{1,17},{8,0},{9,25},{16,24},{17,1},{24,16},{25,9},{2,10},{3,... | collective-permute-start | bytes 1572872 | tf_op jit(solution)/shard_map/ppermute | solution.py:427
  12.9 8.7 %prepare.1 = (bf16[2,1024,768]{2,1,0:T(8,128)(2,1)S(1)}, bf16[2,1024,768]{2,1,0:T(8,128)(2,1)S(1)}, bf16[2,1024,256]{2,1,0:T(8,128)(2,1)S(1)}, bf16[2,1024,256]{2,1,0:T(8,128)(2,1)S(1)}) custom-call(s32[3]{0:T(128)S(1)} %pad_add_fusion.where, s32[1,8]{1,0:T(1,128)S(1)} %copy-done.5, f32[2,1024,256]{2,1,0:T(8,128)} %collective-permute-done.3.f_other, ...), custom_call_target="tpu_custom_call" | custom-call | flops 1 | bytes 1 | tf_op jit(solution)/shard_map/prepare/pallas_call | solution.py:151
  21.6 2.2 %collective-permute-start.7 = (f32[2,128,1024]{2,1,0:T(8,128)S(1)}, f32[2,128,1024]{2,1,0:T(8,128)S(1)}, u32[]{:S(2)}, u32[]{:S(2)}) collective-permute-start(f32[2,128,1024]{2,1,0:T(8,128)S(1)} %collective-permute-done.2.refs_0_), channel_id=1, source_target_pairs={{0,1},{1,0},{2,3},{3,2},{4,5},{5,4},{6,7},{7,6},{8,9},{9,8},{10,11... | collective-permute-start | bytes 3145736 | tf_op jit(solution)/shard_map/ppermute | solution.py:412
  25.1 6.0 %first.1 = (f32[256,512]{1,0:T(8,128)S(1)}, f32[2,768,512]{2,1,0:T(8,128)S(1)}, f32[2,256,256]{2,1,0:T(8,128)S(1)}) custom-call(s32[3]{0:T(128)S(1)} %pad_add_fusion.where, f32[2]{0:T(128)S(1)} %copy-done.4, f32[2,128,1024]{2,1,0:T(8,128)S(1)} %copy-done, f32[2,128,1024]{2,1,0:T(8,128)S(1)} %collective-permute-done.refs_1_, ...), custom_call_target="tpu_custom_call" | custom-call | flops 1 | bytes 1 | tf_op jit(solution)/shard_map/first/pallas_call | solution.py:70
  32.5 1.3 collective-permute-start.9
  35.0 6.5 %collective-permute-done.6.refs_4_.refs_0_ = f32[2,128,1024]{2,1,0:T(8,128)S(1)} collective-permute-done((f32[2,128,1024]{2,1,0:T(8,128)S(1)}, f32[2,128,1024]{2,1,0:T(8,128)S(1)}, u32[]{:S(2)}, u32[]{:S(2)}) %collective-permute-start.6) | collective-permute-done | bytes 1048608 | tf_op jit(solution)/shard_map/ppermute | solution.py:409
  42.9 4.4 %collective-permute-done.9.refs_1_ = f32[512,512]{1,0:T(8,128)S(1)} collective-permute-done((f32[512,512]{1,0:T(8,128)S(1)}, f32[512,512]{1,0:T(8,128)S(1)}, u32[]{:S(2)}, u32[]{:S(2)}) %collective-permute-start.9) | collective-permute-done | bytes 1048608 | tf_op jit(solution)/shard_map/ppermute | solution.py:427
  47.3 6.7 %next.2 = (f32[256,512]{1,0:T(8,128)S(1)}, f32[2,768,512]{2,1,0:T(8,128)S(1)}, f32[2,256,256]{2,1,0:T(8,128)S(1)}) custom-call(s32[3]{0:T(128)S(1)} %pad_add_fusion.where, f32[2]{0:T(128)S(1)} %copy-done.4, f32[2,128,1024]{2,1,0:T(8,128)S(1)} %collective-permute-done.2.refs_0_, ...), custom_call_target="tpu_custom_call", output_to_operand_aliasing={{1}: (10, {}), {2}: (11, {})} | custom-call | flops 1 | bytes 1 | tf_op jit(solution)/shard_map/next/pallas_call | solution.py:70
  54.2 1.6 %collective-permute-start.14 = (f32[512,512]{1,0:T(8,128)S(1)}, f32[512,512]{1,0:T(8,128)S(1)}, u32[]{:S(2)}, u32[]{:S(2)}) collective-permute-start(f32[512,512]{1,0:T(8,128)S(1)} %pad_maximum_fusion.1.refs_2_), channel_id=1, source_target_pairs={{0,8},{1,17},{8,0},{9,25},{16,24},{17,1},{24,16},{25,9},{2,10},{3,... | collective-permute-start | bytes 3145736 | tf_op jit(solution)/shard_map/ppermute | solution.py:427
  57.0 7.0 %collective-permute-done.12.refs_2_ = f32[2,128,1024]{2,1,0:T(8,128)S(1)} collective-permute-done((f32[2,128,1024]{2,1,0:T(8,128)S(1)}, f32[2,128,1024]{2,1,0:T(8,128)S(1)}, u32[]{:S(2)}, u32[]{:S(2)}) %collective-permute-start.12) | collective-permute-done | bytes 1048608 | tf_op jit(solution)/shard_map/ppermute | solution.py:409
  64.1 5.0 %collective-permute-done.14.refs_3_ = f32[512,512]{1,0:T(8,128)S(1)} collective-permute-done((f32[512,512]{1,0:T(8,128)S(1)}, f32[512,512]{1,0:T(8,128)S(1)}, u32[]{:S(2)}, u32[]{:S(2)}) %collective-permute-start.14) | collective-permute-done | bytes 1048608 | tf_op jit(solution)/shard_map/ppermute | solution.py:427
  69.0 6.5 %next.3 = (f32[256,512]{1,0:T(8,128)S(1)}, f32[2,768,512]{2,1,0:T(8,128)S(1)}, f32[2,256,256]{2,1,0:T(8,128)S(1)}) custom-call(s32[3]{0:T(128)S(1)} %pad_add_fusion.where, f32[2]{0:T(128)S(1)} %copy-done.4, f32[2,128,1024]{2,1,0:T(8,128)S(1)} %collective-permute-done.2.refs_0_, ...), custom_call_target="tpu_custom_call", output_to_operand_aliasing={{1}: (14, {}), {2}: (15, {})} | custom-call | flops 1 | bytes 1 | tf_op jit(solution)/shard_map/next/pallas_call | solution.py:70
  77.5 1.5 %collective-permute-start.18 = (f32[256,512]{1,0:T(8,128)S(1)}, f32[256,512]{1,0:T(8,128)S(1)}, u32[]{:S(2)}, u32[]{:S(2)}) collective-permute-start(f32[256,512]{1,0:T(8,128)S(1)} %get-tuple-element.179), channel_id=1, source_target_pairs={{0,8},{1,17},{8,0},{9,25},{16,24},{17,1},{24,16},{25,9},{2,10},{3,... | collective-permute-start | bytes 1572872 | tf_op jit(solution)/shard_map/ppermute | solution.py:427
  79.0 2.5 %part.1 = (f32[128,512]{1,0:T(8,128)S(1)}, bf16[2,128,768]{2,1,0:T(8,128)(2,1)S(1)}, bf16[2,128,768]{2,1,0:T(8,128)(2,1)S(1)}) custom-call(s32[3]{0:T(128)S(1)} %pad_add_fusion.where, f32[2]{0:T(128)S(1)} %copy-done.4, f32[2,128,1024]{2,1,0:T(8,128)S(1)} %collective-permute-done.6.refs_4_.refs_0_, ...), custom_call_target="tpu_custom_call" | custom-call | flops 1 | bytes 1 | tf_op jit(solution)/shard_map/part/pallas_call | solution.py:70
  81.6 9.2 %collective-permute-done.17.refs_5_ = f32[256,512]{1,0:T(8,128)S(1)} collective-permute-done((f32[256,512]{1,0:T(8,128)S(1)}, f32[256,512]{1,0:T(8,128)S(1)}, u32[]{:S(2)}, u32[]{:S(2)}) %collective-permute-start.17) | collective-permute-done | bytes 524320 | tf_op jit(solution)/shard_map/ppermute | solution.py:427
  90.9 7.1 %last.1 = (f32[448,512]{1,0:T(8,128)S(1)}, f32[448,512]{1,0:T(8,128)S(1)}) custom-call(s32[3]{0:T(128)S(1)} %pad_add_fusion.where, f32[2]{0:T(128)S(1)} %copy-done.4, f32[2,128,1024]{2,1,0:T(8,128)S(1)} %collective-permute-done.4.refs_5_.refs_0_, f32[2,128,1024]{2,1,0:T(8,128)S(1)} %collective-permute-done.11.refs_7_.refs_1_, ...), custom_call_target="tpu_custom_call" | custom-call | flops 1 | bytes 1 | tf_op jit(solution)/shard_map/last/pallas_call | solution.py:70
  99.2 1.7 %collective-permute-start.20 = (f32[256,512]{1,0:T(8,128)S(1)}, f32[256,512]{1,0:T(8,128)S(1)}, u32[]{:S(2)}, u32[]{:S(2)}) collective-permute-start(f32[256,512]{1,0:T(8,128)S(1)} %add.22.refs_6_), channel_id=1, source_target_pairs={{0,16},{1,9},{8,24},{9,1},{16,0},{17,25},{24,8},{25,17},{2,18},{3,... | collective-permute-start | bytes 1572872 | tf_op jit(solution)/shard_map/ppermute | solution.py:427
  100.9 13.2 %collective-permute-done.20.refs_7_ = f32[256,512]{1,0:T(8,128)S(1)} collective-permute-done((f32[256,512]{1,0:T(8,128)S(1)}, f32[256,512]{1,0:T(8,128)S(1)}, u32[]{:S(2)}, u32[]{:S(2)}) %collective-permute-start.20) | collective-permute-done | bytes 524320 | tf_op jit(solution)/shard_map/ppermute | solution.py:427
  114.1 2.3 %place.1 = (f32[128,1024]{1,0:T(8,128)}, f32[1024,256]{1,0:T(8,128)}, f32[1024,256]{1,0:T(8,128)}) custom-call(s32[3]{0:T(128)S(1)} %pad_add_fusion.where, f32[512,512]{1,0:T(8,128)S(1)} %pad_maximum_fusion.refs_0_, f32[512,512]{1,0:T(8,128)S(1)} %collective-permute-done.9.refs_1_, f32[512,512]{1,0:T(8,128)S(1)} %pad_maximum_fusion.1.refs_2_, ...), custom_call_target="tpu_custom_call" | custom-call | flops 1 | bytes 1 | tf_op jit(solution)/shard_map/place/pallas_call | solution.py:70
  118.3 12.4 %collective-permute-done.21 = f32[448,512]{1,0:T(8,128)S(1)} collective-permute-done((f32[448,512]{1,0:T(8,128)S(1)}, f32[448,512]{1,0:T(8,128)S(1)}, u32[]{:S(2)}, u32[]{:S(2)}) %collective-permute-start.21) | collective-permute-done | bytes 917536 | tf_op jit(solution)/shard_map/ppermute | solution.py:427
  132.0 12.3 %collective-permute-done.22.got = f32[448,512]{1,0:T(8,128)S(1)} collective-permute-done((f32[448,512]{1,0:T(8,128)S(1)}, f32[448,512]{1,0:T(8,128)S(1)}, u32[]{:S(2)}, u32[]{:S(2)}) %collective-permute-start.22) | collective-permute-done | bytes 917536 | tf_op jit(solution)/shard_map/ppermute | solution.py:427
  144.3 2.5 %finish.1 = (f32[1024,256]{1,0:T(8,128)}, f32[1024,256]{1,0:T(8,128)}, f32[256,512]{1,0:T(8,128)}, f32[512,256]{1,0:T(8,128)}, f32[256,256]{1,0:T(8,128)}) custom-call(s32[3]{0:T(128)S(1)} %pad_add_fusion.where, f32[448,512]{1,0:T(8,128)S(1)} %add.24.kept, f32[448,512]{1,0:T(8,128)S(1)} %collective-permute-done.22.got, ...), custom_call_target="tpu_custom_call", output_to_operand_aliasing={{0}: (3, {}), {1}: (4, {})} | custom-call | flops 1 | bytes 1 | tf_op jit(solution)/shard_map/finish/pallas_call | solution.py:349
  (54 shorter events, 17.2 us)
Async XLA Ops:
  0.6 12.2 %collective-permute-start.3 = (f32[2,1024,256]{2,1,0:T(8,128)}, f32[2,1024,256]{2,1,0:T(8,128)}, u32[]{:S(2)}, u32[]{:S(2)}) collective-permute-start(f32[2,1024,256]{2,1,0:T(8,128)} %bitcast.17), channel_id=1, source_target_pairs={{0,1},{1,0},{2,3},{3,2},{4,5},{5,4},{6,7},{7,6},{8,9},{9,8},{10,11... | collective-permute-start | bytes 6291464 | tf_op jit(solution)/shard_map/ppermute | solution.py:437
  1.2 5.4 %collective-permute-start = (f32[2,128,1024]{2,1,0:T(8,128)}, f32[2,128,1024]{2,1,0:T(8,128)S(1)}, u32[]{:S(2)}, u32[]{:S(2)}) collective-permute-start(f32[2,128,1024]{2,1,0:T(8,128)} %refs_0_.1), channel_id=1, source_target_pairs={{0,1},{1,0},{2,3},{3,2},{4,5},{5,4},{6,7},{7,6},{8,9},{9,8},{10,11... | collective-permute-start | bytes 3145736 | tf_op jit(solution)/shard_map/ppermute | solution.py:412
  1.2 20.3 %collective-permute-start.2 = (f32[2,128,1024]{2,1,0:T(8,128)}, f32[2,128,1024]{2,1,0:T(8,128)S(1)}, u32[]{:S(2)}, u32[]{:S(2)}) collective-permute-start(f32[2,128,1024]{2,1,0:T(8,128)} %refs_0_.1), channel_id=1, source_target_pairs={{2,0},{4,2},{6,4},{1,3},{3,5},{5,7},{10,8},{12,10},{14,12},{9,11},... | collective-permute-start | bytes 3145736 | tf_op jit(solution)/shard_map/ppermute | solution.py:409
  6.6 24.5 %collective-permute-start.1 = (f32[2,128,1024]{2,1,0:T(8,128)S(1)}, f32[2,128,1024]{2,1,0:T(8,128)S(1)}, u32[]{:S(2)}, u32[]{:S(2)}) collective-permute-start(f32[2,128,1024]{2,1,0:T(8,128)S(1)} %collective-permute-done.refs_1_), channel_id=1, source_target_pairs={{2,0},{4,2},{6,4},{1,3},{3,5},{5,7},{10,8},{12,10},{14,12},{9,11},... | collective-permute-start | bytes 3145736 | tf_op jit(solution)/shard_map/ppermute | solution.py:409
  10.2 20.9 %collective-permute-start.8 = (f32[256,512]{1,0:T(8,128)}, f32[256,512]{1,0:T(8,128)}, u32[]{:S(2)}, u32[]{:S(2)}) collective-permute-start(f32[256,512]{1,0:T(8,128)} %pad_maximum_fusion.2), channel_id=1, source_target_pairs={{0,8},{1,17},{8,0},{9,25},{16,24},{17,1},{24,16},{25,9},{2,10},{3,... | collective-permute-start | bytes 1572872 | tf_op jit(solution)/shard_map/ppermute | solution.py:427
  21.6 13.4 %collective-permute-start.7 = (f32[2,128,1024]{2,1,0:T(8,128)S(1)}, f32[2,128,1024]{2,1,0:T(8,128)S(1)}, u32[]{:S(2)}, u32[]{:S(2)}) collective-permute-start(f32[2,128,1024]{2,1,0:T(8,128)S(1)} %collective-permute-done.2.refs_0_), channel_id=1, source_target_pairs={{0,1},{1,0},{2,3},{3,2},{4,5},{5,4},{6,7},{7,6},{8,9},{9,8},{10,11... | collective-permute-start | bytes 3145736 | tf_op jit(solution)/shard_map/ppermute | solution.py:412
  23.8 17.8 %collective-permute-start.6 = (f32[2,128,1024]{2,1,0:T(8,128)S(1)}, f32[2,128,1024]{2,1,0:T(8,128)S(1)}, u32[]{:S(2)}, u32[]{:S(2)}) collective-permute-start(f32[2,128,1024]{2,1,0:T(8,128)S(1)} %collective-permute-done.2.refs_0_), channel_id=1, source_target_pairs={{2,0},{4,2},{3,5},{5,7},{10,8},{12,10},{11,13},{13,15},{18,16},{20... | collective-permute-start | bytes 3145736 | tf_op jit(solution)/shard_map/ppermute | solution.py:409
  32.5 14.9 %collective-permute-start.9 = (f32[512,512]{1,0:T(8,128)S(1)}, f32[512,512]{1,0:T(8,128)S(1)}, u32[]{:S(2)}, u32[]{:S(2)}) collective-permute-start(f32[512,512]{1,0:T(8,128)S(1)} %pad_maximum_fusion.refs_0_), channel_id=1, source_target_pairs={{0,16},{1,9},{8,24},{9,1},{16,0},{17,25},{24,8},{25,17},{2,18},{3,... | collective-permute-start | bytes 3145736 | tf_op jit(solution)/shard_map/ppermute | solution.py:427
  33.7 13.6 %collective-permute-start.5 = (f32[2,128,1024]{2,1,0:T(8,128)S(1)}, f32[2,128,1024]{2,1,0:T(8,128)S(1)}, u32[]{:S(2)}, u32[]{:S(2)}) collective-permute-start(f32[2,128,1024]{2,1,0:T(8,128)S(1)} %collective-permute-done.1.refs_1_), channel_id=1, source_target_pairs={{0,1},{1,0},{2,3},{3,2},{4,5},{5,4},{6,7},{7,6},{8,9},{9,8},{10,11... | collective-permute-start | bytes 3145736 | tf_op jit(solution)/shard_map/ppermute | solution.py:412
  33.7 22.0 %collective-permute-start.4 = (f32[2,128,1024]{2,1,0:T(8,128)S(1)}, f32[2,128,1024]{2,1,0:T(8,128)S(1)}, u32[]{:S(2)}, u32[]{:S(2)}) collective-permute-start(f32[2,128,1024]{2,1,0:T(8,128)S(1)} %collective-permute-done.1.refs_1_), channel_id=1, source_target_pairs={{2,0},{4,2},{3,5},{5,7},{10,8},{12,10},{11,13},{13,15},{18,16},{20... | collective-permute-start | bytes 3145736 | tf_op jit(solution)/shard_map/ppermute | solution.py:409
  41.6 15.4 %collective-permute-start.13 = (f32[2,128,1024]{2,1,0:T(8,128)S(1)}, f32[2,128,1024]{2,1,0:T(8,128)S(1)}, u32[]{:S(2)}, u32[]{:S(2)}) collective-permute-start(f32[2,128,1024]{2,1,0:T(8,128)S(1)} %collective-permute-done.6.refs_4_.refs_0_), channel_id=1, source_target_pairs={{0,1},{1,0},{2,3},{3,2},{4,5},{5,4},{6,7},{7,6},{8,9},{9,8},{10,11... | collective-permute-start | bytes 3145736 | tf_op jit(solution)/shard_map/ppermute | solution.py:412
  41.6 22.5 %collective-permute-start.12 = (f32[2,128,1024]{2,1,0:T(8,128)S(1)}, f32[2,128,1024]{2,1,0:T(8,128)S(1)}, u32[]{:S(2)}, u32[]{:S(2)}) collective-permute-start(f32[2,128,1024]{2,1,0:T(8,128)S(1)} %collective-permute-done.6.refs_4_.refs_0_), channel_id=1, source_target_pairs={{2,0},{5,7},{10,8},{13,15},{18,16},{21,23},{26,24},{29,31}} | collective-permute-start | bytes 3145736 | tf_op jit(solution)/shard_map/ppermute | solution.py:409
  54.2 14.9 %collective-permute-start.14 = (f32[512,512]{1,0:T(8,128)S(1)}, f32[512,512]{1,0:T(8,128)S(1)}, u32[]{:S(2)}, u32[]{:S(2)}) collective-permute-start(f32[512,512]{1,0:T(8,128)S(1)} %pad_maximum_fusion.1.refs_2_), channel_id=1, source_target_pairs={{0,8},{1,17},{8,0},{9,25},{16,24},{17,1},{24,16},{25,9},{2,10},{3,... | collective-permute-start | bytes 3145736 | tf_op jit(solution)/shard_map/ppermute | solution.py:427
  55.7 13.3 %collective-permute-start.11 = (f32[2,128,1024]{2,1,0:T(8,128)S(1)}, f32[2,128,1024]{2,1,0:T(8,128)S(1)}, u32[]{:S(2)}, u32[]{:S(2)}) collective-permute-start(f32[2,128,1024]{2,1,0:T(8,128)S(1)} %collective-permute-done.4.refs_5_.refs_0_), channel_id=1, source_target_pairs={{0,1},{1,0},{2,3},{3,2},{4,5},{5,4},{6,7},{7,6},{8,9},{9,8},{10,11... | collective-permute-start | bytes 3145736 | tf_op jit(solution)/shard_map/ppermute | solution.py:412
  55.7 19.8 %collective-permute-start.10 = (f32[2,128,1024]{2,1,0:T(8,128)S(1)}, f32[2,128,1024]{2,1,0:T(8,128)S(1)}, u32[]{:S(2)}, u32[]{:S(2)}) collective-permute-start(f32[2,128,1024]{2,1,0:T(8,128)S(1)} %collective-permute-done.4.refs_5_.refs_0_), channel_id=1, source_target_pairs={{2,0},{5,7},{10,8},{13,15},{18,16},{21,23},{26,24},{29,31}} | collective-permute-start | bytes 3145736 | tf_op jit(solution)/shard_map/ppermute | solution.py:409
  69.0 10.0 %collective-permute-start.16 = (f32[2,128,1024]{2,1,0:T(8,128)S(1)}, f32[2,128,1024]{2,1,0:T(8,128)S(1)}, u32[]{:S(2)}, u32[]{:S(2)}) collective-permute-start(f32[2,128,1024]{2,1,0:T(8,128)S(1)} %collective-permute-done.12.refs_2_), channel_id=1, source_target_pairs={{0,1},{1,0},{2,3},{3,2},{4,5},{5,4},{6,7},{7,6},{8,9},{9,8},{10,11... | collective-permute-start | bytes 3145736 | tf_op jit(solution)/shard_map/ppermute | solution.py:412
  75.6 15.3 %collective-permute-start.15 = (f32[2,128,1024]{2,1,0:T(8,128)S(1)}, f32[2,128,1024]{2,1,0:T(8,128)S(1)}, u32[]{:S(2)}, u32[]{:S(2)}) collective-permute-start(f32[2,128,1024]{2,1,0:T(8,128)S(1)} %collective-permute-done.10.refs_2_), channel_id=1, source_target_pairs={{0,1},{1,0},{2,3},{3,2},{4,5},{5,4},{6,7},{7,6},{8,9},{9,8},{10,11... | collective-permute-start | bytes 3145736 | tf_op jit(solution)/shard_map/ppermute | solution.py:412
  76.2 14.6 %copy-start.1 = (f32[2,1,512,256]{3,2,1,0:T(8,128)S(1)}, f32[2,1,512,256]{3,2,1,0:T(8,128)}, u32[]{:S(2)}) copy-start(f32[2,1,512,256]{3,2,1,0:T(8,128)} %param.12) | copy-start | bytes 3145732
  76.2 14.6 %collective-permute-start.17 = (f32[256,512]{1,0:T(8,128)S(1)}, f32[256,512]{1,0:T(8,128)S(1)}, u32[]{:S(2)}, u32[]{:S(2)}) collective-permute-start(f32[256,512]{1,0:T(8,128)S(1)} %slice_add_fusion.refs_4_), channel_id=1, source_target_pairs={{0,16},{1,9},{8,24},{9,1},{16,0},{17,25},{24,8},{25,17},{2,18},{3,... | collective-permute-start | bytes 1572872 | tf_op jit(solution)/shard_map/ppermute | solution.py:427
  77.5 13.3 %collective-permute-start.18 = (f32[256,512]{1,0:T(8,128)S(1)}, f32[256,512]{1,0:T(8,128)S(1)}, u32[]{:S(2)}, u32[]{:S(2)}) collective-permute-start(f32[256,512]{1,0:T(8,128)S(1)} %get-tuple-element.179), channel_id=1, source_target_pairs={{0,8},{1,17},{8,0},{9,25},{16,24},{17,1},{24,16},{25,9},{2,10},{3,... | collective-permute-start | bytes 1572872 | tf_op jit(solution)/shard_map/ppermute | solution.py:427
  98.0 19.1 %collective-permute-start.19 = (f32[448,512]{1,0:T(8,128)S(1)}, f32[448,512]{1,0:T(8,128)S(1)}, u32[]{:S(2)}, u32[]{:S(2)}) collective-permute-start(f32[448,512]{1,0:T(8,128)S(1)} %get-tuple-element.176), channel_id=1, source_target_pairs={{0,8},{1,17},{8,0},{9,25},{16,24},{17,1},{24,16},{25,9},{2,10},{3,... | collective-permute-start | bytes 2752520 | tf_op jit(solution)/shard_map/ppermute | solution.py:427
  99.2 14.9 %collective-permute-start.20 = (f32[256,512]{1,0:T(8,128)S(1)}, f32[256,512]{1,0:T(8,128)S(1)}, u32[]{:S(2)}, u32[]{:S(2)}) collective-permute-start(f32[256,512]{1,0:T(8,128)S(1)} %add.22.refs_6_), channel_id=1, source_target_pairs={{0,16},{1,9},{8,24},{9,1},{16,0},{17,25},{24,8},{25,17},{2,18},{3,... | collective-permute-start | bytes 1572872 | tf_op jit(solution)/shard_map/ppermute | solution.py:427
  117.2 13.5 %collective-permute-start.21 = (f32[448,512]{1,0:T(8,128)S(1)}, f32[448,512]{1,0:T(8,128)S(1)}, u32[]{:S(2)}, u32[]{:S(2)}) collective-permute-start(f32[448,512]{1,0:T(8,128)S(1)} %add.23), channel_id=1, source_target_pairs={{0,16},{1,9},{8,24},{9,1},{16,0},{17,25},{24,8},{25,17},{2,18},{3,... | collective-permute-start | bytes 2752520 | tf_op jit(solution)/shard_map/ppermute | solution.py:427
  130.9 13.5 %collective-permute-start.22 = (f32[448,512]{1,0:T(8,128)S(1)}, f32[448,512]{1,0:T(8,128)S(1)}, u32[]{:S(2)}, u32[]{:S(2)}) collective-permute-start(f32[448,512]{1,0:T(8,128)S(1)} %add.24.kept), channel_id=1, source_target_pairs={{0,8},{1,17},{8,0},{9,25},{16,24},{17,1},{24,16},{25,9},{2,10},{3,... | collective-permute-start | bytes 2752520 | tf_op jit(solution)/shard_map/ppermute | solution.py:427
  (5 other events, 65.9 us)

commit v3 on v2

--- a/solution.py
+++ b/solution.py
@@ -88,7 +88,10 @@
     def one(a, b):
         return lax.dot_general(a, b, (dims, ((), ())), preferred_element_type=jnp.float32)
 
-    return one(left[0], right[0]) + (one(left[0], right[1]) + one(left[1], right[0]))
+    k = dims[0][0]
+    return one(
+        jnp.concatenate([left[0], left[0], left[1]], axis=k), jnp.concatenate([right[0], right[1], right[0]], axis=0)
+    )
 
 
 def pick(table, row):
@@ -166,21 +169,24 @@
     )(where, pattern, f_other, *hbm)
 
 
-def unit_kernel(form, slots, owners, slot_of, ways, where, weight, *refs):
-    count = {"first": 1, "next": 2, "part": 1, "last": 1}[form]
-    shards, refs = refs[: 2 * slots * count], refs[2 * slots * count :]
+def unit_kernel(form, slots, cuts, owners, slot_of, ways, where, weight, *refs):
+    count = {"first": 1, "next": 2, "halves": 2, "part": 1, "last": 1}[form]
+    shards = []
+    for n in cuts:
+        shards.append(refs[:n])
+        refs = refs[n:]
     (w_high, w_low, l_high, l_low), refs = refs[:4], refs[4:]
-    if form in ("next", "last"):
+    if form in ("next", "halves", "last"):
         (gram_in, square_in), refs = refs[:2], refs[2:]
     if form == "last":
-        (kept_rows, kept_high, kept_low, inv_n, leaf_n, inv_l), refs = refs[:6], refs[6:]
+        (kept_rows, kept_high, kept_low, inv_n), refs = refs[:4], refs[4:]
     if form == "last":
-        outs, (r_high, r_low, sent_at, rest_at) = refs[:-4], refs[-4:]
+        outs, (r_high, r_low, sent_at, sep_at) = refs[:-4], refs[-4:]
     else:
         outs, (r_high, r_low) = refs[:-2], refs[-2:]
     col, row = where[0], where[1]
     owner, slot, way = (pick(table, row) for table in (owners, slot_of, ways))
-    poles, rows, _ = shards[0].shape
+    poles, rows, _ = shards[0][0].shape
     w2 = l_high.shape[2]
     w1 = w_high.shape[2] - w2
     width = w1 // 2
@@ -189,18 +195,19 @@
         for i in range(2):
             at = pl.ds(pl.multiple_of(jnp.where(col == i, 0, rows), rows), rows)
             for p in range(poles):
-                r_high[p, at], r_low[p, at] = split(shards[i][p])
+                r_high[p, at], r_low[p, at] = split(shards[i][0][p])
     else:
         for i in range(count):
             at = pl.ds(begin[i] if count == 2 else 0, rows)
             for s in range(slots):
                 for j in range(2):
-                    ref = shards[(2 * s + j) * count + i]
+                    pieces = shards[(2 * s + j) * count + i]
 
                     @pl.when((slot == s) & ((way == col) == (j == 0)))
                     def _():
                         for p in range(poles):
-                            r_high[p, at], r_low[p, at] = split(ref[p])
+                            piece = pieces[p * len(pieces) // poles]
+                            r_high[p, at], r_low[p, at] = split(piece[p % piece.shape[0]])
 
     span = r_high.shape[1]
     base = owner * 2 * rows
@@ -214,7 +221,12 @@
         mine = jnp.where(col == 0, x[:, :width], x[:, width:w1])
         sent = -scale * jnp.concatenate([mine, x[:, w1:]], axis=1)
         sent_ref = sent_at if form == "last" else outs[0]
-        if p == 0:
+        if form == "halves":
+            if p == 0:
+                total = sent
+            else:
+                total = total + sent
+        elif p == 0:
             sent_ref[...] = sent
         else:
             sent_ref[...] += sent
@@ -235,58 +247,105 @@
             cross = cross + gram_in[p, :w1]
             below = below + gram_in[p, w1:]
             inner = inner + square_in[p]
-        if form != "last":
-            gram, square = outs[-2:]
-            gram[p, :w1] = cross
-            gram[p, w1:] = below
-            square[p] = inner
-            continue
-        sep = inv_n[p] + cross
-        ns = split(leaf_n[p])
-        middle = below.T - dot3(split(sep), ns)
-        lower = inv_l[p] + inner - dot3(ns, split(middle), ACROSS)
-        sep = scale * jnp.where(col == 0, sep[:width], sep[width:])
-        middle = scale * jnp.concatenate([middle[:width], middle[width:]], axis=1)
-        lower = scale * jnp.concatenate([lower[: w2 // 2], lower[w2 // 2 :]], axis=1)
-        value = jnp.concatenate([sep, middle, lower], axis=0)
-        if p == 0:
-            rest_at[...] = value
-        else:
-            rest_at[...] += value
-    if form == "last":
-        keep, send = outs
-        head = keep.shape[0] - 2 * rows
-        for i, halves in enumerate([(keep, send), (send, keep)]):
+        gram, square = outs[-2:]
+        gram[p, :w1] = cross
+        gram[p, w1:] = below
+        square[p] = inner
+        if form == "last":
+            sep = inv_n[p] + cross
+            sep = scale * jnp.where(col == 0, sep[:width], sep[width:])
+            if p == 0:
+                sep_at[...] = sep
+            else:
+                sep_at[...] += sep
+    if form == "halves":
+        for i in range(2):
 
             @pl.when(where[2] == i)
             def _():
-                halves[0][:rows] = kept_rows[...]
-                halves[0][rows : 2 * rows] = sent_at[...]
-                halves[0][2 * rows :] = rest_at[:head]
-                halves[1][...] = rest_at[head:]
+                outs[i][...] = total[:rows]
+                outs[1 - i][...] = total[rows:]
+
+    if form == "last":
+        half = outs[0].shape[0]
+        split_at = half - rows
+        for i in range(2):
+
+            @pl.when(where[2] == i)
+            def _():
+                outs[i][:rows] = kept_rows[...]
+                outs[i][rows:] = sent_at[:split_at]
+                outs[1 - i][: rows - split_at] = sent_at[split_at:]
+                outs[1 - i][rows - split_at :] = sep_at[: half + split_at - rows]
+
+        outs[2][...] = sep_at[half + split_at - rows :]
+
+
+def ends_kernel(where, weight, gram, square, sep, inv_n, leaf_n, inv_l, keep, send, rest_at):
+    poles, w1, w2 = leaf_n.shape
+    width = w1 // 2
+    start = sep.shape[0]
+    rest_at[:start] = sep[...]
+    for p in range(poles):
+        ns = split(leaf_n[p])
+        middle = gram[p, w1:].T - dot3(split(inv_n[p] + gram[p, :w1]), ns)
+        lower = inv_l[p] + square[p] - dot3(ns, split(middle), ACROSS)
+        middle = jnp.concatenate([middle[:width], middle[width:]], axis=1)
+        lower = jnp.concatenate([lower[: w2 // 2], lower[w2 // 2 :]], axis=1)
+        value = weight[p] * jnp.concatenate([middle, lower], axis=0)
+        if p == 0:
+            rest_at[start:] = value
+        else:
+            rest_at[start:] += value
+    head = keep.shape[0]
+    for i, (a, b) in enumerate([(keep, send), (send, keep)]):
+
+        @pl.when(where[2] == i)
+        def _():
+            a[...] = rest_at[:head]
+            b[...] = rest_at[head:]
+
+
+def ends_call(where, weight, gram, square, sep, inv_n, leaf_n, inv_l):
+    w1, w2 = leaf_n.shape[1:]
+    rows = sep.shape[0] + (w1 + w2) // 2
+    outs = [pltpu.VMEM((rows // 2, w1), jnp.float32)] * 2
+    args = [where, weight, gram, square, sep, inv_n, leaf_n, inv_l]
+    return call(ends_kernel, "ends", outs, args, 2, scratch_shapes=[pltpu.VMEM((rows, w1), jnp.float32)])
+
+
+def halved(rows, w1, w2):
+    quarter = (2 * rows + w1 + w2 // 2) // 4
+    return (quarter + 0, quarter - 0), (112, rows - 112)
 
 
 def unit_call(form, tables, where, weight, shards, factors, sums=(), ends=()):
-    poles, rows, w0 = shards[0].shape
+    poles, rows, w0 = shards[0][0].shape
     lanes, w2 = factors[0].shape[2], factors[2].shape[2]
     w1 = lanes - w2
     f32 = jnp.float32
+    head = halved(rows, w1, w2)[0][0]
     gram = [pltpu.VMEM((poles, lanes, w1), f32), pltpu.VMEM((poles, w2, w2), f32)]
     outs = {
         "first": [pltpu.VMEM((2 * rows, w1), f32)] + gram,
         "next": [pltpu.VMEM((2 * rows, w1), f32)] + gram,
+        "halves": [pltpu.VMEM((rows, w1), f32)] * 2 + gram,
         "part": [pltpu.VMEM((rows, w1), f32)] + [pltpu.VMEM((poles, rows, lanes), jnp.bfloat16)] * 2,
-        "last": [pltpu.VMEM(((2 * rows + w1 // 2 + w1 // 2 + w2 // 2) // 2, w1), f32)] * 2,
+        "last": [pltpu.VMEM((n, w1), f32) for n in (head, head, 2 * rows + w1 // 2 - 2 * head)] + gram,
     }[form]
-    args = [where, weight, *shards, *factors, *sums, *ends]
-    slots = len(shards) // (4 if form == "next" else 2)
-    span = rows * (2 if form in ("first", "next") else 1)
+    cuts = [len(pieces) for pieces in shards]
+    args = [where, weight, *(x for pieces in shards for x in pieces), *factors, *sums, *ends]
+    slots = len(shards) // (4 if form in ("next", "halves") else 2)
+    span = rows * (1 if form in ("part", "last") else 2)
     options = {"scratch_shapes": [pltpu.VMEM((poles, span, w0), jnp.bfloat16)] * 2}
     if form == "last":
-        options["scratch_shapes"] += [pltpu.VMEM((rows, w1), f32), pltpu.VMEM((w1 + w2 // 2, w1), f32)]
-    if form == "next":
-        options["input_output_aliases"] = {len(args) - 2: 1, len(args) - 1: 2}
-    return list(call(functools.partial(unit_kernel, form, slots, *tables), form, outs, args, 2, **options))
+        options["scratch_shapes"] += [pltpu.VMEM((rows, w1), f32), pltpu.VMEM((w1 // 2, w1), f32)]
+        at = len(args) - len(ends) - 2
+        options["input_output_aliases"] = {at: 3, at + 1: 4}
+    if form in ("next", "halves"):
+        at = 2 if form == "halves" else 1
+        options["input_output_aliases"] = {len(args) - 2: at, len(args) - 1: at + 1}
+    return list(call(functools.partial(unit_kernel, form, slots, cuts, *tables), form, outs, args, 2, **options))
 
 
 def place_kernel(unit, owners, pieces, where, *refs):
@@ -309,58 +368,83 @@
     return call(functools.partial(place_kernel, unit, owners, pieces), "place", outs, [where, *sums], 1)
 
 
-def finish_kernel(unit, owners, ways, where, kept, got, _off, _upper, off, upper, sep, middle, lower, *scratch):
-    off_part, upper_part, sem = scratch
-    rows = unit // 2
+def finish_kernel(unit, halves, shares, part, table, owners, where, *refs):
+    rows, half = unit // 2, halves[0]
+    first, refs = refs[:2], refs[2:]
+    if part:
+        second, refs = refs[:2], refs[2:]
+    (_, _, off, upper), refs = refs[:4], refs[4:]
+    if part:
+        (sep, middle, lower), refs = refs[:3], refs[3:]
+    off_at, upper_at, sem = refs
     width = off.shape[1]
-    w2 = lower.shape[1]
-    head = kept.shape[0] - unit
-    base, way = (pick(table, where[1]) for table in (owners, ways))
-    copies = []
-    for i in range(2):
-        here = pl.ds(i * rows, rows)
-        there = pl.ds(pl.multiple_of(base * unit + jnp.where(way == i, 0, rows), rows), rows)
-        for part, out in [(off_part, off), (upper_part, upper)]:
-            copies.append(pltpu.make_async_copy(part.at[here], out.at[there], sem.at[len(copies)]))
-    for i, (a, b) in enumerate([(kept, got), (got, kept)]):
+    base, way = (pick(t, where[1]) for t in table)
+    before = pick(owners, where[1]) * unit
+    places, start = [], 0
+    for i, (a, b) in enumerate([first, first[::-1]]):
 
         @pl.when(where[2] == i)
         def _():
-            off_part[...] = a[:unit, :width]
-            upper_part[...] = a[:unit, width:]
-            sep[:head] = a[unit:]
-            sep[head:] = b[: width - head]
-            at = width - head
-            middle[:width] = b[at : at + width, :w2]
-            middle[width:] = b[at : at + width, w2:]
-            at += width
-            lower[: w2 // 2] = b[at:, :w2]
-            lower[w2 // 2 :] = b[at:, w2:]
-
+            if part == 0:
+                for at, value in [(0, a[:half]), (half, b[: unit - half])]:
+                    off_at[at : at + value.shape[0]] = value[:, :width]
+                    upper_at[at : at + value.shape[0]] = value[:, width:]
+                return
+            c, d = second if i == 0 else second[::-1]
+            w1, w2 = middle.shape
+            rest = 2 * half - unit
+            sep[:rest] = b[unit - half : half]
+            sep[rest:] = c[: width - rest]
+            end = halves[1]
+            at = end - (width - rest)
+            middle[:at] = c[width - rest : end, :w2]
+            middle[width : width + at] = c[width - rest : end, w2:]
+            middle[at:width] = d[: width - at, :w2]
+            middle[width + at :] = d[: width - at, w2:]
+            lower[: w2 // 2] = d[width - at : end, :w2]
+            lower[w2 // 2 :] = d[width - at : end, w2:]
+
+    if part == 0:
+        places = [(i * rows, base * unit + jnp.where(way == i, 0, rows), rows) for i in range(2)]
+        start = unit
+    for i, ref in enumerate(second if part else first):
+        size = shares[part]
+        value = ref[halves[part] :]
+        off_at[start : start + size] = value[:, :width]
+        upper_at[start : start + size] = value[:, width:]
+        places.append((start, before + jnp.where(where[2] == i, 0, rows) + part * shares[0], size))
+        start += size
+    copies = []
+    for at, place, size in places:
+        there = pl.ds(pl.multiple_of(place, 8), size)
+        for value, out in [(off_at, off), (upper_at, upper)]:
+            copies.append(pltpu.make_async_copy(value.at[pl.ds(at, size)], out.at[there], sem.at[len(copies)]))
     for copy in copies:
         copy.start()
     for copy in copies:
         copy.wait()
 
 
-def finish(tables, where, kept, got, off, upper, unit, w1, w2):
+def finish(part, table, owners, where, sums, off, upper, unit, halves, shares, shapes=()):
     anywhere = pl.BlockSpec(memory_space=pl.ANY)
-    shapes = [off.shape, upper.shape, (w1 // 2, w1), (w1, w2), (w2, w2)]
+    rows = 2 * shares[part] + (0 if part else unit)
+    outs = [off.shape, upper.shape, *shapes]
+    at = 1 + len(sums)
     return pl.pallas_call(
-        functools.partial(finish_kernel, unit, *tables),
-        in_specs=[SMEM] + [VMEM] * 2 + [anywhere] * 2,
-        out_specs=[anywhere] * 2 + [VMEM] * 3,
-        out_shape=[jax.ShapeDtypeStruct(s, jnp.float32) for s in shapes],
+        functools.partial(finish_kernel, unit, halves, shares, part, table, owners),
+        in_specs=[SMEM] + [VMEM] * len(sums) + [anywhere] * 2,
+        out_specs=[anywhere] * 2 + [VMEM] * len(shapes),
+        out_shape=[jax.ShapeDtypeStruct(shape, jnp.float32) for shape in outs],
         scratch_shapes=[
-            pltpu.VMEM((unit, w1 // 2), jnp.float32),
-            pltpu.VMEM((unit, w2), jnp.float32),
-            pltpu.SemaphoreType.DMA((4,)),
+            pltpu.VMEM((rows, off.shape[1]), jnp.float32),
+            pltpu.VMEM((rows, upper.shape[1]), jnp.float32),
+            pltpu.SemaphoreType.DMA((4 if part else 8,)),
         ],
-        input_output_aliases={3: 0, 4: 1},
+        input_output_aliases={at: 0, at + 1: 1},
         compiler_params=pltpu.CompilerParams(vmem_limit_bytes=20 * MIB),
         cost_estimate=pl.CostEstimate(flops=1, bytes_accessed=1, transcendentals=0),
         name="finish",
-    )(where, kept, got, off, upper)
+    )(where, *sums, off, upper)
 
 
 def line_plan(n):
@@ -390,7 +474,8 @@
     pole_weight,
 ):
     pole, col = lax.axis_index("pole"), lax.axis_index("col")
-    where = jnp.stack([col, lax.axis_index("row"), jnp.where(col == 0, pole & 1, pole // 2)]).astype(jnp.int32)
+    far = jnp.where(col == 0, pole // 2, pole & 1)
+    where = jnp.stack([col, lax.axis_index("row"), far]).astype(jnp.int32)
     w0 = root_inverse.shape[2]
     w1, w2 = leaf_node_factor.shape[2:]
     own_rows = root_inverse.shape[1]
@@ -408,8 +493,10 @@
         up = [(2 * j + 1, 2 * j + 3) for j in range(slot - 1, n_row - 1)]
         moved[slot, i] = lax.ppermute(moved[slot - 1, i], ("row", "col"), down + up)
 
-    def swap(key):
-        other[key] = lax.ppermute(moved[key], "col", SWAP)
+    def swap(key, cuts=1):
+        size = moved[key].shape[0] // cuts
+        pieces = [moved[key][i * size : (i + 1) * size] for i in range(cuts)] if cuts > 1 else [moved[key]]
+        other[key] = tuple(lax.ppermute(piece, "col", SWAP) for piece in pieces)
 
     token = pole_weight
 
@@ -430,7 +517,9 @@
         return pair[0][:rows] + pair[1][:rows]
 
     def unit_of(form, k, which, *rest):
-        shards = [held[slot, i] for slot in slots[k] for held in (moved, other) for i in which]
+        shards = []
+        for slot in slots[k]:
+            shards += [(moved[slot, i],) for i in which] + [other[slot, i] for i in which]
         return unit_call(form, tables[k], where, token, shards, *rest)
 
     f_own = node_factor[:, 0]
@@ -438,12 +527,13 @@
     moved[0, 0] = root_inverse
     advance(1, 0)
     swap((0, 0))
-    moved[0, 1] = other[0, 0]
+    (moved[0, 1],) = other[0, 0]
     advance(1, 1)
-    root = weighted(pole_weight, root_inverse)
+    factors = prepare(where, leaf_pattern, f_own, f_other, leaf_root_factor[:, 0], leaf_node_factor[:, 0])
+    factors, root = together(factors, root_inverse)
+    root = weighted(pole_weight, root)
     root = jnp.concatenate([root[:, :w1], root[:, w1:]], axis=0)
     roots = (root, step(root, 0))
-    factors = prepare(where, leaf_pattern, f_own, f_other, leaf_root_factor[:, 0], leaf_node_factor[:, 0])
 
     (factors,) = hold([(1, 0)], factors)
     swap((1, 0))
@@ -463,46 +553,55 @@
     (first,) = hold([], first)
     hold([(1, 1)])
     rows, *sums = unit_of("next", 1, (0, 1), factors, sums)
-    rows, sums = hold([], rows, sums)
+    rows, sums = hold([(2, 1)], rows, sums)
     value = jnp.concatenate([rows, cut(first, unit)], axis=0)
+    swap((2, 1))
     second = (value, step(value, 0))
-
-    hold([(2, 1)])
-    swap((2, 1))
     advance(3, 1)
     hold([(2, 0)])
 
     hold([(3, 0)])
-    swap((3, 0))
-    (second,) = hold([], second)
-    value = cut(second, unit)
+    swap((3, 0), 2)
+    hold([(2, 1)])
+    keep3, send3, *sums = unit_of("halves", 2, (0, 1), factors, sums)
+    keep3, send3, sums, second = hold([], keep3, send3, sums, second)
+    value = jnp.concatenate([cut(second, unit), send3], axis=0)
     third = (value, step(value, 1))
-    hold([(2, 1)])
-    rows, *sums = unit_of("next", 2, (0, 1), factors, sums)
-    rows, sums = hold([], rows, sums)
-    fourth = (rows, step(rows, 0))
-
-    hold([(3, 1)])
-    swap((3, 1))
+
     hold([(3, 0)])
     kept = unit_of("part", 3, (0,), factors)
-    (third,) = hold([], third)
-    fourth, kept = hold([], fourth, kept)
-    value = cut(fourth, unit)
-    fifth = (value, step(value, 1))
+    (kept,) = hold([(3, 1)], kept)
+    swap((3, 1))
     hold([(3, 1)])
-    ends = (*kept, node_inverse[:, 0], leaf_node_factor[:, 0], leaf_inverse[:, 0])
-    keep, send = unit_of("last", 3, (1,), factors, sums, ends)
-    got = step(send, 0)
-    pieces = [(0, unit, own_rows, None, 0), (0, unit + own_rows, own_rows, None, w1), (1, unit, unit, 0, 0)]
-    pieces += [(2, 0, unit, 1, 0), (3, 0, unit, 2, 0)]
-    early = [v for pair in (first, second, third, fifth) for v in pair]
+    inv_n = node_inverse[:, 0]
+    keep, send, rest, *sums = unit_of("last", 3, (1,), factors, sums, (*kept, inv_n))
+    keep, send, rest, sums = hold([], keep, send, rest, sums)
+    got = step(send, 1)
+    keep2, send2 = ends_call(where, token, *sums, rest, inv_n, leaf_node_factor[:, 0], leaf_inverse[:, 0])
+    keep2, send2, keep3, third = hold([], keep2, send2, keep3, third)
+    got2 = step(send2, 1)
+    keep3 = keep3 + third[1][unit:]
+    halves, shares = halved(own_rows, w1, w2)
+    keep, got = hold([], keep, got)
+    keep = jnp.concatenate([keep + got, keep3[: shares[0]]], axis=0)
+    got = step(keep, 0)
+    keep2, got2 = hold([], keep2, got2)
+    keep2 = jnp.concatenate([keep2 + got2, keep3[shares[0] :]], axis=0)
+    got2 = step(keep2, 0)
+    pieces = [(0, unit, own_rows, None, 0), (0, unit + own_rows, own_rows, None, w1), (1, unit, unit, 0, 0), (2, 0, unit, 1, 0)]
+    early = [v for pair in (first, second, third) for v in pair]
     root, off, upper = place(owners, pieces, where, early, unit, w0, w2)
     keep, got, root, off, upper = hold([], keep, got, root, off, upper)
     keep = keep + got
-    keep = keep + step(keep, 1)
-    got = step(keep, 0)
-    off, upper, sep, middle, lower = finish(tables[3][::2], where, keep, got, off, upper, unit, w1, w2)
+    got = step(keep, 1)
+    keep2, got2 = hold([], keep2, got2)
+    keep2 = keep2 + got2
+    got2 = step(keep2, 1)
+    keep, got = hold([], keep, got)
+    places = (tables[3][::2], owners[2], where)
+    off, upper = finish(0, *places, (keep, got), off, upper, unit, halves, shares)
+    shapes = [(w1 // 2, w1), (w1, w2), (w2, w2)]
+    off, upper, sep, middle, lower = finish(1, *places, (keep, got, keep2, got2), off, upper, unit, halves, shares, shapes)
     return root, off[None], sep[None], upper[None], middle[None], lower[None]
 
 

time: 147 us -> 125 us (0.85)
  waiting for transfers between devices: 74.9 us -> 49.9 us
  starting transfers between devices: 24.3 us -> 31.1 us
  other arithmetic: 4.37 us -> 1.16 us
    ppermute x9 -> x10, waiting for transfers between devices: 57.2 us -> 23.4 us  [step(): return lax.ppermute(value, ('pole', 'col'), pairs)]
    ppermute x6, waiting for transfers between devices: 13.6 us -> 21.8 us  [advance(): moved[slot, i] = lax.ppermute(moved[slot - 1, i], ('row', 'col'), down + up)]
    ppermute x9 -> x10, starting transfers between devices: 13.3 us -> 20.2 us  [step(): return lax.ppermute(value, ('pole', 'col'), pairs)]
    pallas_call x6 -> x7, Pallas kernels: 31.1 us -> 29.3 us  [call(): pl.pallas_call(kernel, in_specs=[SMEM] * smem + [VMEM] * (len(args) - sme...]
    pallas_call x1 -> x2, Pallas kernels: 2.54 us -> 3.95 us  [finish(): pl.pallas_call(functools.partial(finish_kernel, unit, halves, shares, par...]
    ppermute x7 -> x8, waiting for transfers between devices: 4.06 us -> 4.67 us  [swap(): other[key] = tuple((lax.ppermute(piece, 'col', SWAP) for piece in pieces))]
  transfers between devices with their start and end apart: 23 -> 25, of which waited for: 10 -> 14; matrix products, arithmetic and copies ran while one was open for 3% -> 1% of each run, Pallas kernels for 22% -> 31%
where the time goes in v3:
time: 125 us
  waiting for transfers between devices  49.9 us (40%)
  Pallas kernels  41 us (33%)
  starting transfers between devices  31.1 us (25%)
    pallas_call x7, Pallas kernels, call(): pl.pallas_call(kernel, in_specs=[SMEM] * smem + [VMEM] * (len(args) - sme...  29.3 us
    ppermute x10, waiting for transfers between devices, step(): return lax.ppermute(value, ('pole', 'col'), pairs)  23.4 us
    ppermute x6, waiting for transfers between devices, advance(): moved[slot, i] = lax.ppermute(moved[slot - 1, i], ('row', 'col'), down + up)  21.8 us
    ppermute x10, starting transfers between devices, step(): return lax.ppermute(value, ('pole', 'col'), pairs)  20.2 us
    pallas_call x1, Pallas kernels, prepare(): pl.pallas_call(prepare_kernel, in_specs=[SMEM] * 2 + [VMEM] + [pl.BlockSp...  7.69 us
    ppermute x6, starting transfers between devices, advance(): moved[slot, i] = lax.ppermute(moved[slot - 1, i], ('row', 'col'), down + up)  7.68 us
    ppermute x8, waiting for transfers between devices, swap(): other[key] = tuple((lax.ppermute(piece, 'col', SWAP) for piece in pieces))  4.67 us
    pallas_call x2, Pallas kernels, finish(): pl.pallas_call(functools.partial(finish_kernel, unit, halves, shares, par...  3.95 us
  transfers between devices with their start and end apart: 25, of which 14 were waited for; matrix products, arithmetic and copies ran while one was open for 1% of the time, Pallas kernels for 31%

profile of v3, /device:TPU:0, one launch (start us, length us, event | category | flops | bytes accessed | tf_op | source)
XLA Modules:
  0.0 125.1 jit_solution(16456459132359448979)
XLA Ops:
  2.5 4.2 %collective-permute-done.refs_1_ = f32[2,128,1024]{2,1,0:T(8,128)} collective-permute-done((f32[2,128,1024]{2,1,0:T(8,128)}, f32[2,128,1024]{2,1,0:T(8,128)}, u32[]{:S(2)}, u32[]{:S(2)}) %collective-permute-start) | collective-permute-done | bytes 1048608 | tf_op jit(solution)/shard_map/ppermute | solution.py:499
  8.7 7.7 %prepare.1 = (bf16[2,1024,768]{2,1,0:T(8,128)(2,1)S(1)}, bf16[2,1024,768]{2,1,0:T(8,128)(2,1)S(1)}, bf16[2,1024,256]{2,1,0:T(8,128)(2,1)S(1)}, bf16[2,1024,256]{2,1,0:T(8,128)(2,1)S(1)}) custom-call(s32[3]{0:T(128)S(1)} %pad_add_fusion.where, s32[1,8]{1,0:T(1,128)S(1)} %copy-done.5, f32[2,1024,256]{2,1,0:T(8,128)S(1)} %collective-permute-done.3.f_other, ...), custom_call_target="tpu_custom_call" | custom-call | flops 1 | bytes 1 | tf_op jit(solution)/shard_map/prepare/pallas_call | solution.py:154
  16.7 2.6 %collective-permute-start.8 = (f32[256,512]{1,0:T(8,128)S(1)}, f32[256,512]{1,0:T(8,128)S(1)}, u32[]{:S(2)}, u32[]{:S(2)}) collective-permute-start(f32[256,512]{1,0:T(8,128)S(1)} %pad_maximum_fusion.4), channel_id=1, source_target_pairs={{0,8},{1,17},{8,0},{9,25},{16,24},{17,1},{24,16},{25,9},{2,10},{3,... | collective-permute-start | bytes 1572872 | tf_op jit(solution)/shard_map/ppermute | solution.py:514
  19.4 2.1 %collective-permute-start.7 = (f32[2,128,1024]{2,1,0:T(8,128)S(1)}, f32[2,128,1024]{2,1,0:T(8,128)S(1)}, u32[]{:S(2)}, u32[]{:S(2)}) collective-permute-start(f32[2,128,1024]{2,1,0:T(8,128)S(1)} %collective-permute-done.2.refs_0_), channel_id=1, source_target_pairs={{0,1},{1,0},{2,3},{3,2},{4,5},{5,4},{6,7},{7,6},{8,9},{9,8},{10,11... | collective-permute-start | bytes 3145736 | tf_op jit(solution)/shard_map/ppermute | solution.py:499
  22.7 5.6 %first.1 = (f32[256,512]{1,0:T(8,128)S(1)}, f32[2,768,512]{2,1,0:T(8,128)S(1)}, f32[2,256,256]{2,1,0:T(8,128)S(1)}) custom-call(s32[3]{0:T(128)S(1)} %pad_add_fusion.where, f32[2]{0:T(128)S(1)} %copy-done.4, f32[2,128,1024]{2,1,0:T(8,128)S(1)} %copy-done.2, f32[2,128,1024]{2,1,0:T(8,128)} %collective-permute-done.refs_1_, ...), custom_call_target="tpu_custom_call" | custom-call | flops 1 | bytes 1 | tf_op jit(solution)/shard_map/first/pallas_call | solution.py:70
  33.8 7.7 %collective-permute-done.6.refs_4_.refs_0_ = f32[2,128,1024]{2,1,0:T(8,128)S(1)} collective-permute-done((f32[2,128,1024]{2,1,0:T(8,128)S(1)}, f32[2,128,1024]{2,1,0:T(8,128)S(1)}, u32[]{:S(2)}, u32[]{:S(2)}) %collective-permute-start.6) | collective-permute-done | bytes 1048608 | tf_op jit(solution)/shard_map/ppermute | solution.py:494
  42.9 2.5 %collective-permute-done.9.refs_1_ = f32[512,512]{1,0:T(8,128)S(1)} collective-permute-done((f32[512,512]{1,0:T(8,128)S(1)}, f32[512,512]{1,0:T(8,128)S(1)}, u32[]{:S(2)}, u32[]{:S(2)}) %collective-permute-start.9) | collective-permute-done | bytes 1048608 | tf_op jit(solution)/shard_map/ppermute | solution.py:514
  45.4 5.6 %next.1 = (f32[256,512]{1,0:T(8,128)S(1)}, f32[2,768,512]{2,1,0:T(8,128)S(1)}, f32[2,256,256]{2,1,0:T(8,128)S(1)}) custom-call(s32[3]{0:T(128)S(1)} %pad_add_fusion.where, f32[2]{0:T(128)S(1)} %copy-done.4, f32[2,128,1024]{2,1,0:T(8,128)S(1)} %collective-permute-done.2.refs_0_, ...), custom_call_target="tpu_custom_call", output_to_operand_aliasing={{1}: (10, {}), {2}: (11, {})} | custom-call | flops 1 | bytes 1 | tf_op jit(solution)/shard_map/next/pallas_call | solution.py:70
  56.3 7.8 %collective-permute-done.11.refs_2_ = f32[2,128,1024]{2,1,0:T(8,128)S(1)} collective-permute-done((f32[2,128,1024]{2,1,0:T(8,128)S(1)}, f32[2,128,1024]{2,1,0:T(8,128)S(1)}, u32[]{:S(2)}, u32[]{:S(2)}) %collective-permute-start.11) | collective-permute-done | bytes 1048608 | tf_op jit(solution)/shard_map/ppermute | solution.py:494
  64.7 5.5 %halves.1 = (f32[128,512]{1,0:T(8,128)S(1)}, f32[128,512]{1,0:T(8,128)S(1)}, f32[2,768,512]{2,1,0:T(8,128)S(1)}, f32[2,256,256]{2,1,0:T(8,128)S(1)}) custom-call(s32[3]{0:T(128)S(1)} %pad_add_fusion.where, f32[2]{0:T(128)S(1)} %copy-done.4, f32[2,128,1024]{2,1,0:T(8,128)S(1)} %collective-permute-done.2.refs_0_, ...), custom_call_target="tpu_custom_call", output_to_operand_aliasing={{2}: (14, {}), {3}: (15, {})} | custom-call | flops 1 | bytes 1 | tf_op jit(solution)/shard_map/halves/pallas_call | solution.py:70
  70.3 2.5 %part.1 = (f32[128,512]{1,0:T(8,128)S(1)}, bf16[2,128,768]{2,1,0:T(8,128)(2,1)S(1)}, bf16[2,128,768]{2,1,0:T(8,128)(2,1)S(1)}) custom-call(s32[3]{0:T(128)S(1)} %pad_add_fusion.where, f32[2]{0:T(128)S(1)} %copy-done.4, f32[2,128,1024]{2,1,0:T(8,128)S(1)} %collective-permute-done.6.refs_4_.refs_0_, ...), custom_call_target="tpu_custom_call" | custom-call | flops 1 | bytes 1 | tf_op jit(solution)/shard_map/part/pallas_call | solution.py:70
  72.8 2.5 %collective-permute-done.10.refs_2_ = f32[2,128,1024]{2,1,0:T(8,128)S(1)} collective-permute-done((f32[2,128,1024]{2,1,0:T(8,128)S(1)}, f32[2,128,1024]{2,1,0:T(8,128)S(1)}, u32[]{:S(2)}, u32[]{:S(2)}) %collective-permute-start.10) | collective-permute-done | bytes 1048608 | tf_op jit(solution)/shard_map/ppermute | solution.py:494
  75.4 2.0 %collective-permute-start.19 = (f32[384,512]{1,0:T(8,128)S(1)}, f32[384,512]{1,0:T(8,128)S(1)}, u32[]{:S(2)}, u32[]{:S(2)}) collective-permute-start(f32[384,512]{1,0:T(8,128)S(1)} %pad_maximum_fusion.2.refs_4_), channel_id=1, source_target_pairs={{0,16},{1,9},{8,24},{9,1},{16,0},{17,25},{24,8},{25,17},{2,18},{3,... | collective-permute-start | bytes 2359304 | tf_op jit(solution)/shard_map/ppermute | solution.py:514
  78.0 4.5 %last.1 = (f32[224,512]{1,0:T(8,128)S(1)}, f32[224,512]{1,0:T(8,128)S(1)}, f32[64,512]{1,0:T(8,128)S(1)}, f32[2,768,512]{2,1,0:T(8,128)S(1)}, f32[2,256,256]{2,1,0:T(8,128)S(1)}) custom-call(s32[3]{0:T(128)S(1)} %pad_add_fusion.where, f32[2]{0:T(128)S(1)} %copy-done.4, ...), custom_call_target="tpu_custom_call", output_to_operand_aliasing={{3}: (10, {}), {4}: (11, {})} | custom-call | flops 1 | bytes 1 | tf_op jit(solution)/shard_map/last/pallas_call | solution.py:70
  82.5 2.0 %collective-permute-start.18 = (f32[224,512]{1,0:T(8,128)S(1)}, f32[224,512]{1,0:T(8,128)S(1)}, u32[]{:S(2)}, u32[]{:S(2)}) collective-permute-start(f32[224,512]{1,0:T(8,128)S(1)} %get-tuple-element.207), channel_id=1, source_target_pairs={{0,16},{1,9},{8,24},{9,1},{16,0},{17,25},{24,8},{25,17},{2,18},{3,... | collective-permute-start | bytes 1376264 | tf_op jit(solution)/shard_map/ppermute | solution.py:514
  84.5 3.3 %ends.1 = (f32[224,512]{1,0:T(8,128)S(1)}, f32[224,512]{1,0:T(8,128)S(1)}) custom-call(s32[3]{0:T(128)S(1)} %pad_add_fusion.where, f32[2]{0:T(128)S(1)} %copy-done.4, f32[2,768,512]{2,1,0:T(8,128)S(1)} %get-tuple-element.211.gram, f32[2,256,256]{2,1,0:T(8,128)S(1)} %get-tuple-element.212.square, f32[64,512]{1,0:T(8,128)S(1)} %get-tuple-element.213.sep, ...), custom_call_target="tpu_custom_call" | custom-call | flops 1 | bytes 1 | tf_op jit(solution)/shard_map/ends/pallas_call | solution.py:70
  89.5 2.9 %collective-permute-done.18 = f32[224,512]{1,0:T(8,128)S(1)} collective-permute-done((f32[224,512]{1,0:T(8,128)S(1)}, f32[224,512]{1,0:T(8,128)S(1)}, u32[]{:S(2)}, u32[]{:S(2)}) %collective-permute-start.18) | collective-permute-done | bytes 458784 | tf_op jit(solution)/shard_map/ppermute | solution.py:514
  94.5 5.0 %collective-permute-done.22 = f32[224,512]{1,0:T(8,128)S(1)} collective-permute-done((f32[224,512]{1,0:T(8,128)S(1)}, f32[224,512]{1,0:T(8,128)S(1)}, u32[]{:S(2)}, u32[]{:S(2)}) %collective-permute-start.22) | collective-permute-done | bytes 458784 | tf_op jit(solution)/shard_map/ppermute | solution.py:514
  99.6 2.2 %collective-permute-start.23 = (f32[240,512]{1,0:T(8,128)S(1)}, f32[240,512]{1,0:T(8,128)S(1)}, u32[]{:S(2)}, u32[]{:S(2)}) collective-permute-start(f32[240,512]{1,0:T(8,128)S(1)} %pad_maximum_fusion.5), channel_id=1, source_target_pairs={{0,8},{1,17},{8,0},{9,25},{16,24},{17,1},{24,16},{25,9},{2,10},{3,... | collective-permute-start | bytes 1474568 | tf_op jit(solution)/shard_map/ppermute | solution.py:514
  101.8 2.2 %place.1 = (f32[128,1024]{1,0:T(8,128)}, f32[1024,256]{1,0:T(8,128)}, f32[1024,256]{1,0:T(8,128)}) custom-call(s32[3]{0:T(128)S(1)} %pad_add_fusion.where, f32[512,512]{1,0:T(8,128)S(1)} %pad_maximum_fusion.refs_0_, f32[512,512]{1,0:T(8,128)S(1)} %collective-permute-done.9.refs_1_, f32[512,512]{1,0:T(8,128)S(1)} %pad_maximum_fusion.1.refs_2_, ...), custom_call_target="tpu_custom_call" | custom-call | flops 1 | bytes 1 | tf_op jit(solution)/shard_map/place/pallas_call | solution.py:70
  106.4 5.2 %collective-permute-done.23 = f32[240,512]{1,0:T(8,128)S(1)} collective-permute-done((f32[240,512]{1,0:T(8,128)S(1)}, f32[240,512]{1,0:T(8,128)S(1)}, u32[]{:S(2)}, u32[]{:S(2)}) %collective-permute-start.23) | collective-permute-done | bytes 491552 | tf_op jit(solution)/shard_map/ppermute | solution.py:514
  113.4 3.9 %collective-permute-done.21.refs_1_ = f32[336,512]{1,0:T(8,128)S(1)} collective-permute-done((f32[336,512]{1,0:T(8,128)S(1)}, f32[336,512]{1,0:T(8,128)S(1)}, u32[]{:S(2)}, u32[]{:S(2)}) %collective-permute-start.21) | collective-permute-done | bytes 688160 | tf_op jit(solution)/shard_map/ppermute | solution.py:514
  118.9 3.7 %collective-permute-done.24.refs_3_ = f32[240,512]{1,0:T(8,128)S(1)} collective-permute-done((f32[240,512]{1,0:T(8,128)S(1)}, f32[240,512]{1,0:T(8,128)S(1)}, u32[]{:S(2)}, u32[]{:S(2)}) %collective-permute-start.24) | collective-permute-done | bytes 491552 | tf_op jit(solution)/shard_map/ppermute | solution.py:514
  122.6 2.3 %finish.3 = (f32[1024,256]{1,0:T(8,128)}, f32[1024,256]{1,0:T(8,128)}, f32[256,512]{1,0:T(8,128)}, f32[512,256]{1,0:T(8,128)}, f32[256,256]{1,0:T(8,128)}) custom-call(s32[3]{0:T(128)S(1)} %pad_add_fusion.where, f32[336,512]{1,0:T(8,128)S(1)} %add.30.refs_0_, ...), custom_call_target="tpu_custom_call", output_to_operand_aliasing={{0}: (5, {}), {1}: (6, {})} | custom-call | flops 1 | bytes 1 | tf_op jit(solution)/shard_map/finish/pallas_call | solution.py:433
  (68 shorter events, 28.3 us)
Async XLA Ops:
  0.6 7.4 %collective-permute-start.3 = (f32[2,1024,256]{2,1,0:T(8,128)}, f32[2,1024,256]{2,1,0:T(8,128)S(1)}, u32[]{:S(2)}, u32[]{:S(2)}) collective-permute-start(f32[2,1024,256]{2,1,0:T(8,128)} %bitcast.20), channel_id=1, source_target_pairs={{0,1},{1,0},{2,3},{3,2},{4,5},{5,4},{6,7},{7,6},{8,9},{9,8},{10,11... | collective-permute-start | bytes 6291464 | tf_op jit(solution)/shard_map/ppermute | solution.py:526
  1.1 5.5 %collective-permute-start = (f32[2,128,1024]{2,1,0:T(8,128)}, f32[2,128,1024]{2,1,0:T(8,128)}, u32[]{:S(2)}, u32[]{:S(2)}) collective-permute-start(f32[2,128,1024]{2,1,0:T(8,128)} %refs_0_.1), channel_id=1, source_target_pairs={{0,1},{1,0},{2,3},{3,2},{4,5},{5,4},{6,7},{7,6},{8,9},{9,8},{10,11... | collective-permute-start | bytes 3145736 | tf_op jit(solution)/shard_map/ppermute | solution.py:499
  1.2 18.1 %collective-permute-start.2 = (f32[2,128,1024]{2,1,0:T(8,128)}, f32[2,128,1024]{2,1,0:T(8,128)S(1)}, u32[]{:S(2)}, u32[]{:S(2)}) collective-permute-start(f32[2,128,1024]{2,1,0:T(8,128)} %refs_0_.1), channel_id=1, source_target_pairs={{2,0},{4,2},{6,4},{1,3},{3,5},{5,7},{10,8},{12,10},{14,12},{9,11},... | collective-permute-start | bytes 3145736 | tf_op jit(solution)/shard_map/ppermute | solution.py:494
  6.7 23.6 %collective-permute-start.1 = (f32[2,128,1024]{2,1,0:T(8,128)}, f32[2,128,1024]{2,1,0:T(8,128)S(1)}, u32[]{:S(2)}, u32[]{:S(2)}) collective-permute-start(f32[2,128,1024]{2,1,0:T(8,128)} %collective-permute-done.refs_1_), channel_id=1, source_target_pairs={{2,0},{4,2},{6,4},{1,3},{3,5},{5,7},{10,8},{12,10},{14,12},{9,11},... | collective-permute-start | bytes 3145736 | tf_op jit(solution)/shard_map/ppermute | solution.py:494
  16.7 13.6 %collective-permute-start.8 = (f32[256,512]{1,0:T(8,128)S(1)}, f32[256,512]{1,0:T(8,128)S(1)}, u32[]{:S(2)}, u32[]{:S(2)}) collective-permute-start(f32[256,512]{1,0:T(8,128)S(1)} %pad_maximum_fusion.4), channel_id=1, source_target_pairs={{0,8},{1,17},{8,0},{9,25},{16,24},{17,1},{24,16},{25,9},{2,10},{3,... | collective-permute-start | bytes 1572872 | tf_op jit(solution)/shard_map/ppermute | solution.py:514
  19.4 14.5 %collective-permute-start.7 = (f32[2,128,1024]{2,1,0:T(8,128)S(1)}, f32[2,128,1024]{2,1,0:T(8,128)S(1)}, u32[]{:S(2)}, u32[]{:S(2)}) collective-permute-start(f32[2,128,1024]{2,1,0:T(8,128)S(1)} %collective-permute-done.2.refs_0_), channel_id=1, source_target_pairs={{0,1},{1,0},{2,3},{3,2},{4,5},{5,4},{6,7},{7,6},{8,9},{9,8},{10,11... | collective-permute-start | bytes 3145736 | tf_op jit(solution)/shard_map/ppermute | solution.py:499
  21.4 20.1 %collective-permute-start.6 = (f32[2,128,1024]{2,1,0:T(8,128)S(1)}, f32[2,128,1024]{2,1,0:T(8,128)S(1)}, u32[]{:S(2)}, u32[]{:S(2)}) collective-permute-start(f32[2,128,1024]{2,1,0:T(8,128)S(1)} %collective-permute-done.2.refs_0_), channel_id=1, source_target_pairs={{2,0},{4,2},{3,5},{5,7},{10,8},{12,10},{11,13},{13,15},{18,16},{20... | collective-permute-start | bytes 3145736 | tf_op jit(solution)/shard_map/ppermute | solution.py:494
  30.5 14.9 %collective-permute-start.9 = (f32[512,512]{1,0:T(8,128)S(1)}, f32[512,512]{1,0:T(8,128)S(1)}, u32[]{:S(2)}, u32[]{:S(2)}) collective-permute-start(f32[512,512]{1,0:T(8,128)S(1)} %pad_maximum_fusion.refs_0_), channel_id=1, source_target_pairs={{0,16},{1,9},{8,24},{9,1},{16,0},{17,25},{24,8},{25,17},{2,18},{3,... | collective-permute-start | bytes 3145736 | tf_op jit(solution)/shard_map/ppermute | solution.py:514
  32.5 12.8 %collective-permute-start.5 = (f32[2,128,1024]{2,1,0:T(8,128)S(1)}, f32[2,128,1024]{2,1,0:T(8,128)S(1)}, u32[]{:S(2)}, u32[]{:S(2)}) collective-permute-start(f32[2,128,1024]{2,1,0:T(8,128)S(1)} %collective-permute-done.1.refs_1_), channel_id=1, source_target_pairs={{0,1},{1,0},{2,3},{3,2},{4,5},{5,4},{6,7},{7,6},{8,9},{9,8},{10,11... | collective-permute-start | bytes 3145736 | tf_op jit(solution)/shard_map/ppermute | solution.py:499
  32.5 20.3 %collective-permute-start.4 = (f32[2,128,1024]{2,1,0:T(8,128)S(1)}, f32[2,128,1024]{2,1,0:T(8,128)S(1)}, u32[]{:S(2)}, u32[]{:S(2)}) collective-permute-start(f32[2,128,1024]{2,1,0:T(8,128)S(1)} %collective-permute-done.1.refs_1_), channel_id=1, source_target_pairs={{2,0},{4,2},{3,5},{5,7},{10,8},{12,10},{11,13},{13,15},{18,16},{20... | collective-permute-start | bytes 3145736 | tf_op jit(solution)/shard_map/ppermute | solution.py:494
  41.6 14.7 %collective-permute-start.12 = (f32[2,128,1024]{2,1,0:T(8,128)S(1)}, f32[2,128,1024]{2,1,0:T(8,128)S(1)}, u32[]{:S(2)}, u32[]{:S(2)}) collective-permute-start(f32[2,128,1024]{2,1,0:T(8,128)S(1)} %collective-permute-done.6.refs_4_.refs_0_), channel_id=1, source_target_pairs={{0,1},{1,0},{2,3},{3,2},{4,5},{5,4},{6,7},{7,6},{8,9},{9,8},{10,11... | collective-permute-start | bytes 3145736 | tf_op jit(solution)/shard_map/ppermute | solution.py:499
  41.6 22.5 %collective-permute-start.11 = (f32[2,128,1024]{2,1,0:T(8,128)S(1)}, f32[2,128,1024]{2,1,0:T(8,128)S(1)}, u32[]{:S(2)}, u32[]{:S(2)}) collective-permute-start(f32[2,128,1024]{2,1,0:T(8,128)S(1)} %collective-permute-done.6.refs_4_.refs_0_), channel_id=1, source_target_pairs={{2,0},{5,7},{10,8},{13,15},{18,16},{21,23},{26,24},{29,31}} | collective-permute-start | bytes 3145736 | tf_op jit(solution)/shard_map/ppermute | solution.py:494
  52.8 11.9 %collective-permute-start.15 = (f32[2,128,1024]{2,1,0:T(8,128)S(1)}, f32[2,128,1024]{2,1,0:T(8,128)S(1)}, u32[]{:S(2)}, u32[]{:S(2)}) collective-permute-start(f32[2,128,1024]{2,1,0:T(8,128)S(1)} %collective-permute-done.4.refs_5_.refs_0_), channel_id=1, source_target_pairs={{0,1},{1,0},{2,3},{3,2},{4,5},{5,4},{6,7},{7,6},{8,9},{9,8},{10,11... | collective-permute-start | bytes 3145736 | tf_op jit(solution)/shard_map/ppermute | solution.py:499
  53.0 17.3 %collective-permute-start.16 = (f32[512,512]{1,0:T(8,128)S(1)}, f32[512,512]{1,0:T(8,128)S(1)}, u32[]{:S(2)}, u32[]{:S(2)}) collective-permute-start(f32[512,512]{1,0:T(8,128)S(1)} %pad_maximum_fusion.1.refs_2_), channel_id=1, source_target_pairs={{0,8},{1,17},{8,0},{9,25},{16,24},{17,1},{24,16},{25,9},{2,10},{3,... | collective-permute-start | bytes 3145736 | tf_op jit(solution)/shard_map/ppermute | solution.py:514
  55.0 20.3 %collective-permute-start.10 = (f32[2,128,1024]{2,1,0:T(8,128)S(1)}, f32[2,128,1024]{2,1,0:T(8,128)S(1)}, u32[]{:S(2)}, u32[]{:S(2)}) collective-permute-start(f32[2,128,1024]{2,1,0:T(8,128)S(1)} %collective-permute-done.4.refs_5_.refs_0_), channel_id=1, source_target_pairs={{2,0},{5,7},{10,8},{13,15},{18,16},{21,23},{26,24},{29,31}} | collective-permute-start | bytes 3145736 | tf_op jit(solution)/shard_map/ppermute | solution.py:494
  64.2 6.1 %collective-permute-start.13 = (f32[1,128,1024]{2,1,0:T(8,128)S(1)}, f32[1,128,1024]{2,1,0:T(8,128)S(1)}, u32[]{:S(2)}, u32[]{:S(2)}) collective-permute-start(f32[1,128,1024]{2,1,0:T(8,128)S(1)} %get-tuple-element.247), channel_id=1, source_target_pairs={{0,1},{1,0},{2,3},{3,2},{4,5},{5,4},{6,7},{7,6},{8,9},{9,8},{10,11... | collective-permute-start | bytes 1572872 | tf_op jit(solution)/shard_map/ppermute | solution.py:499
  64.2 6.0 %collective-permute-start.14 = (f32[1,128,1024]{2,1,0:T(8,128)S(1)}, f32[1,128,1024]{2,1,0:T(8,128)S(1)}, u32[]{:S(2)}, u32[]{:S(2)}) collective-permute-start(f32[1,128,1024]{2,1,0:T(8,128)S(1)} %get-tuple-element.246), channel_id=1, source_target_pairs={{0,1},{1,0},{2,3},{3,2},{4,5},{5,4},{6,7},{7,6},{8,9},{9,8},{10,11... | collective-permute-start | bytes 1572872 | tf_op jit(solution)/shard_map/ppermute | solution.py:499
  75.4 12.4 %collective-permute-start.19 = (f32[384,512]{1,0:T(8,128)S(1)}, f32[384,512]{1,0:T(8,128)S(1)}, u32[]{:S(2)}, u32[]{:S(2)}) collective-permute-start(f32[384,512]{1,0:T(8,128)S(1)} %pad_maximum_fusion.2.refs_4_), channel_id=1, source_target_pairs={{0,16},{1,9},{8,24},{9,1},{16,0},{17,25},{24,8},{25,17},{2,18},{3,... | collective-permute-start | bytes 2359304 | tf_op jit(solution)/shard_map/ppermute | solution.py:514
  82.5 9.9 %collective-permute-start.18 = (f32[224,512]{1,0:T(8,128)S(1)}, f32[224,512]{1,0:T(8,128)S(1)}, u32[]{:S(2)}, u32[]{:S(2)}) collective-permute-start(f32[224,512]{1,0:T(8,128)S(1)} %get-tuple-element.207), channel_id=1, source_target_pairs={{0,16},{1,9},{8,24},{9,1},{16,0},{17,25},{24,8},{25,17},{2,18},{3,... | collective-permute-start | bytes 1376264 | tf_op jit(solution)/shard_map/ppermute | solution.py:514
  87.9 11.6 %collective-permute-start.22 = (f32[224,512]{1,0:T(8,128)S(1)}, f32[224,512]{1,0:T(8,128)S(1)}, u32[]{:S(2)}, u32[]{:S(2)}) collective-permute-start(f32[224,512]{1,0:T(8,128)S(1)} %get-tuple-element.232), channel_id=1, source_target_pairs={{0,16},{1,9},{8,24},{9,1},{16,0},{17,25},{24,8},{25,17},{2,18},{3,... | collective-permute-start | bytes 1376264 | tf_op jit(solution)/shard_map/ppermute | solution.py:514
  92.5 11.9 %collective-permute-start.20 = (f32[336,512]{1,0:T(8,128)S(1)}, f32[336,512]{1,0:T(8,128)S(1)}, u32[]{:S(2)}, u32[]{:S(2)}) collective-permute-start(f32[336,512]{1,0:T(8,128)S(1)} %pad_maximum_fusion.3), channel_id=1, source_target_pairs={{0,8},{1,17},{8,0},{9,25},{16,24},{17,1},{24,16},{25,9},{2,10},{3,... | collective-permute-start | bytes 2064392 | tf_op jit(solution)/shard_map/ppermute | solution.py:514
  99.6 11.9 %collective-permute-start.23 = (f32[240,512]{1,0:T(8,128)S(1)}, f32[240,512]{1,0:T(8,128)S(1)}, u32[]{:S(2)}, u32[]{:S(2)}) collective-permute-start(f32[240,512]{1,0:T(8,128)S(1)} %pad_maximum_fusion.5), channel_id=1, source_target_pairs={{0,8},{1,17},{8,0},{9,25},{16,24},{17,1},{24,16},{25,9},{2,10},{3,... | collective-permute-start | bytes 1474568 | tf_op jit(solution)/shard_map/ppermute | solution.py:514
  104.5 12.8 %collective-permute-start.21 = (f32[336,512]{1,0:T(8,128)S(1)}, f32[336,512]{1,0:T(8,128)S(1)}, u32[]{:S(2)}, u32[]{:S(2)}) collective-permute-start(f32[336,512]{1,0:T(8,128)S(1)} %add.30.refs_0_), channel_id=1, source_target_pairs={{0,16},{1,9},{8,24},{9,1},{16,0},{17,25},{24,8},{25,17},{2,18},{3,... | collective-permute-start | bytes 2064392 | tf_op jit(solution)/shard_map/ppermute | solution.py:514
  111.6 11.0 %collective-permute-start.24 = (f32[240,512]{1,0:T(8,128)S(1)}, f32[240,512]{1,0:T(8,128)S(1)}, u32[]{:S(2)}, u32[]{:S(2)}) collective-permute-start(f32[240,512]{1,0:T(8,128)S(1)} %add.32.refs_2_), channel_id=1, source_target_pairs={{0,16},{1,9},{8,24},{9,1},{16,0},{17,25},{24,8},{25,17},{2,18},{3,... | collective-permute-start | bytes 1474568 | tf_op jit(solution)/shard_map/ppermute | solution.py:514
  (7 other events, 37.1 us)

commit v4 on v3

--- a/solution.py
+++ b/solution.py
@@ -179,7 +179,7 @@
     if form in ("next", "halves", "last"):
         (gram_in, square_in), refs = refs[:2], refs[2:]
     if form == "last":
-        (kept_rows, kept_high, kept_low, inv_n), refs = refs[:4], refs[4:]
+        (kept_high, kept_low, inv_n), refs = refs[:3], refs[3:]
     if form == "last":
         outs, (r_high, r_low, sent_at, sep_at) = refs[:-4], refs[-4:]
     else:
@@ -221,18 +221,15 @@
         mine = jnp.where(col == 0, x[:, :width], x[:, width:w1])
         sent = -scale * jnp.concatenate([mine, x[:, w1:]], axis=1)
         sent_ref = sent_at if form == "last" else outs[0]
-        if form == "halves":
-            if p == 0:
-                total = sent
-            else:
-                total = total + sent
+        if form in ("halves", "part"):
+            total = sent if p == 0 else total + sent
         elif p == 0:
             sent_ref[...] = sent
         else:
             sent_ref[...] += sent
         xs = split(x)
         if form == "part":
-            outs[1][p], outs[2][p] = xs
+            outs[2][p], outs[3][p] = xs
             continue
         if form == "last":
             xs = [jnp.concatenate([kept[p], v], axis=0) for kept, v in zip((kept_high, kept_low), xs)]
@@ -258,34 +255,28 @@
                 sep_at[...] = sep
             else:
                 sep_at[...] += sep
-    if form == "halves":
+    if form in ("halves", "part"):
         for i in range(2):
 
             @pl.when(where[2] == i)
             def _():
-                outs[i][...] = total[:rows]
-                outs[1 - i][...] = total[rows:]
+                outs[i][...] = total[: span // 2]
+                outs[1 - i][...] = total[span // 2 :]
 
     if form == "last":
-        half = outs[0].shape[0]
-        split_at = half - rows
+        head = outs[0].shape[0] - rows
         for i in range(2):
 
             @pl.when(where[2] == i)
             def _():
-                outs[i][:rows] = kept_rows[...]
-                outs[i][rows:] = sent_at[:split_at]
-                outs[1 - i][: rows - split_at] = sent_at[split_at:]
-                outs[1 - i][rows - split_at :] = sep_at[: half + split_at - rows]
-
-        outs[2][...] = sep_at[half + split_at - rows :]
-
-
-def ends_kernel(where, weight, gram, square, sep, inv_n, leaf_n, inv_l, keep, send, rest_at):
+                outs[i][:rows] = sent_at[...]
+                outs[i][rows:] = sep_at[:head]
+                outs[1 - i][...] = sep_at[head:]
+
+
+def ends_kernel(where, weight, gram, square, inv_n, leaf_n, inv_l, keep, send, rest_at):
     poles, w1, w2 = leaf_n.shape
     width = w1 // 2
-    start = sep.shape[0]
-    rest_at[:start] = sep[...]
     for p in range(poles):
         ns = split(leaf_n[p])
         middle = gram[p, w1:].T - dot3(split(inv_n[p] + gram[p, :w1]), ns)
@@ -294,9 +285,9 @@
         lower = jnp.concatenate([lower[: w2 // 2], lower[w2 // 2 :]], axis=1)
         value = weight[p] * jnp.concatenate([middle, lower], axis=0)
         if p == 0:
-            rest_at[start:] = value
+            rest_at[...] = value
         else:
-            rest_at[start:] += value
+            rest_at[...] += value
     head = keep.shape[0]
     for i, (a, b) in enumerate([(keep, send), (send, keep)]):
 
@@ -306,17 +297,12 @@
             b[...] = rest_at[head:]
 
 
-def ends_call(where, weight, gram, square, sep, inv_n, leaf_n, inv_l):
+def ends_call(where, weight, gram, square, inv_n, leaf_n, inv_l):
     w1, w2 = leaf_n.shape[1:]
-    rows = sep.shape[0] + (w1 + w2) // 2
+    rows = (w1 + w2) // 2
     outs = [pltpu.VMEM((rows // 2, w1), jnp.float32)] * 2
-    args = [where, weight, gram, square, sep, inv_n, leaf_n, inv_l]
+    args = [where, weight, gram, square, inv_n, leaf_n, inv_l]
     return call(ends_kernel, "ends", outs, args, 2, scratch_shapes=[pltpu.VMEM((rows, w1), jnp.float32)])
-
-
-def halved(rows, w1, w2):
-    quarter = (2 * rows + w1 + w2 // 2) // 4
-    return (quarter + 0, quarter - 0), (112, rows - 112)
 
 
 def unit_call(form, tables, where, weight, shards, factors, sums=(), ends=()):
@@ -324,14 +310,13 @@
     lanes, w2 = factors[0].shape[2], factors[2].shape[2]
     w1 = lanes - w2
     f32 = jnp.float32
-    head = halved(rows, w1, w2)[0][0]
     gram = [pltpu.VMEM((poles, lanes, w1), f32), pltpu.VMEM((poles, w2, w2), f32)]
     outs = {
         "first": [pltpu.VMEM((2 * rows, w1), f32)] + gram,
         "next": [pltpu.VMEM((2 * rows, w1), f32)] + gram,
         "halves": [pltpu.VMEM((rows, w1), f32)] * 2 + gram,
-        "part": [pltpu.VMEM((rows, w1), f32)] + [pltpu.VMEM((poles, rows, lanes), jnp.bfloat16)] * 2,
-        "last": [pltpu.VMEM((n, w1), f32) for n in (head, head, 2 * rows + w1 // 2 - 2 * head)] + gram,
+        "part": [pltpu.VMEM((rows // 2, w1), f32)] * 2 + [pltpu.VMEM((poles, rows, lanes), jnp.bfloat16)] * 2,
+        "last": [pltpu.VMEM(((rows + w1 // 2) // 2, w1), f32)] * 2 + gram,
     }[form]
     cuts = [len(pieces) for pieces in shards]
     args = [where, weight, *(x for pieces in shards for x in pieces), *factors, *sums, *ends]
@@ -341,7 +326,7 @@
     if form == "last":
         options["scratch_shapes"] += [pltpu.VMEM((rows, w1), f32), pltpu.VMEM((w1 // 2, w1), f32)]
         at = len(args) - len(ends) - 2
-        options["input_output_aliases"] = {at: 3, at + 1: 4}
+        options["input_output_aliases"] = {at: 2, at + 1: 3}
     if form in ("next", "halves"):
         at = 2 if form == "halves" else 1
         options["input_output_aliases"] = {len(args) - 2: at, len(args) - 1: at + 1}
@@ -368,83 +353,83 @@
     return call(functools.partial(place_kernel, unit, owners, pieces), "place", outs, [where, *sums], 1)
 
 
-def finish_kernel(unit, halves, shares, part, table, owners, where, *refs):
-    rows, half = unit // 2, halves[0]
-    first, refs = refs[:2], refs[2:]
-    if part:
-        second, refs = refs[:2], refs[2:]
-    (_, _, off, upper), refs = refs[:4], refs[4:]
-    if part:
-        (sep, middle, lower), refs = refs[:3], refs[3:]
-    off_at, upper_at, sem = refs
-    width = off.shape[1]
-    base, way = (pick(t, where[1]) for t in table)
-    before = pick(owners, where[1]) * unit
-    places, start = [], 0
-    for i, (a, b) in enumerate([first, first[::-1]]):
-
-        @pl.when(where[2] == i)
-        def _():
-            if part == 0:
-                for at, value in [(0, a[:half]), (half, b[: unit - half])]:
-                    off_at[at : at + value.shape[0]] = value[:, :width]
-                    upper_at[at : at + value.shape[0]] = value[:, width:]
-                return
-            c, d = second if i == 0 else second[::-1]
-            w1, w2 = middle.shape
-            rest = 2 * half - unit
-            sep[:rest] = b[unit - half : half]
-            sep[rest:] = c[: width - rest]
-            end = halves[1]
-            at = end - (width - rest)
-            middle[:at] = c[width - rest : end, :w2]
-            middle[width : width + at] = c[width - rest : end, w2:]
-            middle[at:width] = d[: width - at, :w2]
-            middle[width + at :] = d[: width - at, w2:]
-            lower[: w2 // 2] = d[width - at : end, :w2]
-            lower[w2 // 2 :] = d[width - at : end, w2:]
-
-    if part == 0:
-        places = [(i * rows, base * unit + jnp.where(way == i, 0, rows), rows) for i in range(2)]
-        start = unit
-    for i, ref in enumerate(second if part else first):
-        size = shares[part]
-        value = ref[halves[part] :]
-        off_at[start : start + size] = value[:, :width]
-        upper_at[start : start + size] = value[:, width:]
-        places.append((start, before + jnp.where(where[2] == i, 0, rows) + part * shares[0], size))
-        start += size
-    copies = []
-    for at, place, size in places:
-        there = pl.ds(pl.multiple_of(place, 8), size)
-        for value, out in [(off_at, off), (upper_at, upper)]:
-            copies.append(pltpu.make_async_copy(value.at[pl.ds(at, size)], out.at[there], sem.at[len(copies)]))
+def send_out(copies, sem):
+    copies = [pltpu.make_async_copy(a, b, sem.at[i]) for i, (a, b) in enumerate(copies)]
     for copy in copies:
         copy.start()
     for copy in copies:
         copy.wait()
 
 
-def finish(part, table, owners, where, sums, off, upper, unit, halves, shares, shapes=()):
+def rows_kernel(unit, table, owners, where, kept, got, _off, _upper, off, upper, sep, sem):
+    rows = unit // 2
+    width = off.shape[1]
+    base, way = (pick(t, where[1]) for t in table)
+    last, before = base * unit, pick(owners, where[1]) * unit
+    second_at = last + jnp.where(way == 1, 0, rows)
+    head = kept.shape[0] - rows
+    for i, halves in enumerate([(kept, got), (got, kept)]):
+
+        @pl.when(where[2] == i)
+        def _():
+            moves = [(halves[0], 0, rows, second_at)]
+            for j, half in enumerate(halves):
+                moves.append((half, head, rows, before + j * rows))
+            copies = []
+            for half, start, size, place in moves:
+                there = pl.ds(pl.multiple_of(place, rows), size)
+                for k, out in enumerate([off, upper]):
+                    copies.append((half.at[pl.ds(start, size), pl.ds(k * width, width)], out.at[there]))
+            rest = head - rows
+            copies.append((halves[0].at[pl.ds(rows, rest)], sep.at[pl.ds(0, rest)]))
+            copies.append((halves[1].at[pl.ds(0, head)], sep.at[pl.ds(rest, head)]))
+            send_out(copies, sem)
+
+
+def leaf_kernel(unit, table, flip, where, half, *refs):
+    off, upper, middle, lower, sem = refs[-5:]
+    w1, w2 = middle.shape
+    width, rows = w1 // 2, unit // 4
+    size = half.shape[0] - rows
+    rest = width - size
+    base, way = (pick(t, where[1]) for t in table)
+    index = where[2] if flip == 0 else 1 - where[2]
+    there = base * unit + jnp.where(way == 0, 0, 2 * rows) + index * rows
+    there = pl.ds(pl.multiple_of(there, rows), rows)
+
+    def lanes(start, n, k):
+        return half.at[pl.ds(start, n), pl.ds(k * w2, w2)]
+
+    shared = [
+        (half.at[pl.ds(size, rows), pl.ds(k * out.shape[1], out.shape[1])], out.at[there])
+        for k, out in enumerate([off, upper])
+    ]
+
+    @pl.when(index == 0)
+    def _():
+        send_out(shared + [(lanes(0, size, k), middle.at[pl.ds(k * width, size)]) for k in range(2)], sem)
+
+    @pl.when(index == 1)
+    def _():
+        copies = [(lanes(0, rest, k), middle.at[pl.ds(k * width + size, rest)]) for k in range(2)]
+        n = w2 // 2
+        copies += [(lanes(rest, n, k), lower.at[pl.ds(k * n, n)]) for k in range(2)]
+        send_out(shared + copies, sem)
+
+
+def place_out(kernel, name, where, sums, into, shapes, copies):
     anywhere = pl.BlockSpec(memory_space=pl.ANY)
-    rows = 2 * shares[part] + (0 if part else unit)
-    outs = [off.shape, upper.shape, *shapes]
-    at = 1 + len(sums)
     return pl.pallas_call(
-        functools.partial(finish_kernel, unit, halves, shares, part, table, owners),
-        in_specs=[SMEM] + [VMEM] * len(sums) + [anywhere] * 2,
-        out_specs=[anywhere] * 2 + [VMEM] * len(shapes),
-        out_shape=[jax.ShapeDtypeStruct(shape, jnp.float32) for shape in outs],
-        scratch_shapes=[
-            pltpu.VMEM((rows, off.shape[1]), jnp.float32),
-            pltpu.VMEM((rows, upper.shape[1]), jnp.float32),
-            pltpu.SemaphoreType.DMA((4 if part else 8,)),
-        ],
-        input_output_aliases={at: 0, at + 1: 1},
+        kernel,
+        in_specs=[SMEM] + [VMEM] * len(sums) + [anywhere] * len(into),
+        out_specs=[anywhere] * (len(into) + len(shapes)),
+        out_shape=[jax.ShapeDtypeStruct(s, jnp.float32) for s in [x.shape for x in into] + list(shapes)],
+        scratch_shapes=[pltpu.SemaphoreType.DMA((copies,))],
+        input_output_aliases={1 + len(sums) + i: i for i in range(len(into))},
         compiler_params=pltpu.CompilerParams(vmem_limit_bytes=20 * MIB),
         cost_estimate=pl.CostEstimate(flops=1, bytes_accessed=1, transcendentals=0),
-        name="finish",
-    )(where, *sums, off, upper)
+        name=name,
+    )(where, *sums, *into)
 
 
 def line_plan(n):
@@ -551,45 +536,49 @@
     swap((2, 0))
     advance(3, 0)
     (first,) = hold([], first)
+    value = cut(first, unit)
+    second = (value, step(value, 0))
     hold([(1, 1)])
     rows, *sums = unit_of("next", 1, (0, 1), factors, sums)
+    rows, sums, second = hold([], rows, sums, second)
     rows, sums = hold([(2, 1)], rows, sums)
-    value = jnp.concatenate([rows, cut(first, unit)], axis=0)
     swap((2, 1))
-    second = (value, step(value, 0))
+    third = (rows, step(rows, 1))
     advance(3, 1)
     hold([(2, 0)])
 
     hold([(3, 0)])
     swap((3, 0), 2)
+    (third,) = hold([], third)
+    value = third[0] + third[1]
+    fourth = (value, step(value, 0))
     hold([(2, 1)])
     keep3, send3, *sums = unit_of("halves", 2, (0, 1), factors, sums)
-    keep3, send3, sums, second = hold([], keep3, send3, sums, second)
-    value = jnp.concatenate([cut(second, unit), send3], axis=0)
-    third = (value, step(value, 1))
+    keep3, send3, sums, fourth = hold([], keep3, send3, sums, fourth)
 
     hold([(3, 0)])
     kept = unit_of("part", 3, (0,), factors)
-    (kept,) = hold([(3, 1)], kept)
+    kept, keep3, send3 = hold([(3, 1)], kept, keep3, send3)
     swap((3, 1))
+    keep4, send4, *kept = kept
+    got3 = step(jnp.concatenate([send3, send4], axis=0), 1)
     hold([(3, 1)])
     inv_n = node_inverse[:, 0]
-    keep, send, rest, *sums = unit_of("last", 3, (1,), factors, sums, (*kept, inv_n))
-    keep, send, rest, sums = hold([], keep, send, rest, sums)
+    keep, send, *sums = unit_of("last", 3, (1,), factors, sums, (*kept, inv_n))
+    keep, send, sums, (keep3, keep4), got3 = hold([], keep, send, sums, (keep3, keep4), got3)
     got = step(send, 1)
-    keep2, send2 = ends_call(where, token, *sums, rest, inv_n, leaf_node_factor[:, 0], leaf_inverse[:, 0])
-    keep2, send2, keep3, third = hold([], keep2, send2, keep3, third)
+    keep2, send2 = ends_call(where, token, *sums, inv_n, leaf_node_factor[:, 0], leaf_inverse[:, 0])
+    keep2, send2 = hold([], keep2, send2)
     got2 = step(send2, 1)
-    keep3 = keep3 + third[1][unit:]
-    halves, shares = halved(own_rows, w1, w2)
+    keep3 = keep3 + got3[:own_rows]
     keep, got = hold([], keep, got)
-    keep = jnp.concatenate([keep + got, keep3[: shares[0]]], axis=0)
+    keep = jnp.concatenate([keep + got, keep3], axis=0)
     got = step(keep, 0)
     keep2, got2 = hold([], keep2, got2)
-    keep2 = jnp.concatenate([keep2 + got2, keep3[shares[0] :]], axis=0)
+    keep2 = jnp.concatenate([keep2 + got2, keep4 + got3[own_rows:]], axis=0)
     got2 = step(keep2, 0)
-    pieces = [(0, unit, own_rows, None, 0), (0, unit + own_rows, own_rows, None, w1), (1, unit, unit, 0, 0), (2, 0, unit, 1, 0)]
-    early = [v for pair in (first, second, third) for v in pair]
+    pieces = [(0, unit, own_rows, None, 0), (0, unit + own_rows, own_rows, None, w1), (1, 0, unit, 0, 0), (2, 0, unit, 1, 0)]
+    early = [v for pair in (first, second, fourth) for v in pair]
     root, off, upper = place(owners, pieces, where, early, unit, w0, w2)
     keep, got, root, off, upper = hold([], keep, got, root, off, upper)
     keep = keep + got
@@ -597,11 +586,15 @@
     keep2, got2 = hold([], keep2, got2)
     keep2 = keep2 + got2
     got2 = step(keep2, 1)
-    keep, got = hold([], keep, got)
-    places = (tables[3][::2], owners[2], where)
-    off, upper = finish(0, *places, (keep, got), off, upper, unit, halves, shares)
-    shapes = [(w1 // 2, w1), (w1, w2), (w2, w2)]
-    off, upper, sep, middle, lower = finish(1, *places, (keep, got, keep2, got2), off, upper, unit, halves, shares, shapes)
+    (keep2,) = hold([], keep2)
+    blocks = [(w1, w2), (w2, w2)]
+    kernels = [functools.partial(leaf_kernel, unit, tables[3][::2], flip) for flip in range(2)]
+    off, upper, middle, lower = place_out(kernels[0], "leaf", where, [keep2], [off, upper], blocks, 6)
+    keep, got, off, upper, middle, lower = hold([], keep, got, off, upper, middle, lower)
+    kernel = functools.partial(rows_kernel, unit, tables[3][::2], owners[2])
+    off, upper, sep = place_out(kernel, "rows", where, [keep, got], [off, upper], [(w1 // 2, w1)], 8)
+    off, upper, sep, got2 = hold([], off, upper, sep, got2)
+    off, upper, middle, lower = place_out(kernels[1], "leaf", where, [got2], [off, upper, middle, lower], [], 6)
     return root, off[None], sep[None], upper[None], middle[None], lower[None]
 
 

time: 125 us -> 124 us (level)
  starting transfers between devices: 31.1 us -> 29.1 us
    ppermute x10 -> x12, waiting for transfers between devices: 23.4 us -> 29.9 us  [step(): return lax.ppermute(value, ('pole', 'col'), pairs)]
    ppermute x6, waiting for transfers between devices: 21.8 us -> 15.9 us  [advance(): moved[slot, i] = lax.ppermute(moved[slot - 1, i], ('row', 'col'), down + up)]
    ppermute x10 -> x12, starting transfers between devices: 20.2 us -> 18 us  [step(): return lax.ppermute(value, ('pole', 'col'), pairs)]
    pallas_call x2 -> x3, Pallas kernels: 3.95 us -> 4.45 us  [place_out(): pl.pallas_call(kernel, in_specs=[SMEM] + [VMEM] * len(sums) + [anywhere]...]
  transfers between devices with their start and end apart: 25 -> 27, of which waited for: 14 -> 14; matrix products, arithmetic and copies ran while one was open for 1% -> 1% of each run, Pallas kernels for 31% -> 32%
where the time goes in v4:
time: 124 us
  waiting for transfers between devices  50.7 us (41%)
  Pallas kernels  41.4 us (33%)
  starting transfers between devices  29.1 us (23%)
    ppermute x12, waiting for transfers between devices, step(): return lax.ppermute(value, ('pole', 'col'), pairs)  29.9 us
    pallas_call x7, Pallas kernels, call(): pl.pallas_call(kernel, in_specs=[SMEM] * smem + [VMEM] * (len(args) - sme...  29.3 us
    ppermute x12, starting transfers between devices, step(): return lax.ppermute(value, ('pole', 'col'), pairs)  18 us
    ppermute x6, waiting for transfers between devices, advance(): moved[slot, i] = lax.ppermute(moved[slot - 1, i], ('row', 'col'), down + up)  15.9 us
    pallas_call x1, Pallas kernels, prepare(): pl.pallas_call(prepare_kernel, in_specs=[SMEM] * 2 + [VMEM] + [pl.BlockSp...  7.69 us
    ppermute x6, starting transfers between devices, advance(): moved[slot, i] = lax.ppermute(moved[slot - 1, i], ('row', 'col'), down + up)  7.68 us
    ppermute x8, waiting for transfers between devices, swap(): other[key] = tuple((lax.ppermute(piece, 'col', SWAP) for piece in pieces))  4.85 us
    pallas_call x3, Pallas kernels, place_out(): pl.pallas_call(kernel, in_specs=[SMEM] + [VMEM] * len(sums) + [anywhere]...  4.45 us
  transfers between devices with their start and end apart: 27, of which 14 were waited for; matrix products, arithmetic and copies ran while one was open for 1% of the time, Pallas kernels for 32%

profile of v4, /device:TPU:0, one launch (start us, length us, event | category | flops | bytes accessed | tf_op | source)
XLA Modules:
  0.0 124.2 jit_solution(5041858425976370782)
XLA Ops:
  2.5 4.2 %collective-permute-done.refs_1_ = f32[2,128,1024]{2,1,0:T(8,128)} collective-permute-done((f32[2,128,1024]{2,1,0:T(8,128)}, f32[2,128,1024]{2,1,0:T(8,128)}, u32[]{:S(2)}, u32[]{:S(2)}) %collective-permute-start) | collective-permute-done | bytes 1048608 | tf_op jit(solution)/shard_map/ppermute | solution.py:484
  8.7 7.7 %prepare.1 = (bf16[2,1024,768]{2,1,0:T(8,128)(2,1)S(1)}, bf16[2,1024,768]{2,1,0:T(8,128)(2,1)S(1)}, bf16[2,1024,256]{2,1,0:T(8,128)(2,1)S(1)}, bf16[2,1024,256]{2,1,0:T(8,128)(2,1)S(1)}) custom-call(s32[3]{0:T(128)S(1)} %pad_add_fusion.where, s32[1,8]{1,0:T(1,128)S(1)} %copy-done.5, f32[2,1024,256]{2,1,0:T(8,128)S(1)} %collective-permute-done.3.f_other, ...), custom_call_target="tpu_custom_call" | custom-call | flops 1 | bytes 1 | tf_op jit(solution)/shard_map/prepare/pallas_call | solution.py:154
  16.7 2.6 %collective-permute-start.8 = (f32[256,512]{1,0:T(8,128)S(1)}, f32[256,512]{1,0:T(8,128)S(1)}, u32[]{:S(2)}, u32[]{:S(2)}) collective-permute-start(f32[256,512]{1,0:T(8,128)S(1)} %pad_maximum_fusion.2), channel_id=1, source_target_pairs={{0,8},{1,17},{8,0},{9,25},{16,24},{17,1},{24,16},{25,9},{2,10},{3,... | collective-permute-start | bytes 1572872 | tf_op jit(solution)/shard_map/ppermute | solution.py:499
  19.4 2.1 %collective-permute-start.7 = (f32[2,128,1024]{2,1,0:T(8,128)S(1)}, f32[2,128,1024]{2,1,0:T(8,128)S(1)}, u32[]{:S(2)}, u32[]{:S(2)}) collective-permute-start(f32[2,128,1024]{2,1,0:T(8,128)S(1)} %collective-permute-done.2.refs_0_), channel_id=1, source_target_pairs={{0,1},{1,0},{2,3},{3,2},{4,5},{5,4},{6,7},{7,6},{8,9},{9,8},{10,11... | collective-permute-start | bytes 3145736 | tf_op jit(solution)/shard_map/ppermute | solution.py:484
  22.7 5.6 %first.1 = (f32[256,512]{1,0:T(8,128)S(1)}, f32[2,768,512]{2,1,0:T(8,128)S(1)}, f32[2,256,256]{2,1,0:T(8,128)S(1)}) custom-call(s32[3]{0:T(128)S(1)} %pad_add_fusion.where, f32[2]{0:T(128)S(1)} %copy-done.4, f32[2,128,1024]{2,1,0:T(8,128)S(1)} %copy-done.2, f32[2,128,1024]{2,1,0:T(8,128)} %collective-permute-done.refs_1_, ...), custom_call_target="tpu_custom_call" | custom-call | flops 1 | bytes 1 | tf_op jit(solution)/shard_map/first/pallas_call | solution.py:70
  28.4 2.0 %collective-permute-done.1.refs_1_ = f32[2,128,1024]{2,1,0:T(8,128)S(1)} collective-permute-done((f32[2,128,1024]{2,1,0:T(8,128)}, f32[2,128,1024]{2,1,0:T(8,128)S(1)}, u32[]{:S(2)}, u32[]{:S(2)}) %collective-permute-start.1) | collective-permute-done | bytes 1048608 | tf_op jit(solution)/shard_map/ppermute | solution.py:479
  30.5 2.0 %collective-permute-start.9 = (f32[512,512]{1,0:T(8,128)S(1)}, f32[512,512]{1,0:T(8,128)S(1)}, u32[]{:S(2)}, u32[]{:S(2)}) collective-permute-start(f32[512,512]{1,0:T(8,128)S(1)} %pad_maximum_fusion.refs_0_), channel_id=1, source_target_pairs={{0,16},{1,9},{8,24},{9,1},{16,0},{17,25},{24,8},{25,17},{2,18},{3,... | collective-permute-start | bytes 3145736 | tf_op jit(solution)/shard_map/ppermute | solution.py:499
  33.8 7.7 %collective-permute-done.6.refs_4_.refs_0_ = f32[2,128,1024]{2,1,0:T(8,128)S(1)} collective-permute-done((f32[2,128,1024]{2,1,0:T(8,128)S(1)}, f32[2,128,1024]{2,1,0:T(8,128)S(1)}, u32[]{:S(2)}, u32[]{:S(2)}) %collective-permute-start.6) | collective-permute-done | bytes 1048608 | tf_op jit(solution)/shard_map/ppermute | solution.py:479
  41.6 3.8 %collective-permute-done.9.refs_1_ = f32[512,512]{1,0:T(8,128)S(1)} collective-permute-done((f32[512,512]{1,0:T(8,128)S(1)}, f32[512,512]{1,0:T(8,128)S(1)}, u32[]{:S(2)}, u32[]{:S(2)}) %collective-permute-start.9) | collective-permute-done | bytes 1048608 | tf_op jit(solution)/shard_map/ppermute | solution.py:499
  45.5 2.0 %collective-permute-start.10 = (f32[256,512]{1,0:T(8,128)S(1)}, f32[256,512]{1,0:T(8,128)S(1)}, u32[]{:S(2)}, u32[]{:S(2)}) collective-permute-start(f32[256,512]{1,0:T(8,128)S(1)} %slice_add_fusion.refs_2_), channel_id=1, source_target_pairs={{0,8},{1,17},{8,0},{9,25},{16,24},{17,1},{24,16},{25,9},{2,10},{3,... | collective-permute-start | bytes 1572872 | tf_op jit(solution)/shard_map/ppermute | solution.py:499
  48.8 5.6 %next.1 = (f32[256,512]{1,0:T(8,128)S(1)}, f32[2,768,512]{2,1,0:T(8,128)S(1)}, f32[2,256,256]{2,1,0:T(8,128)S(1)}) custom-call(s32[3]{0:T(128)S(1)} %pad_add_fusion.where, f32[2]{0:T(128)S(1)} %copy-done.4, f32[2,128,1024]{2,1,0:T(8,128)S(1)} %collective-permute-done.2.refs_0_, ...), custom_call_target="tpu_custom_call", output_to_operand_aliasing={{1}: (10, {}), {2}: (11, {})} | custom-call | flops 1 | bytes 1 | tf_op jit(solution)/shard_map/next/pallas_call | solution.py:70
  54.7 2.0 %collective-permute-start.17 = (f32[256,512]{1,0:T(8,128)S(1)}, f32[256,512]{1,0:T(8,128)S(1)}, u32[]{:S(2)}, u32[]{:S(2)}) collective-permute-start(f32[256,512]{1,0:T(8,128)S(1)} %get-tuple-element.211), channel_id=1, source_target_pairs={{0,16},{1,9},{8,24},{9,1},{16,0},{17,25},{24,8},{25,17},{2,18},{3,... | collective-permute-start | bytes 1572872 | tf_op jit(solution)/shard_map/ppermute | solution.py:499
  58.0 6.2 %collective-permute-done.12.refs_2_ = f32[2,128,1024]{2,1,0:T(8,128)S(1)} collective-permute-done((f32[2,128,1024]{2,1,0:T(8,128)S(1)}, f32[2,128,1024]{2,1,0:T(8,128)S(1)}, u32[]{:S(2)}, u32[]{:S(2)}) %collective-permute-start.12) | collective-permute-done | bytes 1048608 | tf_op jit(solution)/shard_map/ppermute | solution.py:479
  64.2 1.9 %collective-permute-start.18 = (f32[256,512]{1,0:T(8,128)S(1)}, f32[256,512]{1,0:T(8,128)S(1)}, u32[]{:S(2)}, u32[]{:S(2)}) collective-permute-start(f32[256,512]{1,0:T(8,128)S(1)} %add.30.refs_4_), channel_id=1, source_target_pairs={{0,8},{1,17},{8,0},{9,25},{16,24},{17,1},{24,16},{25,9},{2,10},{3,... | collective-permute-start | bytes 1572872 | tf_op jit(solution)/shard_map/ppermute | solution.py:499
  66.8 5.5 %halves.1 = (f32[128,512]{1,0:T(8,128)S(1)}, f32[128,512]{1,0:T(8,128)S(1)}, f32[2,768,512]{2,1,0:T(8,128)S(1)}, f32[2,256,256]{2,1,0:T(8,128)S(1)}) custom-call(s32[3]{0:T(128)S(1)} %pad_add_fusion.where, f32[2]{0:T(128)S(1)} %copy-done.4, f32[2,128,1024]{2,1,0:T(8,128)S(1)} %collective-permute-done.2.refs_0_, ...), custom_call_target="tpu_custom_call", output_to_operand_aliasing={{2}: (14, {}), {3}: (15, {})} | custom-call | flops 1 | bytes 1 | tf_op jit(solution)/shard_map/halves/pallas_call | solution.py:70
  73.5 2.5 %part.1 = (f32[64,512]{1,0:T(8,128)S(1)}, f32[64,512]{1,0:T(8,128)S(1)}, bf16[2,128,768]{2,1,0:T(8,128)(2,1)S(1)}, bf16[2,128,768]{2,1,0:T(8,128)(2,1)S(1)}) custom-call(s32[3]{0:T(128)S(1)} %pad_add_fusion.where, f32[2]{0:T(128)S(1)} %copy-done.4, f32[2,128,1024]{2,1,0:T(8,128)S(1)} %collective-permute-done.6.refs_4_.refs_0_, ...), custom_call_target="tpu_custom_call" | custom-call | flops 1 | bytes 1 | tf_op jit(solution)/shard_map/part/pallas_call | solution.py:70
  76.1 1.9 %collective-permute-start.20 = (f32[192,512]{1,0:T(8,128)S(1)}, f32[192,512]{1,0:T(8,128)S(1)}, u32[]{:S(2)}, u32[]{:S(2)}) collective-permute-start(f32[192,512]{1,0:T(8,128)S(1)} %pad_maximum_fusion.4), channel_id=1, source_target_pairs={{0,16},{1,9},{8,24},{9,1},{16,0},{17,25},{24,8},{25,17},{2,18},{3,... | collective-permute-start | bytes 1179656 | tf_op jit(solution)/shard_map/ppermute | solution.py:499
  78.8 4.5 %last.1 = (f32[192,512]{1,0:T(8,128)S(1)}, f32[192,512]{1,0:T(8,128)S(1)}, f32[2,768,512]{2,1,0:T(8,128)S(1)}, f32[2,256,256]{2,1,0:T(8,128)S(1)}) custom-call(s32[3]{0:T(128)S(1)} %pad_add_fusion.where, f32[2]{0:T(128)S(1)} %copy-done.4, f32[2,128,1024]{2,1,0:T(8,128)S(1)} %collective-permute-done.4.refs_5_.refs_0_, ...), custom_call_target="tpu_custom_call", output_to_operand_aliasing={{2}: (10, {}), {3}: (11, {})} | custom-call | flops 1 | bytes 1 | tf_op jit(solution)/shard_map/last/pallas_call | solution.py:70
  85.9 3.3 %ends.1 = (f32[192,512]{1,0:T(8,128)S(1)}, f32[192,512]{1,0:T(8,128)S(1)}) custom-call(s32[3]{0:T(128)S(1)} %pad_add_fusion.where, f32[2]{0:T(128)S(1)} %copy-done.4, f32[2,768,512]{2,1,0:T(8,128)S(1)} %get-tuple-element.258.gram, f32[2,256,256]{2,1,0:T(8,128)S(1)} %get-tuple-element.259.square, f32[2,512,512]{2,1,0:T(8,128)S(1)} %bitcast.14, ...), custom_call_target="tpu_custom_call" | custom-call | flops 1 | bytes 1 | tf_op jit(solution)/shard_map/ends/pallas_call | solution.py:70
  89.4 2.3 %collective-permute-done.21 = f32[192,512]{1,0:T(8,128)S(1)} collective-permute-done((f32[192,512]{1,0:T(8,128)S(1)}, f32[192,512]{1,0:T(8,128)S(1)}, u32[]{:S(2)}, u32[]{:S(2)}) %collective-permute-start.21) | collective-permute-done | bytes 393248 | tf_op jit(solution)/shard_map/ppermute | solution.py:499
  93.8 6.8 %collective-permute-done.24 = f32[192,512]{1,0:T(8,128)S(1)} collective-permute-done((f32[192,512]{1,0:T(8,128)S(1)}, f32[192,512]{1,0:T(8,128)S(1)}, u32[]{:S(2)}, u32[]{:S(2)}) %collective-permute-start.24) | collective-permute-done | bytes 393248 | tf_op jit(solution)/shard_map/ppermute | solution.py:499
  102.1 2.2 %place.1 = (f32[128,1024]{1,0:T(8,128)}, f32[1024,256]{1,0:T(8,128)}, f32[1024,256]{1,0:T(8,128)}) custom-call(s32[3]{0:T(128)S(1)} %pad_add_fusion.where, f32[512,512]{1,0:T(8,128)S(1)} %pad_maximum_fusion.refs_0_, f32[512,512]{1,0:T(8,128)S(1)} %collective-permute-done.9.refs_1_, f32[256,512]{1,0:T(8,128)S(1)} %slice_add_fusion.refs_2_, ...), custom_call_target="tpu_custom_call" | custom-call | flops 1 | bytes 1 | tf_op jit(solution)/shard_map/place/pallas_call | solution.py:70
  104.6 8.7 %collective-permute-done.25 = f32[256,512]{1,0:T(8,128)S(1)} collective-permute-done((f32[256,512]{1,0:T(8,128)S(1)}, f32[256,512]{1,0:T(8,128)S(1)}, u32[]{:S(2)}, u32[]{:S(2)}) %collective-permute-start.25) | collective-permute-done | bytes 524320 | tf_op jit(solution)/shard_map/ppermute | solution.py:499
  118.3 4.3 %collective-permute-done.26.half = f32[256,512]{1,0:T(8,128)S(1)} collective-permute-done((f32[256,512]{1,0:T(8,128)S(1)}, f32[256,512]{1,0:T(8,128)S(1)}, u32[]{:S(2)}, u32[]{:S(2)}) %collective-permute-start.26) | collective-permute-done | bytes 524320 | tf_op jit(solution)/shard_map/ppermute | solution.py:499
  (71 shorter events, 25.6 us)
Async XLA Ops:
  0.6 7.4 %collective-permute-start.3 = (f32[2,1024,256]{2,1,0:T(8,128)}, f32[2,1024,256]{2,1,0:T(8,128)S(1)}, u32[]{:S(2)}, u32[]{:S(2)}) collective-permute-start(f32[2,1024,256]{2,1,0:T(8,128)} %bitcast.20), channel_id=1, source_target_pairs={{0,1},{1,0},{2,3},{3,2},{4,5},{5,4},{6,7},{7,6},{8,9},{9,8},{10,11... | collective-permute-start | bytes 6291464 | tf_op jit(solution)/shard_map/ppermute | solution.py:511
  1.2 18.1 %collective-permute-start.2 = (f32[2,128,1024]{2,1,0:T(8,128)}, f32[2,128,1024]{2,1,0:T(8,128)S(1)}, u32[]{:S(2)}, u32[]{:S(2)}) collective-permute-start(f32[2,128,1024]{2,1,0:T(8,128)} %refs_0_.1), channel_id=1, source_target_pairs={{2,0},{4,2},{6,4},{1,3},{3,5},{5,7},{10,8},{12,10},{14,12},{9,11},... | collective-permute-start | bytes 3145736 | tf_op jit(solution)/shard_map/ppermute | solution.py:479
  6.7 23.6 %collective-permute-start.1 = (f32[2,128,1024]{2,1,0:T(8,128)}, f32[2,128,1024]{2,1,0:T(8,128)S(1)}, u32[]{:S(2)}, u32[]{:S(2)}) collective-permute-start(f32[2,128,1024]{2,1,0:T(8,128)} %collective-permute-done.refs_1_), channel_id=1, source_target_pairs={{2,0},{4,2},{6,4},{1,3},{3,5},{5,7},{10,8},{12,10},{14,12},{9,11},... | collective-permute-start | bytes 3145736 | tf_op jit(solution)/shard_map/ppermute | solution.py:479
  16.7 13.6 %collective-permute-start.8 = (f32[256,512]{1,0:T(8,128)S(1)}, f32[256,512]{1,0:T(8,128)S(1)}, u32[]{:S(2)}, u32[]{:S(2)}) collective-permute-start(f32[256,512]{1,0:T(8,128)S(1)} %pad_maximum_fusion.2), channel_id=1, source_target_pairs={{0,8},{1,17},{8,0},{9,25},{16,24},{17,1},{24,16},{25,9},{2,10},{3,... | collective-permute-start | bytes 1572872 | tf_op jit(solution)/shard_map/ppermute | solution.py:499
  19.4 14.5 %collective-permute-start.7 = (f32[2,128,1024]{2,1,0:T(8,128)S(1)}, f32[2,128,1024]{2,1,0:T(8,128)S(1)}, u32[]{:S(2)}, u32[]{:S(2)}) collective-permute-start(f32[2,128,1024]{2,1,0:T(8,128)S(1)} %collective-permute-done.2.refs_0_), channel_id=1, source_target_pairs={{0,1},{1,0},{2,3},{3,2},{4,5},{5,4},{6,7},{7,6},{8,9},{9,8},{10,11... | collective-permute-start | bytes 3145736 | tf_op jit(solution)/shard_map/ppermute | solution.py:484
  21.4 20.1 %collective-permute-start.6 = (f32[2,128,1024]{2,1,0:T(8,128)S(1)}, f32[2,128,1024]{2,1,0:T(8,128)S(1)}, u32[]{:S(2)}, u32[]{:S(2)}) collective-permute-start(f32[2,128,1024]{2,1,0:T(8,128)S(1)} %collective-permute-done.2.refs_0_), channel_id=1, source_target_pairs={{2,0},{4,2},{3,5},{5,7},{10,8},{12,10},{11,13},{13,15},{18,16},{20... | collective-permute-start | bytes 3145736 | tf_op jit(solution)/shard_map/ppermute | solution.py:479
  30.5 14.9 %collective-permute-start.9 = (f32[512,512]{1,0:T(8,128)S(1)}, f32[512,512]{1,0:T(8,128)S(1)}, u32[]{:S(2)}, u32[]{:S(2)}) collective-permute-start(f32[512,512]{1,0:T(8,128)S(1)} %pad_maximum_fusion.refs_0_), channel_id=1, source_target_pairs={{0,16},{1,9},{8,24},{9,1},{16,0},{17,25},{24,8},{25,17},{2,18},{3,... | collective-permute-start | bytes 3145736 | tf_op jit(solution)/shard_map/ppermute | solution.py:499
  32.5 16.2 %collective-permute-start.5 = (f32[2,128,1024]{2,1,0:T(8,128)S(1)}, f32[2,128,1024]{2,1,0:T(8,128)S(1)}, u32[]{:S(2)}, u32[]{:S(2)}) collective-permute-start(f32[2,128,1024]{2,1,0:T(8,128)S(1)} %collective-permute-done.1.refs_1_), channel_id=1, source_target_pairs={{0,1},{1,0},{2,3},{3,2},{4,5},{5,4},{6,7},{7,6},{8,9},{9,8},{10,11... | collective-permute-start | bytes 3145736 | tf_op jit(solution)/shard_map/ppermute | solution.py:484
  32.5 22.2 %collective-permute-start.4 = (f32[2,128,1024]{2,1,0:T(8,128)S(1)}, f32[2,128,1024]{2,1,0:T(8,128)S(1)}, u32[]{:S(2)}, u32[]{:S(2)}) collective-permute-start(f32[2,128,1024]{2,1,0:T(8,128)S(1)} %collective-permute-done.1.refs_1_), channel_id=1, source_target_pairs={{2,0},{4,2},{3,5},{5,7},{10,8},{12,10},{11,13},{13,15},{18,16},{20... | collective-permute-start | bytes 3145736 | tf_op jit(solution)/shard_map/ppermute | solution.py:479
  45.5 9.2 %collective-permute-start.10 = (f32[256,512]{1,0:T(8,128)S(1)}, f32[256,512]{1,0:T(8,128)S(1)}, u32[]{:S(2)}, u32[]{:S(2)}) collective-permute-start(f32[256,512]{1,0:T(8,128)S(1)} %slice_add_fusion.refs_2_), channel_id=1, source_target_pairs={{0,8},{1,17},{8,0},{9,25},{16,24},{17,1},{24,16},{25,9},{2,10},{3,... | collective-permute-start | bytes 1572872 | tf_op jit(solution)/shard_map/ppermute | solution.py:499
  47.5 10.5 %collective-permute-start.13 = (f32[2,128,1024]{2,1,0:T(8,128)S(1)}, f32[2,128,1024]{2,1,0:T(8,128)S(1)}, u32[]{:S(2)}, u32[]{:S(2)}) collective-permute-start(f32[2,128,1024]{2,1,0:T(8,128)S(1)} %collective-permute-done.6.refs_4_.refs_0_), channel_id=1, source_target_pairs={{0,1},{1,0},{2,3},{3,2},{4,5},{5,4},{6,7},{7,6},{8,9},{9,8},{10,11... | collective-permute-start | bytes 3145736 | tf_op jit(solution)/shard_map/ppermute | solution.py:484
  47.5 16.7 %collective-permute-start.12 = (f32[2,128,1024]{2,1,0:T(8,128)S(1)}, f32[2,128,1024]{2,1,0:T(8,128)S(1)}, u32[]{:S(2)}, u32[]{:S(2)}) collective-permute-start(f32[2,128,1024]{2,1,0:T(8,128)S(1)} %collective-permute-done.6.refs_4_.refs_0_), channel_id=1, source_target_pairs={{2,0},{5,7},{10,8},{13,15},{18,16},{21,23},{26,24},{29,31}} | collective-permute-start | bytes 3145736 | tf_op jit(solution)/shard_map/ppermute | solution.py:479
  54.7 9.4 %collective-permute-start.17 = (f32[256,512]{1,0:T(8,128)S(1)}, f32[256,512]{1,0:T(8,128)S(1)}, u32[]{:S(2)}, u32[]{:S(2)}) collective-permute-start(f32[256,512]{1,0:T(8,128)S(1)} %get-tuple-element.211), channel_id=1, source_target_pairs={{0,16},{1,9},{8,24},{9,1},{16,0},{17,25},{24,8},{25,17},{2,18},{3,... | collective-permute-start | bytes 1572872 | tf_op jit(solution)/shard_map/ppermute | solution.py:499
  56.7 10.2 %collective-permute-start.16 = (f32[2,128,1024]{2,1,0:T(8,128)S(1)}, f32[2,128,1024]{2,1,0:T(8,128)S(1)}, u32[]{:S(2)}, u32[]{:S(2)}) collective-permute-start(f32[2,128,1024]{2,1,0:T(8,128)S(1)} %collective-permute-done.4.refs_5_.refs_0_), channel_id=1, source_target_pairs={{0,1},{1,0},{2,3},{3,2},{4,5},{5,4},{6,7},{7,6},{8,9},{9,8},{10,11... | collective-permute-start | bytes 3145736 | tf_op jit(solution)/shard_map/ppermute | solution.py:484
  56.7 19.3 %collective-permute-start.11 = (f32[2,128,1024]{2,1,0:T(8,128)S(1)}, f32[2,128,1024]{2,1,0:T(8,128)S(1)}, u32[]{:S(2)}, u32[]{:S(2)}) collective-permute-start(f32[2,128,1024]{2,1,0:T(8,128)S(1)} %collective-permute-done.4.refs_5_.refs_0_), channel_id=1, source_target_pairs={{2,0},{5,7},{10,8},{13,15},{18,16},{21,23},{26,24},{29,31}} | collective-permute-start | bytes 3145736 | tf_op jit(solution)/shard_map/ppermute | solution.py:479
  64.2 9.2 %collective-permute-start.18 = (f32[256,512]{1,0:T(8,128)S(1)}, f32[256,512]{1,0:T(8,128)S(1)}, u32[]{:S(2)}, u32[]{:S(2)}) collective-permute-start(f32[256,512]{1,0:T(8,128)S(1)} %add.30.refs_4_), channel_id=1, source_target_pairs={{0,8},{1,17},{8,0},{9,25},{16,24},{17,1},{24,16},{25,9},{2,10},{3,... | collective-permute-start | bytes 1572872 | tf_op jit(solution)/shard_map/ppermute | solution.py:499
  66.2 7.2 %collective-permute-start.14 = (f32[1,128,1024]{2,1,0:T(8,128)S(1)}, f32[1,128,1024]{2,1,0:T(8,128)S(1)}, u32[]{:S(2)}, u32[]{:S(2)}) collective-permute-start(f32[1,128,1024]{2,1,0:T(8,128)S(1)} %get-tuple-element.293), channel_id=1, source_target_pairs={{0,1},{1,0},{2,3},{3,2},{4,5},{5,4},{6,7},{7,6},{8,9},{9,8},{10,11... | collective-permute-start | bytes 1572872 | tf_op jit(solution)/shard_map/ppermute | solution.py:484
  76.1 7.8 %collective-permute-start.20 = (f32[192,512]{1,0:T(8,128)S(1)}, f32[192,512]{1,0:T(8,128)S(1)}, u32[]{:S(2)}, u32[]{:S(2)}) collective-permute-start(f32[192,512]{1,0:T(8,128)S(1)} %pad_maximum_fusion.4), channel_id=1, source_target_pairs={{0,16},{1,9},{8,24},{9,1},{16,0},{17,25},{24,8},{25,17},{2,18},{3,... | collective-permute-start | bytes 1179656 | tf_op jit(solution)/shard_map/ppermute | solution.py:499
  84.0 7.8 %collective-permute-start.21 = (f32[192,512]{1,0:T(8,128)S(1)}, f32[192,512]{1,0:T(8,128)S(1)}, u32[]{:S(2)}, u32[]{:S(2)}) collective-permute-start(f32[192,512]{1,0:T(8,128)S(1)} %get-tuple-element.242), channel_id=1, source_target_pairs={{0,16},{1,9},{8,24},{9,1},{16,0},{17,25},{24,8},{25,17},{2,18},{3,... | collective-permute-start | bytes 1179656 | tf_op jit(solution)/shard_map/ppermute | solution.py:499
  89.2 11.5 %collective-permute-start.24 = (f32[192,512]{1,0:T(8,128)S(1)}, f32[192,512]{1,0:T(8,128)S(1)}, u32[]{:S(2)}, u32[]{:S(2)}) collective-permute-start(f32[192,512]{1,0:T(8,128)S(1)} %get-tuple-element.263), channel_id=1, source_target_pairs={{0,16},{1,9},{8,24},{9,1},{16,0},{17,25},{24,8},{25,17},{2,18},{3,... | collective-permute-start | bytes 1179656 | tf_op jit(solution)/shard_map/ppermute | solution.py:499
  91.9 12.4 %collective-permute-start.22 = (f32[320,512]{1,0:T(8,128)S(1)}, f32[320,512]{1,0:T(8,128)S(1)}, u32[]{:S(2)}, u32[]{:S(2)}) collective-permute-start(f32[320,512]{1,0:T(8,128)S(1)} %pad_maximum_fusion.1), channel_id=1, source_target_pairs={{0,8},{1,17},{8,0},{9,25},{16,24},{17,1},{24,16},{25,9},{2,10},{3,... | collective-permute-start | bytes 1966088 | tf_op jit(solution)/shard_map/ppermute | solution.py:499
  100.7 12.5 %collective-permute-start.25 = (f32[256,512]{1,0:T(8,128)S(1)}, f32[256,512]{1,0:T(8,128)S(1)}, u32[]{:S(2)}, u32[]{:S(2)}) collective-permute-start(f32[256,512]{1,0:T(8,128)S(1)} %pad_maximum_fusion.3), channel_id=1, source_target_pairs={{0,8},{1,17},{8,0},{9,25},{16,24},{17,1},{24,16},{25,9},{2,10},{3,... | collective-permute-start | bytes 1572872 | tf_op jit(solution)/shard_map/ppermute | solution.py:499
  104.4 12.3 %collective-permute-start.23 = (f32[320,512]{1,0:T(8,128)S(1)}, f32[320,512]{1,0:T(8,128)S(1)}, u32[]{:S(2)}, u32[]{:S(2)}) collective-permute-start(f32[320,512]{1,0:T(8,128)S(1)} %add.33.kept), channel_id=1, source_target_pairs={{0,16},{1,9},{8,24},{9,1},{16,0},{17,25},{24,8},{25,17},{2,18},{3,... | collective-permute-start | bytes 1966088 | tf_op jit(solution)/shard_map/ppermute | solution.py:499
  113.4 9.2 %collective-permute-start.26 = (f32[256,512]{1,0:T(8,128)S(1)}, f32[256,512]{1,0:T(8,128)S(1)}, u32[]{:S(2)}, u32[]{:S(2)}) collective-permute-start(f32[256,512]{1,0:T(8,128)S(1)} %add.36.half), channel_id=1, source_target_pairs={{0,16},{1,9},{8,24},{9,1},{16,0},{17,25},{24,8},{25,17},{2,18},{3,... | collective-permute-start | bytes 1572872 | tf_op jit(solution)/shard_map/ppermute | solution.py:499
  (9 other events, 51.0 us)
